TPU v7x, 32 devices: a whole 2x2x4 slice. The times are simulated.
32 devices in a mesh: slab: 2 (over x), energy: 16 (over z, y, core).
Axes of the slice: x: 2, y: 2, z: 4, core: 2. Of those that a mesh axis runs over, the one named last changes fastest.
Arguments:
- retarded: float32 [2, 32, 2, 256, 256], P('slab', 'energy'), may hold values from -0.375 to 0.375
- lesser_prev: float32 [2, 32, 2, 256, 256], P('slab', 'energy'), may hold values from -1.8 to 1.8
- hopping: float32 [2, 256, 256], P('slab'), may hold values from -0.375 to 0.375
- hop_mask: int32 [2, 4, 4], P('slab'), may hold values 0 or 1
- offsets: int32 [3], replicated, may hold values from 1 to 6, as said below
- coupling: float32 [3], replicated, may hold values from 0.3 to 1
- occupation: float32 [3], replicated, may hold values from 0.1 to 3
Outputs:
- lesser: float32 [2, 32, 2, 256, 256], P('slab', 'energy')
Inputs may be any that keep to these rules, and one draw needn't show every extreme that they name: `offsets`: the offset of mode k lies in k * 2 + 1 to (k + 1) * 2, and the last mode's equals 6.
All inputs are finite; a program needn't handle non-finite values. No bound on the sum of `hop_mask` on one device may be relied on, other than what follows from the above.
Results may differ from a plain program's by a relative error of at most 0.00014.
Values sent between devices are 32-bit elements; how exact they have to be, the bound alone decides.
No kernel may reach another device: no remote copies, remote signals or barrier semaphores. Data moves between devices by JAX's collectives and lax.ppermute only.
A program may use at most 64 MiB of HBM per device.

v0:
```python
import jax
import jax.numpy as jnp
from jax import lax
from jax.sharding import PartitionSpec as P


def from_behind(value, axis, by):
    devices = lax.axis_size(axis)
    pairs = [(i, i + by) for i in range(devices) if 0 <= i + by < devices]
    return lax.ppermute(value, axis, pairs)


def matmul_high(left_matrix, right_matrix):
    return jnp.einsum(
        "...ij,...jk->...ik",
        left_matrix,
        right_matrix,
        precision=lax.Precision.HIGHEST,
        preferred_element_type=jnp.float32,
    )


def matmul_transposed(left_matrix, right_matrix):
    return jnp.einsum(
        "...ij,...kj->...ik",
        left_matrix,
        right_matrix,
        precision=lax.Precision.HIGHEST,
        preferred_element_type=jnp.float32,
    )


def complex_product(left_factor, right_factor):
    left_real, left_imag = (left_factor[..., 0, :, :], left_factor[..., 1, :, :])
    right_real, right_imag = (right_factor[..., 0, :, :], right_factor[..., 1, :, :])
    real_part = matmul_high(left_real, right_real) - matmul_high(left_imag, right_imag)
    imag_part = matmul_high(left_real, right_imag) + matmul_high(left_imag, right_real)
    return jnp.stack([real_part, imag_part], axis=-3)


def product_adjoint(left_factor, right_factor):
    left_real, left_imag = (left_factor[..., 0, :, :], left_factor[..., 1, :, :])
    right_real, right_imag = (right_factor[..., 0, :, :], right_factor[..., 1, :, :])
    real_part = matmul_transposed(left_real, right_real) + matmul_transposed(left_imag, right_imag)
    imag_part = matmul_transposed(left_imag, right_real) - matmul_transposed(left_real, right_imag)
    return jnp.stack([real_part, imag_part], axis=-3)


def masked_hopping(hopping_block, mask_block):
    blocks = mask_block.shape[-1]
    tile_size = hopping_block.shape[-1] // blocks
    expanded = jnp.broadcast_to(
        mask_block.astype(jnp.float32)[:, None, :, None], (blocks, tile_size, blocks, tile_size)
    )
    return hopping_block * expanded.reshape(blocks * tile_size, blocks * tile_size)


def offset_term(piece, distance, offsets, coupling, occupation):
    per_device = piece.shape[1]
    source_energy = jnp.arange(per_device, dtype=jnp.int32)[None, :]
    target_energy = jnp.arange(per_device, dtype=jnp.int32)[:, None]
    delta = distance * per_device + source_energy - target_energy
    emission = (offsets[:, None, None] == delta[None]).astype(jnp.float32)
    absorption = (offsets[:, None, None] == -delta[None]).astype(jnp.float32)
    factors = coupling[:, None, None] * (
        (occupation[:, None, None] + 1.0) * emission + occupation[:, None, None] * absorption
    )
    weights = jnp.sum(factors, axis=0)
    return jnp.einsum(
        "ji,sixyz->sjxyz",
        weights,
        piece,
        precision=lax.Precision.HIGHEST,
        preferred_element_type=jnp.float32,
    )


def body(retarded, lesser_prev, hopping, hop_mask, offsets, coupling, occupation):
    mode_count = offsets.shape[0]
    self_energy = offset_term(lesser_prev, 0, offsets, coupling, occupation)
    upper_piece = lesser_prev
    lower_piece = lesser_prev
    for distance in range(1, mode_count + 1):
        upper_piece = from_behind(upper_piece, "energy", -1)
        lower_piece = from_behind(lower_piece, "energy", 1)
        self_energy = self_energy + offset_term(
            upper_piece, distance, offsets, coupling, occupation
        )
        self_energy = self_energy + offset_term(
            lower_piece, -distance, offsets, coupling, occupation
        )
    coupled = matmul_high(retarded, masked_hopping(hopping[0], hop_mask[0]))
    source = product_adjoint(complex_product(retarded, self_energy), retarded)
    position = lax.axis_index("slab")

    def advance(turn_number, current):
        incoming = from_behind(current, "slab", 1)
        return lax.cond(
            position == turn_number,
            lambda: source + product_adjoint(complex_product(coupled, incoming), coupled),
            lambda: current,
        )

    lesser = lax.fori_loop(1, lax.axis_size("slab"), advance, source)
    return lesser


def solution(mesh):
    return jax.shard_map(
        body,
        mesh=mesh,
        in_specs=(
            P("slab", "energy", None, None, None),
            P("slab", "energy", None, None, None),
            P("slab", None, None),
            P("slab", None, None),
            P(),
            P(),
            P(),
        ),
        out_specs=P("slab", "energy", None, None, None),
        check_vma=False,
    )
```

profile of v0, /device:TPU:22, one launch (start us, length us, event | category | flops | bytes accessed | tf_op | source)
XLA Modules:
  0.0 135.6 jit_solution(4300128765706520303)
XLA Ops:
  0.0 2.1 %copy.27 = f32[1,2,2,256,256]{4,1,3,2,0:T(2,128)S(1)} copy(f32[1,2,2,256,256]{4,3,2,1,0:T(8,128)} %param.10) | data formatting | bytes 2097152 | tf_op args[1]
  2.1 1.9 %collective-permute-start.1 = (f32[1,2,2,256,256]{4,1,3,2,0:T(2,128)S(1)}, f32[1,2,2,256,256]{4,1,3,2,0:T(2,128)S(1)}, u32[]{:S(2)}, u32[]{:S(2)}) collective-permute-start(f32[1,2,2,256,256]{4,1,3,2,0:T(2,128)S(1)} %copy.27), channel_id=1, source_target_pairs={{0,1},{1,2},{2,3},{3,4},{4,5},{5,6},{6,7},{7,8},{8,9},{9,10},{10,1... | collective-permute-start | bytes 3145736 | tf_op jit(solution)/shard_map/ppermute | solution.py:10
  4.1 3.6 %collective-permute-start = (f32[1,2,2,256,256]{4,1,3,2,0:T(2,128)S(1)}, f32[1,2,2,256,256]{4,1,3,2,0:T(2,128)S(1)}, u32[]{:S(2)}, u32[]{:S(2)}) collective-permute-start(f32[1,2,2,256,256]{4,1,3,2,0:T(2,128)S(1)} %copy.27), channel_id=1, source_target_pairs={{1,0},{2,1},{3,2},{4,3},{5,4},{6,5},{7,6},{8,7},{9,8},{10,9},{11,1... | collective-permute-start | bytes 3145736 | tf_op jit(solution)/shard_map/ppermute | solution.py:10
  8.4 32.3 %collective-permute-done.1 = f32[1,2,2,256,256]{4,1,3,2,0:T(2,128)S(1)} collective-permute-done((f32[1,2,2,256,256]{4,1,3,2,0:T(2,128)S(1)}, f32[1,2,2,256,256]{4,1,3,2,0:T(2,128)S(1)}, u32[]{:S(2)}, u32[]{:S(2)}) %collective-permute-start.1) | collective-permute-done | bytes 1048608 | tf_op jit(solution)/shard_map/ppermute | solution.py:10
  40.7 1.9 %collective-permute-start.3 = (f32[1,2,2,256,256]{4,1,3,2,0:T(2,128)S(1)}, f32[1,2,2,256,256]{4,1,3,2,0:T(2,128)S(1)}, u32[]{:S(2)}, u32[]{:S(2)}) collective-permute-start(f32[1,2,2,256,256]{4,1,3,2,0:T(2,128)S(1)} %collective-permute-done.1), channel_id=1, source_target_pairs={{0,1},{1,2},{2,3},{3,4},{4,5},{5,6},{6,7},{7,8},{8,9},{9,10},{10,1... | collective-permute-start | bytes 3145736 | tf_op jit(solution)/shard_map/ppermute | solution.py:10
  42.7 3.6 %collective-permute-start.2 = (f32[1,2,2,256,256]{4,1,3,2,0:T(2,128)S(1)}, f32[1,2,2,256,256]{4,1,3,2,0:T(2,128)S(1)}, u32[]{:S(2)}, u32[]{:S(2)}) collective-permute-start(f32[1,2,2,256,256]{4,1,3,2,0:T(2,128)S(1)} %collective-permute-done), channel_id=1, source_target_pairs={{1,0},{2,1},{3,2},{4,3},{5,4},{6,5},{7,6},{8,7},{9,8},{10,9},{11,1... | collective-permute-start | bytes 3145736 | tf_op jit(solution)/shard_map/ppermute | solution.py:10
  47.2 3.8 %fusion.28 = f32[2,2,256,256]{3,0,2,1:T(2,128)S(1)} fusion(f32[2,2,256,256]{3,2,1,0:T(8,128)S(1)} %bitcast.149, f32[2,2]{1,0:T(2,128)S(1)} %get-tuple-element.51), kind=kOutput, calls=%fused_computation.45 | convolution fusion | flops 6291456 | bytes 2097168 | tf_op jit(solution)/shard_map/ji,sixyz->sjxyz/dot_general | solution.py:69
  51.0 5.8 %collective-permute-done.3 = f32[1,2,2,256,256]{4,1,3,2,0:T(2,128)S(1)} collective-permute-done((f32[1,2,2,256,256]{4,1,3,2,0:T(2,128)S(1)}, f32[1,2,2,256,256]{4,1,3,2,0:T(2,128)S(1)}, u32[]{:S(2)}, u32[]{:S(2)}) %collective-permute-start.3) | collective-permute-done | bytes 1048608 | tf_op jit(solution)/shard_map/ppermute | solution.py:10
  56.8 1.9 %collective-permute-start.5 = (f32[1,2,2,256,256]{4,1,3,2,0:T(2,128)S(1)}, f32[1,2,2,256,256]{4,1,3,2,0:T(2,128)S(1)}, u32[]{:S(2)}, u32[]{:S(2)}) collective-permute-start(f32[1,2,2,256,256]{4,1,3,2,0:T(2,128)S(1)} %collective-permute-done.3), channel_id=1, source_target_pairs={{0,1},{1,2},{2,3},{3,4},{4,5},{5,6},{6,7},{7,8},{8,9},{9,10},{10,1... | collective-permute-start | bytes 3145736 | tf_op jit(solution)/shard_map/ppermute | solution.py:10
  58.7 3.9 %convolution_add_fusion.5 = f32[2,2,256,256]{3,0,2,1:T(2,128)S(1)} fusion(f32[2,2,256,256]{3,0,2,1:T(2,128)S(1)} %fusion.28, f32[1,2,2,256,256]{4,1,3,2,0:T(2,128)S(1)} %collective-permute-done, f32[2,2]{1,0:T(2,128)S(1)} %get-tuple-element.46), kind=kOutput, calls=%fused_computation.28 | convolution fusion | flops 6553600 | bytes 3145744 | tf_op jit(solution)/shard_map/ji,sixyz->sjxyz/dot_general | solution.py:69
  62.6 7.2 %collective-permute-done.2 = f32[1,2,2,256,256]{4,1,3,2,0:T(2,128)S(1)} collective-permute-done((f32[1,2,2,256,256]{4,1,3,2,0:T(2,128)S(1)}, f32[1,2,2,256,256]{4,1,3,2,0:T(2,128)S(1)}, u32[]{:S(2)}, u32[]{:S(2)}) %collective-permute-start.2) | collective-permute-done | bytes 1048608 | tf_op jit(solution)/shard_map/ppermute | solution.py:10
  69.8 4.0 %collective-permute-start.4 = (f32[1,2,2,256,256]{4,1,3,2,0:T(2,128)S(1)}, f32[1,2,2,256,256]{4,1,3,2,0:T(2,128)S(1)}, u32[]{:S(2)}, u32[]{:S(2)}) collective-permute-start(f32[1,2,2,256,256]{4,1,3,2,0:T(2,128)S(1)} %collective-permute-done.2), channel_id=1, source_target_pairs={{1,0},{2,1},{3,2},{4,3},{5,4},{6,5},{7,6},{8,7},{9,8},{10,9},{11,1... | collective-permute-start | bytes 3145736 | tf_op jit(solution)/shard_map/ppermute | solution.py:10
  73.8 3.7 %convolution_add_fusion.4 = f32[2,2,256,256]{3,0,2,1:T(2,128)S(1)} fusion(f32[2,2,256,256]{3,0,2,1:T(2,128)S(1)} %convolution_add_fusion.5, f32[1,2,2,256,256]{4,1,3,2,0:T(2,128)S(1)} %collective-permute-done.1, f32[2,2]{1,0:T(2,128)S(1)} %get-tuple-element.47), kind=kOutput, calls=%fused_computation.27 | convolution fusion | flops 6553600 | bytes 3145744 | tf_op jit(solution)/shard_map/ji,sixyz->sjxyz/dot_general | solution.py:69
  77.6 3.6 %fusion.23 = f32[2,2,256,256]{3,0,2,1:T(2,128)S(1)} fusion(f32[1,2,2,256,256]{4,1,3,2,0:T(2,128)S(1)} %collective-permute-done.3, f32[2,2]{1,0:T(2,128)S(1)} %get-tuple-element.49), kind=kOutput, calls=%fused_computation.40 | convolution fusion | flops 6291456 | bytes 2097168 | tf_op jit(solution)/shard_map/ji,sixyz->sjxyz/dot_general | solution.py:69
  81.2 4.1 %fusion.16 = f32[2,2,256,256]{3,0,2,1:T(2,128)S(1)} fusion(f32[2,2,256,256]{3,0,2,1:T(2,128)S(1)} %fusion.23, f32[2,2,256,256]{3,0,2,1:T(2,128)S(1)} %convolution_add_fusion.4, f32[1,2,2,256,256]{4,1,3,2,0:T(2,128)S(1)} %collective-permute-done.2, f32[2,2]{1,0:T(2,128)S(1)} %get-tuple-element.48), kind=kOutput, calls=%fused_computation.26 | convolution fusion | flops 6815744 | bytes 4194320 | tf_op jit(solution)/shard_map/ji,sixyz->sjxyz/dot_general | solution.py:69
  85.3 3.6 %fusion.20 = f32[2,2,256,256]{3,0,2,1:T(2,128)S(1)} fusion(f32[1,2,2,256,256]{4,1,3,2,0:T(2,128)S(1)} %collective-permute-done.5, f32[2,2]{1,0:T(2,128)S(1)} %get-tuple-element.50), kind=kOutput, calls=%fused_computation.37 | convolution fusion | flops 6291456 | bytes 2097168 | tf_op jit(solution)/shard_map/ji,sixyz->sjxyz/dot_general | solution.py:69
  89.0 4.2 %fusion.15 = f32[1,2,2,256,256]{4,1,3,2,0:T(2,128)S(1)} fusion(f32[2,2,256,256]{3,0,2,1:T(2,128)S(1)} %fusion.20, f32[2,2,256,256]{3,0,2,1:T(2,128)S(1)} %fusion.16, f32[1,2,2,256,256]{4,1,3,2,0:T(2,128)S(1)} %collective-permute-done.4, f32[2,2]{1,0:T(2,128)S(1)} %get-tuple-element.45), kind=kOutput, calls=%fused_computation.24 | convolution fusion | flops 6815744 | bytes 4194320 | tf_op jit(solution)/shard_map/ji,sixyz->sjxyz/dot_general | solution.py:69
  94.0 0.8 copy-done
  96.1 0.7 convolution_subtract_fusion.3
  96.8 1.0 fusion.38
  98.5 1.0 fusion.34
  99.6 1.0 fusion.18
  100.6 1.0 fusion.17
  101.8 1.3 collective-permute-start.6
  103.1 0.9 broadcast_in_dim.2
  104.1 1.4 %reshape.464 = f32[1,256,256]{2,1,0:T(8,128)S(1)} reshape(f32[4,64,4,64]{3,2,1,0:T(4,128)} %broadcast_in_dim.2) | data formatting | bytes 524288 | tf_op jit(solution)/shard_map/reshape | solution.py:55
  105.4 3.8 %convolution_bitcast_fusion = f32[2,2,256,256]{2,3,1,0:T(8,128)} fusion(f32[1,2,2,256,256]{4,3,2,1,0:T(8,128)S(1)} %copy-done, f32[1,256,256]{2,1,0:T(8,128)} %param.11, f32[1,256,256]{2,1,0:T(8,128)S(1)} %reshape.464), kind=kOutput, calls=%fused_computation.21 | convolution fusion | flops 805371904 | bytes 2621440 | tf_op jit(solution)/shard_map/...ij,...jk->...ik/dot_general | solution.py:14
  109.2 18.1 %collective-permute-done.6 = f32[1,2,2,256,256]{4,3,1,2,0:T(8,128)S(1)} collective-permute-done((f32[1,2,2,256,256]{4,3,1,2,0:T(8,128)S(1)}, f32[1,2,2,256,256]{4,3,1,2,0:T(8,128)S(1)}, u32[]{:S(2)}, u32[]{:S(2)}) %collective-permute-start.6) | collective-permute-done | bytes 1048608 | tf_op jit(solution)/shard_map/while/body/eval_jaxpr/ppermute | solution.py:10
  127.4 7.1 %conditional.1 = (f32[1,2,2,256,256]{4,3,1,2,0:T(8,128)S(1)}) conditional(s32[]{:T(128)} %convert_element_type.12, f32[1,2,2,256,256]{4,3,1,2,0:T(8,128)S(1)} %pad_maximum_fusion, (f32[2,2,256,256]{2,3,1,0:T(8,128)}, f32[1,2,2,256,256]{4,3,1,2,0:T(8,128)S(1)}, f32[1,2,2,256,256]{4,3,1,2,0:T(8,128)S(1)}) %tuple.14), branch_computations={%region_7.8_spmd, %region_8.9_spmd} | conditional | flops 3222274048 | bytes 19922952 | solution.py:98
  127.4 1.6 %copy.40 = f32[2,2,256,256]{3,2,0,1:T(8,128)S(1)} copy(f32[2,2,256,256]{2,3,1,0:T(8,128)} %get-tuple-element.42) | data formatting | bytes 2097152 | tf_op jit(solution)/shard_map
  132.2 0.7 fusion.1
  134.5 1.0 copy.41
  (42 shorter events, 9.3 us)
Async XLA Ops:
  0.0 47.2 %copy-start.1 = (f32[1,2,2,256,256]{4,3,2,1,0:T(8,128)S(1)}, f32[1,2,2,256,256]{4,3,2,1,0:T(8,128)}, u32[]{:S(2)}) copy-start(f32[1,2,2,256,256]{4,3,2,1,0:T(8,128)} %param.10) | copy-start | bytes 3145732
  2.1 38.6 %collective-permute-start.1 = (f32[1,2,2,256,256]{4,1,3,2,0:T(2,128)S(1)}, f32[1,2,2,256,256]{4,1,3,2,0:T(2,128)S(1)}, u32[]{:S(2)}, u32[]{:S(2)}) collective-permute-start(f32[1,2,2,256,256]{4,1,3,2,0:T(2,128)S(1)} %copy.27), channel_id=1, source_target_pairs={{0,1},{1,2},{2,3},{3,4},{4,5},{5,6},{6,7},{7,8},{8,9},{9,10},{10,1... | collective-permute-start | bytes 3145736 | tf_op jit(solution)/shard_map/ppermute | solution.py:10
  4.1 38.6 %collective-permute-start = (f32[1,2,2,256,256]{4,1,3,2,0:T(2,128)S(1)}, f32[1,2,2,256,256]{4,1,3,2,0:T(2,128)S(1)}, u32[]{:S(2)}, u32[]{:S(2)}) collective-permute-start(f32[1,2,2,256,256]{4,1,3,2,0:T(2,128)S(1)} %copy.27), channel_id=1, source_target_pairs={{1,0},{2,1},{3,2},{4,3},{5,4},{6,5},{7,6},{8,7},{9,8},{10,9},{11,1... | collective-permute-start | bytes 3145736 | tf_op jit(solution)/shard_map/ppermute | solution.py:10
  7.7 0.7 copy-start.3
  40.7 16.1 %collective-permute-start.3 = (f32[1,2,2,256,256]{4,1,3,2,0:T(2,128)S(1)}, f32[1,2,2,256,256]{4,1,3,2,0:T(2,128)S(1)}, u32[]{:S(2)}, u32[]{:S(2)}) collective-permute-start(f32[1,2,2,256,256]{4,1,3,2,0:T(2,128)S(1)} %collective-permute-done.1), channel_id=1, source_target_pairs={{0,1},{1,2},{2,3},{3,4},{4,5},{5,6},{6,7},{7,8},{8,9},{9,10},{10,1... | collective-permute-start | bytes 3145736 | tf_op jit(solution)/shard_map/ppermute | solution.py:10
  42.7 27.2 %collective-permute-start.2 = (f32[1,2,2,256,256]{4,1,3,2,0:T(2,128)S(1)}, f32[1,2,2,256,256]{4,1,3,2,0:T(2,128)S(1)}, u32[]{:S(2)}, u32[]{:S(2)}) collective-permute-start(f32[1,2,2,256,256]{4,1,3,2,0:T(2,128)S(1)} %collective-permute-done), channel_id=1, source_target_pairs={{1,0},{2,1},{3,2},{4,3},{5,4},{6,5},{7,6},{8,7},{9,8},{10,9},{11,1... | collective-permute-start | bytes 3145736 | tf_op jit(solution)/shard_map/ppermute | solution.py:10
  46.3 0.7 copy-start.4
  46.4 0.7 copy-start.5
  56.8 28.5 %collective-permute-start.5 = (f32[1,2,2,256,256]{4,1,3,2,0:T(2,128)S(1)}, f32[1,2,2,256,256]{4,1,3,2,0:T(2,128)S(1)}, u32[]{:S(2)}, u32[]{:S(2)}) collective-permute-start(f32[1,2,2,256,256]{4,1,3,2,0:T(2,128)S(1)} %collective-permute-done.3), channel_id=1, source_target_pairs={{0,1},{1,2},{2,3},{3,4},{4,5},{5,6},{6,7},{7,8},{8,9},{9,10},{10,1... | collective-permute-start | bytes 3145736 | tf_op jit(solution)/shard_map/ppermute | solution.py:10
  69.8 19.2 %collective-permute-start.4 = (f32[1,2,2,256,256]{4,1,3,2,0:T(2,128)S(1)}, f32[1,2,2,256,256]{4,1,3,2,0:T(2,128)S(1)}, u32[]{:S(2)}, u32[]{:S(2)}) collective-permute-start(f32[1,2,2,256,256]{4,1,3,2,0:T(2,128)S(1)} %collective-permute-done.2), channel_id=1, source_target_pairs={{1,0},{2,1},{3,2},{4,3},{5,4},{6,5},{7,6},{8,7},{9,8},{10,9},{11,1... | collective-permute-start | bytes 3145736 | tf_op jit(solution)/shard_map/ppermute | solution.py:10
  93.6 1.2 copy-start
  101.7 1.4 %copy-start.2 = (s32[1,4,4]{2,1,0:T(4,128)S(1)}, s32[1,4,4]{2,1,0:T(4,128)}, u32[]{:S(2)}) copy-start(s32[1,4,4]{2,1,0:T(4,128)} %param.12) | copy-start | bytes 196
  101.8 25.6 %collective-permute-start.6 = (f32[1,2,2,256,256]{4,3,1,2,0:T(8,128)S(1)}, f32[1,2,2,256,256]{4,3,1,2,0:T(8,128)S(1)}, u32[]{:S(2)}, u32[]{:S(2)}) collective-permute-start(f32[1,2,2,256,256]{4,3,1,2,0:T(8,128)S(1)} %pad_maximum_fusion), channel_id=1, source_target_pairs={{0,16},{1,17},{2,18},{3,19},{4,20},{5,21},{6,22},{7,23},{8,24},{9,... | collective-permute-start | bytes 3145736 | tf_op jit(solution)/shard_map/while/body/eval_jaxpr/ppermute | solution.py:10
where the time goes:
time: 136 us
  waiting for transfers between devices  63.4 us (47%)
  matrix products  42.9 us (32%)
  starting transfers between devices  18.3 us (13%)
  local copies, waits for them, and re-layouts  9.89 us (7%)
    ppermute x7, waiting for transfers between devices, from_behind(): return lax.ppermute(value, axis, pairs)  63.4 us
    dot_general x7, matrix products, offset_term(): jnp.einsum('ji,sixyz->sjxyz', weights, piece, precision=lax.Precision.HIG...  27 us
    ppermute x7, starting transfers between devices, from_behind(): return lax.ppermute(value, axis, pairs)  18.3 us
    dot_general x9, matrix products, matmul_high(): jnp.einsum('...ij,...jk->...ik', left_matrix, right_matrix, precision=lax...  9.05 us
    dot_general x8, matrix products, matmul_transposed(): jnp.einsum('...ij,...kj->...ik', left_matrix, right_matrix, precision=lax...  6.83 us
    unnamed x14, local copies, waits for them, and re-layouts  5.24 us
  transfers between devices with their start and end apart: 7, of which 4 were waited for; matrix products, arithmetic and copies ran while one was open for 21% of the time, Pallas kernels for 0%

commit v1 on v0

v1 whole, which is shorter than its diff:
```python
import functools

import jax
import jax.numpy as jnp
from jax import lax
from jax.experimental import pallas as pl
from jax.experimental.pallas import tpu as pltpu
from jax.sharding import PartitionSpec as P

VMEM = pl.BlockSpec(memory_space=pltpu.VMEM)
SMEM = pl.BlockSpec(memory_space=pltpu.SMEM)
CHUNK_ROWS = 32
SMALL_VMEM = 8 * 1024 * 1024
LARGE_VMEM = 24 * 1024 * 1024


def combine_kernel(base, counts, weights_ref, *refs):
    inputs, outputs = refs[: len(counts)], refs[len(counts):]
    blocks = [(ref, index) for ref, count in zip(inputs, counts) for index in range(count)]
    targets = [(ref, index) for ref in outputs for index in range(ref.shape[0])]
    rows, columns = outputs[0].shape[1:]
    lanes = weights_ref.shape[2]
    for top in range(0, rows, CHUNK_ROWS):
        for left in range(0, columns, lanes):
            window = (slice(top, top + CHUNK_ROWS), slice(left, left + lanes))
            totals = [None] * len(targets)
            for column, (ref, index) in enumerate(blocks):
                value = ref[(index,) + window].reshape(CHUNK_ROWS // 8, 8, lanes)
                for row in range(len(targets)):
                    term = weights_ref[base + row * len(blocks) + column][None] * value
                    totals[row] = term if totals[row] is None else totals[row] + term
            for (ref, index), total in zip(targets, totals):
                ref[(index,) + window] = total.reshape(CHUNK_ROWS, lanes)


def combine(weights, base, inputs, output_count):
    counts = tuple(array.shape[0] for array in inputs)
    shape = jax.ShapeDtypeStruct(inputs[0].shape, jnp.float32)
    moved = sum(counts) + output_count * shape.shape[0]
    block_size = shape.shape[1] * shape.shape[2]
    result = pl.pallas_call(
        functools.partial(combine_kernel, base, counts),
        out_shape=[shape] * output_count,
        in_specs=[VMEM] * (1 + len(inputs)),
        out_specs=[VMEM] * output_count,
        compiler_params=pltpu.CompilerParams(vmem_limit_bytes=SMALL_VMEM),
        cost_estimate=pl.CostEstimate(
            flops=2 * block_size * sum(counts), bytes_accessed=4 * block_size * moved, transcendentals=0
        ),
    )(weights, *inputs)
    return result if output_count > 1 else result[0]


def weights_layout(per_device):
    sizes = [(2, 3), (2, 3), (1, 4), (1, 7), (1, 6), (1, 5)]
    bases = [0]
    for outputs, inputs in sizes:
        bases.append(bases[-1] + outputs * inputs * per_device**2)
    return bases


def weights_kernel(total_energies, per_device, offsets_ref, coupling_ref, occupation_ref, table_ref):
    modes = offsets_ref.shape[0]
    offsets = [offsets_ref[mode] for mode in range(modes)]
    lower = [coupling_ref[mode] * occupation_ref[mode] for mode in range(modes)]
    upper = [coupling_ref[mode] * (occupation_ref[mode] + 1.0) for mode in range(modes)]
    bases = weights_layout(per_device)

    me = lax.axis_index("energy")
    core, y, z = me % 2, (me // 2) % 2, me // 4
    chip = me // 2
    swapped = ((z % 2) == 0) == (y == 1)
    first_far_real = core == 1 - y
    away = 2 * y - 1
    beside, diagonal = chip - away, chip + away

    def energy(at_chip, at_core, index):
        return (2 * at_chip + at_core) * per_device + index

    def own(index):
        return energy(chip, core, index)

    def sibling(index):
        return energy(chip, 1 - core, index)

    def far1(index):
        return energy(chip + 2 * away, 1 - y, index)

    def far2(index):
        return energy(chip - 2 * away, y, index)

    def at(place):
        return lambda index: energy(place, core, index)

    def weight(targets, sources, condition=None):
        def entry(row, column):
            target, source = targets(row), sources(column)
            delta = source - target
            result = jnp.float32(0.0)
            for mode in range(modes):
                result = result + jnp.where(delta == offsets[mode], upper[mode], 0.0)
                result = result + jnp.where(delta == -offsets[mode], lower[mode], 0.0)
            inside = (source >= 0) & (source < total_energies)
            if condition is not None:
                inside = inside & condition
            return jnp.where(inside, result, 0.0)

        return entry

    def same(condition=None):
        def entry(row, column):
            if row != column:
                return jnp.float32(0.0)
            return jnp.float32(1.0) if condition is None else jnp.where(condition, 1.0, 0.0)

        return entry

    def choose(condition, one, other):
        return lambda row, column: jnp.where(condition, one(row, column), other(row, column))

    def none(row, column):
        return jnp.float32(0.0)

    def add(one, other):
        return lambda row, column: one(row, column) + other(row, column)

    real1, real2 = first_far_real, ~first_far_real
    here, there = swapped, ~swapped
    diagonal_at, beside_at = at(diagonal), at(beside)
    sum_row = [weight(diagonal_at, own), weight(diagonal_at, sibling), none]
    far1_row = [none, same(~real1), same(real1)]
    pass_row = [same(), none, none]
    far2_row = [none, same(~real2), same(real2)]
    tables = [
        [
            [choose(swapped, a, b) for a, b in zip(sum_row, far1_row)],
            [choose(swapped, b, a) for a, b in zip(sum_row, far1_row)],
        ],
        [
            [choose(swapped, a, b) for a, b in zip(far2_row, pass_row)],
            [choose(swapped, b, a) for a, b in zip(far2_row, pass_row)],
        ],
        [[weight(beside_at, own), weight(beside_at, sibling), same(there), same(here)]],
        [
            [
                weight(own, own),
                weight(own, sibling),
                same(),
                weight(own, far1, ~real1 & here),
                weight(own, far1, ~real1 & there),
                weight(own, far2, ~real2 & there),
                weight(own, far2, ~real2 & here),
            ]
        ],
        [
            [
                weight(sibling, own),
                weight(sibling, beside_at),
                weight(sibling, far1, real1 & here),
                weight(sibling, far1, real1 & there),
                add(weight(sibling, diagonal_at, here), weight(sibling, far2, real2 & there)),
                add(weight(sibling, diagonal_at, there), weight(sibling, far2, real2 & here)),
            ]
        ],
        [
            [
                weight(own, own),
                weight(own, beside_at),
                weight(own, diagonal_at, here),
                weight(own, diagonal_at, there),
                same(),
            ]
        ],
    ]
    for base, table in zip(bases, tables):
        place = base
        for row in table:
            for row_index in range(per_device):
                for entry in row:
                    for column_index in range(per_device):
                        value = entry(row_index, column_index)
                        table_ref[place] = jnp.full(table_ref.shape[1:], value, jnp.float32)
                        place += 1


def split(value):
    high = value.astype(jnp.bfloat16)
    low = (value - high.astype(jnp.float32)).astype(jnp.bfloat16)
    return high, low


def dot3(left, right, transposed=False):
    numbers = (((1,), (1 if transposed else 0,)), ((), ()))

    def one(a, b):
        return lax.dot_general(a, b, numbers, preferred_element_type=jnp.float32)

    return one(left[0], right[0]) + (one(left[0], right[1]) + one(left[1], right[0]))


def times(left, right):
    real = dot3(left[0], right[0]) - dot3(left[1], right[1])
    imag = dot3(left[0], right[1]) + dot3(left[1], right[0])
    return real, imag


def times_adjoint(left, right):
    real = dot3(left[0], right[0], True) + dot3(left[1], right[1], True)
    imag = dot3(left[1], right[0], True) - dot3(left[0], right[1], True)
    return real, imag


def split_pair(pair):
    return split(pair[0]), split(pair[1])


def bridge_kernel(tiles, mask_ref, hopping_ref, retarded_ref, behind_ref, coupled_ref, bridge_ref):
    size = hopping_ref.shape[0]
    tile = size // tiles
    row_tile = lax.broadcasted_iota(jnp.int32, (size, size), 0) // tile
    column_tile = lax.broadcasted_iota(jnp.int32, (size, size), 1) // tile
    mask = jnp.zeros((size, size), jnp.float32)
    for row in range(tiles):
        for column in range(tiles):
            here = (row_tile == row) & (column_tile == column)
            mask = jnp.where(here, mask_ref[row, column].astype(jnp.float32), mask)
    masked = split(hopping_ref[...] * mask)
    for energy in range(retarded_ref.shape[0]):
        coupled = tuple(dot3(split(retarded_ref[energy, part]), masked) for part in range(2))
        for part in range(2):
            coupled_ref[energy, part] = coupled[part]
        bridge = times(
            split_pair(coupled), split_pair((behind_ref[energy, 0], behind_ref[energy, 1]))
        )
        for part in range(2):
            bridge_ref[energy, part] = bridge[part]


def source_kernel(retarded_ref, real_ref, imag_ref, out_ref):
    for energy in range(retarded_ref.shape[0]):
        retarded = split_pair((retarded_ref[energy, 0], retarded_ref[energy, 1]))
        inner = times(retarded, split_pair((real_ref[energy], imag_ref[energy])))
        outer = times_adjoint(split_pair(inner), retarded)
        for part in range(2):
            out_ref[energy, part] = outer[part]


def imag_half_kernel(bridge_ref, imag_ref, out_ref):
    for energy in range(bridge_ref.shape[0]):
        imag = split(imag_ref[energy])
        out_ref[energy, 0] = -dot3(split(bridge_ref[energy, 1]), imag)
        out_ref[energy, 1] = dot3(split(bridge_ref[energy, 0]), imag)


def finish_kernel(flag_ref, bridge_ref, half_ref, real_ref, source_ref, out_ref):
    @pl.when(flag_ref[0] == 0)
    def _():
        out_ref[...] = source_ref[...]

    @pl.when(flag_ref[0] != 0)
    def _():
        for energy in range(bridge_ref.shape[0]):
            bridge = split_pair((bridge_ref[energy, 0], bridge_ref[energy, 1]))
            real = split(real_ref[energy])
            inner = tuple(half_ref[energy, part] + dot3(bridge[part], real) for part in range(2))
            outer = times_adjoint(split_pair(inner), bridge)
            for part in range(2):
                out_ref[energy, part] = source_ref[energy, part] + outer[part]


def advance_kernel(flag_ref, coupled_ref, incoming_ref, source_ref, current_ref, out_ref):
    @pl.when(flag_ref[0] == 0)
    def _():
        out_ref[...] = current_ref[...]

    @pl.when(flag_ref[0] != 0)
    def _():
        for energy in range(coupled_ref.shape[0]):
            coupled = split_pair((coupled_ref[energy, 0], coupled_ref[energy, 1]))
            inner = times(coupled, split_pair((incoming_ref[energy, 0], incoming_ref[energy, 1])))
            outer = times_adjoint(split_pair(inner), coupled)
            for part in range(2):
                out_ref[energy, part] = source_ref[energy, part] + outer[part]


def call(kernel, inputs, specs, outputs, products):
    size = outputs[0].shape[-1]
    return pl.pallas_call(
        kernel,
        out_shape=[jax.ShapeDtypeStruct(array.shape, jnp.float32) for array in outputs],
        in_specs=specs,
        out_specs=[VMEM] * len(outputs),
        compiler_params=pltpu.CompilerParams(vmem_limit_bytes=LARGE_VMEM),
        cost_estimate=pl.CostEstimate(
            flops=6 * products * size**3,
            bytes_accessed=4 * sum(array.size for array in list(inputs) + list(outputs)),
            transcendentals=0,
        ),
    )(*inputs)


def body(retarded, lesser_prev, hopping, hop_mask, offsets, coupling, occupation):
    devices = lax.axis_size("energy")
    slabs = lax.axis_size("slab")
    per_device = lesser_prev.shape[1]
    assert offsets.shape[0] == 3 and devices % 4 == 0
    bases = weights_layout(per_device)
    weights = pl.pallas_call(
        functools.partial(weights_kernel, per_device * devices, per_device),
        out_shape=jax.ShapeDtypeStruct((bases[-1], 8, 128), jnp.float32),
        in_specs=[SMEM] * 3,
        out_specs=VMEM,
        compiler_params=pltpu.CompilerParams(vmem_limit_bytes=SMALL_VMEM),
    )(offsets, coupling, occupation)

    def permute(value, pairs):
        return lax.ppermute(value, "energy", pairs)

    cores = [(i, i ^ 1) for i in range(devices)]
    across = [(i, i ^ 2) for i in range(devices)]
    first_lines = [(i, i ^ 4) for i in range(devices) if (i ^ 4) < devices]
    second_lines = []
    for i in range(devices):
        other = i + 4 if (i // 4) % 2 == 1 else i - 4
        if 0 <= other < devices:
            second_lines.append((i, other))
    ahead = [(s, (s + 1) % slabs) for s in range(slabs)]

    real, imag = lesser_prev[0, :, 0], lesser_prev[0, :, 1]
    blocks = retarded[0]
    imag_sibling = permute(imag, cores)
    real_beside = permute(real, across)
    behind = lax.ppermute(blocks, "slab", ahead)

    send1, send2 = combine(weights, bases[0], [imag, imag_sibling, real], 2)
    got1, got2 = permute(send1, first_lines), permute(send2, second_lines)
    send3, send4 = combine(weights, bases[1], [real_beside, imag_sibling, real], 2)
    got3, got4 = permute(send3, first_lines), permute(send4, second_lines)
    imag_beside = permute(
        combine(weights, bases[2], [imag, imag_sibling, got1, got2], 1), across
    )
    coupled, bridge = call(
        functools.partial(bridge_kernel, hop_mask.shape[-1]),
        [hop_mask[0], hopping[0], blocks, behind],
        [SMEM, VMEM, VMEM, VMEM],
        [blocks, blocks],
        12,
    )
    imag_beside, bridge = lax.optimization_barrier((imag_beside, bridge))
    self_imag = combine(
        weights, bases[3], [imag, imag_sibling, imag_beside, got1, got2, got3, got4], 1
    )
    self_imag_behind = lax.ppermute(self_imag, "slab", ahead)
    real_sibling = permute(
        combine(weights, bases[4], [real, real_beside, got1, got2, got3, got4], 1), cores
    )
    self_real = combine(weights, bases[5], [real, real_beside, got3, got4, real_sibling], 1)
    self_real_behind = lax.ppermute(self_real, "slab", ahead)

    (source,) = call(source_kernel, [blocks, self_real, self_imag], [VMEM] * 3, [blocks], 16)
    (half,) = call(imag_half_kernel, [bridge, self_imag_behind], [VMEM] * 2, [blocks], 4)
    position = lax.axis_index("slab")
    turn_flag = (position == 1).astype(jnp.int32).reshape(1)
    (lesser,) = call(
        finish_kernel,
        [turn_flag, bridge, half, self_real_behind, source],
        [SMEM] + [VMEM] * 4,
        [blocks],
        12,
    )
    for turn in range(2, slabs):
        incoming = lax.ppermute(lesser, "slab", ahead)
        (lesser,) = call(
            advance_kernel,
            [(position == turn).astype(jnp.int32).reshape(1), coupled, incoming, source, lesser],
            [SMEM] + [VMEM] * 4,
            [blocks],
            16,
        )
    return lesser[None]


def solution(mesh):
    return jax.shard_map(
        body,
        mesh=mesh,
        in_specs=(
            P("slab", "energy", None, None, None),
            P("slab", "energy", None, None, None),
            P("slab", None, None),
            P("slab", None, None),
            P(),
            P(),
            P(),
        ),
        out_specs=P("slab", "energy", None, None, None),
        check_vma=False,
    )
```

time: 136 us -> 65.5 us (0.48)
  the two profiles are of different devices: /device:TPU:22 before, /device:TPU:10 now
where the time goes in v1:
time: 65.5 us; the launch traced here: 65.1 us
  waiting for transfers between devices  34.9 us (53%)
  starting transfers between devices  15.4 us (24%)
  Pallas kernels  11.5 us (18%)
  local copies, waits for them, and re-layouts  3.19 us (5%)
    ppermute x8, waiting for transfers between devices, permute(): return lax.ppermute(value, 'energy', pairs)  16.4 us
    ppermute x8, starting transfers between devices, permute(): return lax.ppermute(value, 'energy', pairs)  12.7 us
    ppermute x1, waiting for transfers between devices, body(): self_real_behind = lax.ppermute(self_real, 'slab', ahead)  9.6 us
    ppermute x1, waiting for transfers between devices, body(): self_imag_behind = lax.ppermute(self_imag, 'slab', ahead)  8.95 us
    pallas_call x4, Pallas kernels, call(): pl.pallas_call(kernel, out_shape=[jax.ShapeDtypeStruct(array.shape, jnp.f...  8.09 us
    pallas_call x6, Pallas kernels, combine(): pl.pallas_call(functools.partial(combine_kernel, base, counts), out_shape...  2.31 us
    unnamed x14, local copies, waits for them, and re-layouts  1.83 us
    ppermute x1, starting transfers between devices, body(): self_imag_behind = lax.ppermute(self_imag, 'slab', ahead)  1.55 us
  transfers between devices with their start and end apart: 11, of which 6 were waited for; matrix products, arithmetic and copies ran while one was open for 0% of the time, Pallas kernels for 14%

profile of v1, /device:TPU:10, one launch (start us, length us, event | category | flops | bytes accessed | tf_op | source)
XLA Modules:
  0.0 65.1 jit_solution(2417122258215111708)
XLA Ops:
  0.0 1.4 %slice_bitcast_fusion = (f32[2,256,256]{2,1,0:T(8,128)S(1)}, f32[2,256,256]{2,1,0:T(8,128)S(1)}) fusion(f32[1,2,2,256,256]{4,3,2,1,0:T(8,128)} %param.8), kind=kLoop, calls=%fused_computation | loop fusion | bytes 2097152 | tf_op jit(solution)/shard_map/squeeze | solution.py:329
  1.4 0.1 collective-permute-start
  1.5 0.0 copy-start.1
  1.5 1.6 %collective-permute-start.5 = (f32[2,256,256]{2,1,0:T(8,128)S(1)}, f32[2,256,256]{2,1,0:T(8,128)S(1)}, u32[]{:S(2)}, u32[]{:S(2)}) collective-permute-start(f32[2,256,256]{2,1,0:T(8,128)S(1)} %get-tuple-element.19.refs_2_.refs_0_), channel_id=1, source_target_pairs={{0,2},{1,3},{2,0},{3,1},{4,6},{5,7},{6,4},{7,5},{8,10},{9,11},{10,... | collective-permute-start | bytes 1572872 | tf_op jit(solution)/shard_map/ppermute | solution.py:317
  3.1 0.5 collective-permute-start.4
  3.6 1.1 %shard_map.73.weights_ref = f32[136,8,128]{2,1,0:T(8,128)S(1)} custom-call(s32[3]{0:T(128)S(1)} %copy-done, f32[3]{0:T(128)S(1)} %copy-done.1, f32[3]{0:T(128)S(1)} %copy-done.2), custom_call_target="tpu_custom_call" | custom-call | tf_op jit(solution)/shard_map/pallas_call | solution.py:308
  4.7 0.4 shard_map.74
  5.1 0.5 collective-permute-start.1
  5.6 4.6 %collective-permute-start.2 = (f32[2,256,256]{2,1,0:T(8,128)S(1)}, f32[2,256,256]{2,1,0:T(8,128)S(1)}, u32[]{:S(2)}, u32[]{:S(2)}) collective-permute-start(f32[2,256,256]{2,1,0:T(8,128)S(1)} %get-tuple-element.13), channel_id=1, source_target_pairs={{4,8},{5,9},{6,10},{7,11},{8,4},{9,5},{10,6},{11,7},{20,24},{21,25... | collective-permute-start | bytes 1572872 | tf_op jit(solution)/shard_map/ppermute | solution.py:317
  10.2 5.6 %collective-permute-done.5.refs_0_.refs_1_ = f32[2,256,256]{2,1,0:T(8,128)S(1)} collective-permute-done((f32[2,256,256]{2,1,0:T(8,128)S(1)}, f32[2,256,256]{2,1,0:T(8,128)S(1)}, u32[]{:S(2)}, u32[]{:S(2)}) %collective-permute-start.5) | collective-permute-done | bytes 524320 | tf_op jit(solution)/shard_map/ppermute | solution.py:317
  15.8 0.4 shard_map.77
  16.2 0.5 collective-permute-start.6
  16.7 4.6 %collective-permute-start.7 = (f32[2,256,256]{2,1,0:T(8,128)S(1)}, f32[2,256,256]{2,1,0:T(8,128)S(1)}, u32[]{:S(2)}, u32[]{:S(2)}) collective-permute-start(f32[2,256,256]{2,1,0:T(8,128)S(1)} %get-tuple-element.18), channel_id=1, source_target_pairs={{4,8},{5,9},{6,10},{7,11},{8,4},{9,5},{10,6},{11,7},{20,24},{21,25... | collective-permute-start | bytes 1572872 | tf_op jit(solution)/shard_map/ppermute | solution.py:317
  21.3 0.9 %collective-permute-done.2.refs_3_.refs_4_ = f32[2,256,256]{2,1,0:T(8,128)S(1)} collective-permute-done((f32[2,256,256]{2,1,0:T(8,128)S(1)}, f32[2,256,256]{2,1,0:T(8,128)S(1)}, u32[]{:S(2)}, u32[]{:S(2)}) %collective-permute-start.2) | collective-permute-done | bytes 524320 | tf_op jit(solution)/shard_map/ppermute | solution.py:317
  22.2 0.3 shard_map.75
  22.5 0.7 %collective-permute-start.3 = (f32[2,256,256]{2,1,0:T(8,128)S(1)}, f32[2,256,256]{2,1,0:T(8,128)S(1)}, u32[]{:S(2)}, u32[]{:S(2)}) collective-permute-start(f32[2,256,256]{2,1,0:T(8,128)S(1)} %shard_map.75), channel_id=1, source_target_pairs={{0,2},{1,3},{2,0},{3,1},{4,6},{5,7},{6,4},{7,5},{8,10},{9,11},{10,... | collective-permute-start | bytes 1572872 | tf_op jit(solution)/shard_map/ppermute | solution.py:317
  23.2 6.9 %collective-permute-done.6.refs_5_.refs_4_.refs_2_ = f32[2,256,256]{2,1,0:T(8,128)S(1)} collective-permute-done((f32[2,256,256]{2,1,0:T(8,128)S(1)}, f32[2,256,256]{2,1,0:T(8,128)S(1)}, u32[]{:S(2)}, u32[]{:S(2)}) %collective-permute-start.6) | collective-permute-done | bytes 524320 | tf_op jit(solution)/shard_map/ppermute | solution.py:317
  30.1 3.0 %collective-permute-done.7.refs_6_.refs_5_.refs_3_ = f32[2,256,256]{2,1,0:T(8,128)S(1)} collective-permute-done((f32[2,256,256]{2,1,0:T(8,128)S(1)}, f32[2,256,256]{2,1,0:T(8,128)S(1)}, u32[]{:S(2)}, u32[]{:S(2)}) %collective-permute-start.7) | collective-permute-done | bytes 524320 | tf_op jit(solution)/shard_map/ppermute | solution.py:317
  33.1 0.4 shard_map.80
  33.6 0.1 collective-permute-start.9
  33.7 0.6 copy-done.6
  34.2 2.8 %shard_map.76 = (f32[2,2,256,256]{3,2,1,0:T(8,128)}, f32[2,2,256,256]{3,2,1,0:T(8,128)S(1)}) custom-call(s32[4,4]{1,0:T(4,128)S(1)} %bitcast.17, f32[256,256]{1,0:T(8,128)S(1)} %bitcast.16, f32[2,2,256,256]{3,2,1,0:T(8,128)S(1)} %bitcast.14, f32[2,2,256,256]{3,2,1,0:T(8,128)S(1)} %collective-permute-done.4.behind_ref), custom_call_target="tpu_custom_call" | custom-call | flops 1207959552 | bytes 4456512 | tf_op jit(solution)/shard_map/pallas_call | solution.py:288
  37.1 0.5 shard_map.78.imag_ref
  37.6 1.6 %collective-permute-start.8 = (f32[2,256,256]{2,1,0:T(8,128)S(1)}, f32[2,256,256]{2,1,0:T(8,128)S(1)}, u32[]{:S(2)}, u32[]{:S(2)}) collective-permute-start(f32[2,256,256]{2,1,0:T(8,128)S(1)} %shard_map.78.imag_ref), channel_id=1, source_target_pairs={{0,16},{16,0},{1,17},{17,1},{2,18},{18,2},{3,19},{19,3},{4,20},{20... | collective-permute-start | bytes 1572872 | tf_op jit(solution)/shard_map/ppermute | solution.py:353
  39.1 0.3 shard_map.81.real_ref
  39.5 0.6 collective-permute-start.10
  40.1 1.2 %copy-done.4 = f32[1,2,2,256,256]{4,3,2,1,0:T(8,128)S(1)} copy-done((f32[1,2,2,256,256]{4,3,2,1,0:T(8,128)S(1)}, f32[1,2,2,256,256]{4,3,2,1,0:T(8,128)}, u32[]{:S(2)}) %copy-start.4) | copy-done | bytes 1048600
  41.3 2.2 %shard_map.82.source_ref = f32[2,2,256,256]{3,2,1,0:T(8,128)S(1)} custom-call(f32[2,2,256,256]{3,2,1,0:T(8,128)S(1)} %bitcast.15, f32[2,256,256]{2,1,0:T(8,128)S(1)} %shard_map.81.real_ref, f32[2,256,256]{2,1,0:T(8,128)S(1)} %shard_map.78.imag_ref), custom_call_target="tpu_custom_call" | custom-call | flops 1610612736 | bytes 3145728 | tf_op jit(solution)/shard_map/pallas_call | solution.py:288
  43.5 8.9 %collective-permute-done.8.imag_ref = f32[2,256,256]{2,1,0:T(8,128)S(1)} collective-permute-done((f32[2,256,256]{2,1,0:T(8,128)S(1)}, f32[2,256,256]{2,1,0:T(8,128)S(1)}, u32[]{:S(2)}, u32[]{:S(2)}) %collective-permute-start.8) | collective-permute-done | bytes 524320 | tf_op jit(solution)/shard_map/ppermute | solution.py:353
  52.4 0.6 shard_map.79.half_ref
  53.0 9.6 %collective-permute-done.10.real_ref = f32[2,256,256]{2,1,0:T(8,128)S(1)} collective-permute-done((f32[2,256,256]{2,1,0:T(8,128)S(1)}, f32[2,256,256]{2,1,0:T(8,128)S(1)}, u32[]{:S(2)}, u32[]{:S(2)}) %collective-permute-start.10) | collective-permute-done | bytes 524320 | tf_op jit(solution)/shard_map/ppermute | solution.py:358
  62.6 2.5 %shard_map.83 = f32[2,2,256,256]{3,2,1,0:T(8,128)} custom-call(s32[1]{0:T(128)} %bitcast.flag_ref, f32[2,2,256,256]{3,2,1,0:T(8,128)S(1)} %get-tuple-element.15.bridge_ref, f32[2,2,256,256]{3,2,1,0:T(8,128)S(1)} %shard_map.79.half_ref, f32[2,256,256]{2,1,0:T(8,128)S(1)} %collective-permute-done.10.real_ref, f32[2,2,256,256]{3,2,1,0:T(8,128)S(1)} %shard_map.82.source_ref), custom_call_target="tpu_custom_call" | custom-call | flops 1207959552 | bytes 4718596 | tf_op jit(solution)/shard_map/pallas_call | solution.py:288
  (16 shorter events, 0.0 us)
Async XLA Ops:
  0.0 3.1 %copy-start.3 = (f32[1,2,2,256,256]{4,3,2,1,0:T(8,128)S(1)}, f32[1,2,2,256,256]{4,3,2,1,0:T(8,128)}, u32[]{:S(2)}) copy-start(f32[1,2,2,256,256]{4,3,2,1,0:T(8,128)} %param.7) | copy-start | bytes 3145732
  1.4 3.3 %collective-permute-start = (f32[2,256,256]{2,1,0:T(8,128)S(1)}, f32[2,256,256]{2,1,0:T(8,128)S(1)}, u32[]{:S(2)}, u32[]{:S(2)}) collective-permute-start(f32[2,256,256]{2,1,0:T(8,128)S(1)} %get-tuple-element.20.refs_0_), channel_id=1, source_target_pairs={{0,1},{1,0},{2,3},{3,2},{4,5},{5,4},{6,7},{7,6},{8,9},{9,8},{10,11... | collective-permute-start | bytes 1572872 | tf_op jit(solution)/shard_map/ppermute | solution.py:317
  1.5 2.2 %copy-start = (s32[3]{0:T(128)S(1)}, s32[3]{0:T(128)}, u32[]{:S(2)}) copy-start(s32[3]{0:T(128)} %offsets_ref.1) | copy-start | bytes 40
  1.5 2.2 %copy-start.1 = (f32[3]{0:T(128)S(1)}, f32[3]{0:T(128)}, u32[]{:S(2)}) copy-start(f32[3]{0:T(128)} %coupling_ref.1) | copy-start | bytes 40
  1.5 2.1 %copy-start.2 = (f32[3]{0:T(128)S(1)}, f32[3]{0:T(128)}, u32[]{:S(2)}) copy-start(f32[3]{0:T(128)} %occupation_ref.1) | copy-start | bytes 40
  1.5 14.3 %collective-permute-start.5 = (f32[2,256,256]{2,1,0:T(8,128)S(1)}, f32[2,256,256]{2,1,0:T(8,128)S(1)}, u32[]{:S(2)}, u32[]{:S(2)}) collective-permute-start(f32[2,256,256]{2,1,0:T(8,128)S(1)} %get-tuple-element.19.refs_2_.refs_0_), channel_id=1, source_target_pairs={{0,2},{1,3},{2,0},{3,1},{4,6},{5,7},{6,4},{7,5},{8,10},{9,11},{10,... | collective-permute-start | bytes 1572872 | tf_op jit(solution)/shard_map/ppermute | solution.py:317
  3.1 30.6 %collective-permute-start.4 = (f32[2,2,256,256]{3,2,1,0:T(8,128)S(1)}, f32[2,2,256,256]{3,2,1,0:T(8,128)S(1)}, u32[]{:S(2)}, u32[]{:S(2)}) collective-permute-start(f32[2,2,256,256]{3,2,1,0:T(8,128)S(1)} %bitcast.13), channel_id=1, source_target_pairs={{0,16},{16,0},{1,17},{17,1},{2,18},{18,2},{3,19},{19,3},{4,20},{20... | collective-permute-start | bytes 3145736 | tf_op jit(solution)/shard_map/ppermute | solution.py:333
  5.1 16.2 %collective-permute-start.1 = (f32[2,256,256]{2,1,0:T(8,128)S(1)}, f32[2,256,256]{2,1,0:T(8,128)S(1)}, u32[]{:S(2)}, u32[]{:S(2)}) collective-permute-start(f32[2,256,256]{2,1,0:T(8,128)S(1)} %get-tuple-element.12), channel_id=1, source_target_pairs={{0,4},{1,5},{2,6},{3,7},{4,0},{5,1},{6,2},{7,3},{8,12},{9,13},{10,... | collective-permute-start | bytes 1572872 | tf_op jit(solution)/shard_map/ppermute | solution.py:317
  5.6 16.6 %collective-permute-start.2 = (f32[2,256,256]{2,1,0:T(8,128)S(1)}, f32[2,256,256]{2,1,0:T(8,128)S(1)}, u32[]{:S(2)}, u32[]{:S(2)}) collective-permute-start(f32[2,256,256]{2,1,0:T(8,128)S(1)} %get-tuple-element.13), channel_id=1, source_target_pairs={{4,8},{5,9},{6,10},{7,11},{8,4},{9,5},{10,6},{11,7},{20,24},{21,25... | collective-permute-start | bytes 1572872 | tf_op jit(solution)/shard_map/ppermute | solution.py:317
  16.2 13.9 %collective-permute-start.6 = (f32[2,256,256]{2,1,0:T(8,128)S(1)}, f32[2,256,256]{2,1,0:T(8,128)S(1)}, u32[]{:S(2)}, u32[]{:S(2)}) collective-permute-start(f32[2,256,256]{2,1,0:T(8,128)S(1)} %get-tuple-element.17), channel_id=1, source_target_pairs={{0,4},{1,5},{2,6},{3,7},{4,0},{5,1},{6,2},{7,3},{8,12},{9,13},{10,... | collective-permute-start | bytes 1572872 | tf_op jit(solution)/shard_map/ppermute | solution.py:317
  16.7 16.4 %collective-permute-start.7 = (f32[2,256,256]{2,1,0:T(8,128)S(1)}, f32[2,256,256]{2,1,0:T(8,128)S(1)}, u32[]{:S(2)}, u32[]{:S(2)}) collective-permute-start(f32[2,256,256]{2,1,0:T(8,128)S(1)} %get-tuple-element.18), channel_id=1, source_target_pairs={{4,8},{5,9},{6,10},{7,11},{8,4},{9,5},{10,6},{11,7},{20,24},{21,25... | collective-permute-start | bytes 1572872 | tf_op jit(solution)/shard_map/ppermute | solution.py:317
  22.5 11.2 %copy-start.5 = (f32[1,256,256]{2,1,0:T(8,128)S(1)}, f32[1,256,256]{2,1,0:T(8,128)}, u32[]{:S(2)}) copy-start(f32[1,256,256]{2,1,0:T(8,128)} %param.9) | copy-start | bytes 786436
  22.5 14.6 %collective-permute-start.3 = (f32[2,256,256]{2,1,0:T(8,128)S(1)}, f32[2,256,256]{2,1,0:T(8,128)S(1)}, u32[]{:S(2)}, u32[]{:S(2)}) collective-permute-start(f32[2,256,256]{2,1,0:T(8,128)S(1)} %shard_map.75), channel_id=1, source_target_pairs={{0,2},{1,3},{2,0},{3,1},{4,6},{5,7},{6,4},{7,5},{8,10},{9,11},{10,... | collective-permute-start | bytes 1572872 | tf_op jit(solution)/shard_map/ppermute | solution.py:317
  33.6 0.7 %copy-start.6 = (s32[1,4,4]{2,1,0:T(4,128)S(1)}, s32[1,4,4]{2,1,0:T(4,128)}, u32[]{:S(2)}) copy-start(s32[1,4,4]{2,1,0:T(4,128)} %param.10) | copy-start | bytes 196
  33.6 5.6 %collective-permute-start.9 = (f32[2,256,256]{2,1,0:T(8,128)S(1)}, f32[2,256,256]{2,1,0:T(8,128)S(1)}, u32[]{:S(2)}, u32[]{:S(2)}) collective-permute-start(f32[2,256,256]{2,1,0:T(8,128)S(1)} %shard_map.80), channel_id=1, source_target_pairs={{0,1},{1,0},{2,3},{3,2},{4,5},{5,4},{6,7},{7,6},{8,9},{9,8},{10,11... | collective-permute-start | bytes 1572872 | tf_op jit(solution)/shard_map/ppermute | solution.py:317
  37.6 14.9 %collective-permute-start.8 = (f32[2,256,256]{2,1,0:T(8,128)S(1)}, f32[2,256,256]{2,1,0:T(8,128)S(1)}, u32[]{:S(2)}, u32[]{:S(2)}) collective-permute-start(f32[2,256,256]{2,1,0:T(8,128)S(1)} %shard_map.78.imag_ref), channel_id=1, source_target_pairs={{0,16},{16,0},{1,17},{17,1},{2,18},{18,2},{3,19},{19,3},{4,20},{20... | collective-permute-start | bytes 1572872 | tf_op jit(solution)/shard_map/ppermute | solution.py:353
  39.5 23.1 %collective-permute-start.10 = (f32[2,256,256]{2,1,0:T(8,128)S(1)}, f32[2,256,256]{2,1,0:T(8,128)S(1)}, u32[]{:S(2)}, u32[]{:S(2)}) collective-permute-start(f32[2,256,256]{2,1,0:T(8,128)S(1)} %shard_map.81.real_ref), channel_id=1, source_target_pairs={{0,16},{16,0},{1,17},{17,1},{2,18},{18,2},{3,19},{19,3},{4,20},{20... | collective-permute-start | bytes 1572872 | tf_op jit(solution)/shard_map/ppermute | solution.py:358
  40.1 1.2 %copy-start.4 = (f32[1,2,2,256,256]{4,3,2,1,0:T(8,128)S(1)}, f32[1,2,2,256,256]{4,3,2,1,0:T(8,128)}, u32[]{:S(2)}) copy-start(f32[1,2,2,256,256]{4,3,2,1,0:T(8,128)} %param.7) | copy-start | bytes 3145732

commit v2 on v1

--- a/solution.py
+++ b/solution.py
@@ -10,6 +10,8 @@
 VMEM = pl.BlockSpec(memory_space=pltpu.VMEM)
 SMEM = pl.BlockSpec(memory_space=pltpu.SMEM)
 CHUNK_ROWS = 32
+PIECES = 2
+FIRST_PARTS, PARTS = 5, 8
 SMALL_VMEM = 8 * 1024 * 1024
 LARGE_VMEM = 24 * 1024 * 1024
 
@@ -236,23 +238,41 @@
             bridge_ref[energy, part] = bridge[part]
 
 
-def source_kernel(retarded_ref, real_ref, imag_ref, out_ref):
+def row_windows(size):
+    cut = size * FIRST_PARTS // PARTS
+    return [slice(0, cut), slice(cut, size)]
+
+
+def source_kernel(pieces, retarded_ref, *refs):
+    real_refs, imag_refs, out_ref = refs[:pieces], refs[pieces : 2 * pieces], refs[-1]
     for energy in range(retarded_ref.shape[0]):
         retarded = split_pair((retarded_ref[energy, 0], retarded_ref[energy, 1]))
-        inner = times(retarded, split_pair((real_ref[energy], imag_ref[energy])))
+        real = jnp.concatenate([ref[energy] for ref in real_refs], axis=0)
+        imag = jnp.concatenate([ref[energy] for ref in imag_refs], axis=0)
+        inner = times(retarded, split_pair((real, imag)))
         outer = times_adjoint(split_pair(inner), retarded)
         for part in range(2):
             out_ref[energy, part] = outer[part]
 
 
-def imag_half_kernel(bridge_ref, imag_ref, out_ref):
+def piece_kernel(window, bridge_ref, real_ref, imag_ref, out_ref):
+    for energy in range(bridge_ref.shape[0]):
+        bridge = split_pair((bridge_ref[energy, 0, :, window], bridge_ref[energy, 1, :, window]))
+        inner = times(bridge, split_pair((real_ref[energy], imag_ref[energy])))
+        for part in range(2):
+            out_ref[energy, part] = inner[part]
+
+
+def imag_half_kernel(window, bridge_ref, imag_ref, total_ref, out_ref):
     for energy in range(bridge_ref.shape[0]):
         imag = split(imag_ref[energy])
-        out_ref[energy, 0] = -dot3(split(bridge_ref[energy, 1]), imag)
-        out_ref[energy, 1] = dot3(split(bridge_ref[energy, 0]), imag)
-
-
-def finish_kernel(flag_ref, bridge_ref, half_ref, real_ref, source_ref, out_ref):
+        real_share = dot3(split(bridge_ref[energy, 1, :, window]), imag)
+        imag_share = dot3(split(bridge_ref[energy, 0, :, window]), imag)
+        out_ref[energy, 0] = total_ref[energy, 0] - real_share
+        out_ref[energy, 1] = total_ref[energy, 1] + imag_share
+
+
+def finish_kernel(window, flag_ref, bridge_ref, half_ref, real_ref, source_ref, out_ref):
     @pl.when(flag_ref[0] == 0)
     def _():
         out_ref[...] = source_ref[...]
@@ -262,7 +282,8 @@
         for energy in range(bridge_ref.shape[0]):
             bridge = split_pair((bridge_ref[energy, 0], bridge_ref[energy, 1]))
             real = split(real_ref[energy])
-            inner = tuple(half_ref[energy, part] + dot3(bridge[part], real) for part in range(2))
+            left = [(high[:, window], low[:, window]) for high, low in bridge]
+            inner = tuple(half_ref[energy, part] + dot3(left[part], real) for part in range(2))
             outer = times_adjoint(split_pair(inner), bridge)
             for part in range(2):
                 out_ref[energy, part] = source_ref[energy, part] + outer[part]
@@ -299,6 +320,10 @@
     )(*inputs)
 
 
+def after(value, *gates):
+    return lax.optimization_barrier((value,) + gates)[0]
+
+
 def body(retarded, lesser_prev, hopping, hop_mask, offsets, coupling, occupation):
     devices = lax.axis_size("energy")
     slabs = lax.axis_size("slab")
@@ -326,19 +351,51 @@
             second_lines.append((i, other))
     ahead = [(s, (s + 1) % slabs) for s in range(slabs)]
 
-    real, imag = lesser_prev[0, :, 0], lesser_prev[0, :, 1]
     blocks = retarded[0]
-    imag_sibling = permute(imag, cores)
-    real_beside = permute(real, across)
+    size = blocks.shape[-1]
+    windows = row_windows(size)
     behind = lax.ppermute(blocks, "slab", ahead)
 
-    send1, send2 = combine(weights, bases[0], [imag, imag_sibling, real], 2)
-    got1, got2 = permute(send1, first_lines), permute(send2, second_lines)
-    send3, send4 = combine(weights, bases[1], [real_beside, imag_sibling, real], 2)
-    got3, got4 = permute(send3, first_lines), permute(send4, second_lines)
-    imag_beside = permute(
-        combine(weights, bases[2], [imag, imag_sibling, got1, got2], 1), across
-    )
+    reals, imags, reals_behind, imags_behind = [], [], [], []
+    gates = None
+    for number, window in enumerate(windows):
+        real, imag = lesser_prev[0, :, 0, window], lesser_prev[0, :, 1, window]
+        real_sent, imag_own = real, imag
+        imag_sibling = permute(imag, cores)
+        if gates is not None:
+            real_sent = after(real, gates[0])
+            imag_own = after(imag, gates[1], gates[2])
+        real_beside = permute(real_sent, across)
+        send1, send2 = combine(weights, bases[0], [imag_own, imag_sibling, real], 2)
+        got1, got2 = permute(send1, first_lines), permute(send2, second_lines)
+        if gates is not None:
+            real_beside = after(real_beside, gates[3])
+        send3, send4 = combine(weights, bases[1], [real_beside, imag_sibling, real], 2)
+        got3, got4 = permute(send3, first_lines), permute(send4, second_lines)
+        if number == PIECES - 1:
+            got1, behind = lax.optimization_barrier((got1, behind))
+        if gates is not None:
+            got1 = after(got1, imags_behind[-1])
+        beside_sum = combine(weights, bases[2], [imag, imag_sibling, got1, got2], 1)
+        imag_beside = permute(beside_sum, across)
+        if gates is not None:
+            pass
+        self_imag = combine(
+            weights, bases[3], [imag, imag_sibling, imag_beside, got1, got2, got3, got4], 1
+        )
+        real_late = real if gates is None else after(real, self_imag)
+        sibling_sum = combine(weights, bases[4], [real_late, real_beside, got1, got2, got3, got4], 1)
+        real_sibling = permute(sibling_sum, cores)
+        if gates is not None:
+            real_sibling = after(real_sibling, reals_behind[-1])
+        self_real = combine(weights, bases[5], [real, real_beside, got3, got4, real_sibling], 1)
+        gates = (imag_beside, self_imag, sibling_sum, self_real)
+        imags.append(self_imag)
+        reals.append(self_real)
+        imags_behind.append(lax.ppermute(self_imag, "slab", ahead))
+        reals_behind.append(lax.ppermute(self_real, "slab", ahead))
+
+    behind, reals[-1] = lax.optimization_barrier((behind, reals[-1]))
     coupled, bridge = call(
         functools.partial(bridge_kernel, hop_mask.shape[-1]),
         [hop_mask[0], hopping[0], blocks, behind],
@@ -346,24 +403,32 @@
         [blocks, blocks],
         12,
     )
-    imag_beside, bridge = lax.optimization_barrier((imag_beside, bridge))
-    self_imag = combine(
-        weights, bases[3], [imag, imag_sibling, imag_beside, got1, got2, got3, got4], 1
-    )
-    self_imag_behind = lax.ppermute(self_imag, "slab", ahead)
-    real_sibling = permute(
-        combine(weights, bases[4], [real, real_beside, got1, got2, got3, got4], 1), cores
-    )
-    self_real = combine(weights, bases[5], [real, real_beside, got3, got4, real_sibling], 1)
-    self_real_behind = lax.ppermute(self_real, "slab", ahead)
-
-    (source,) = call(source_kernel, [blocks, self_real, self_imag], [VMEM] * 3, [blocks], 16)
-    (half,) = call(imag_half_kernel, [bridge, self_imag_behind], [VMEM] * 2, [blocks], 4)
+    (source,) = call(
+        functools.partial(source_kernel, PIECES),
+        [blocks] + reals + imags,
+        [VMEM] * (1 + 2 * PIECES),
+        [blocks],
+        16,
+    )
+    (total,) = call(
+        functools.partial(piece_kernel, windows[0]),
+        [bridge, reals_behind[0], imags_behind[0]],
+        [VMEM] * 3,
+        [blocks],
+        8,
+    )
+    (half,) = call(
+        functools.partial(imag_half_kernel, windows[-1]),
+        [bridge, imags_behind[-1], after(total, source)],
+        [VMEM] * 3,
+        [blocks],
+        4,
+    )
     position = lax.axis_index("slab")
     turn_flag = (position == 1).astype(jnp.int32).reshape(1)
     (lesser,) = call(
-        finish_kernel,
-        [turn_flag, bridge, half, self_real_behind, source],
+        functools.partial(finish_kernel, windows[-1]),
+        [turn_flag, bridge, half, reals_behind[-1], source],
         [SMEM] + [VMEM] * 4,
         [blocks],
         12,

time: 65.5 us -> 60.1 us (0.918)
  waiting for transfers between devices: 34.9 us -> 15.8 us
  starting transfers between devices: 15.4 us -> 27.5 us
  Pallas kernels: 11.5 us -> 12.7 us
    ppermute x2 -> x4, waiting for transfers between devices: 18.5 us -> 1.78 us  [the longest x2 1.78 us: body(): reals_behind.append(lax.ppermute(self_real, 'slab', ahead))]
    ppermute x8 -> x16, starting transfers between devices: 12.7 us -> 23 us  [permute(): return lax.ppermute(value, 'energy', pairs)]
    ppermute x8 -> x16, waiting for transfers between devices: 16.4 us -> 14 us  [permute(): return lax.ppermute(value, 'energy', pairs)]
    ppermute x2 -> x4, starting transfers between devices: 2.16 us -> 3.92 us  [the longest x2 2.78 us: body(): imags_behind.append(lax.ppermute(self_imag, 'slab', ahead))]
    pallas_call x4 -> x5, Pallas kernels: 8.09 us -> 9.16 us  [call(): pl.pallas_call(kernel, out_shape=[jax.ShapeDtypeStruct(array.shape, jnp.f...]
    squeeze x1 -> x2, local copies, waits for them, and re-layouts: 1.36 us -> 2.26 us  [body(): real, imag = (lesser_prev[0, :, 0, window], lesser_prev[0, :, 1, window])]
    unnamed x14 -> x18, local copies, waits for them, and re-layouts: 1.83 us -> 1.34 us
    pallas_call x6 -> x12, Pallas kernels: 2.31 us -> 2.4 us  [combine(): pl.pallas_call(functools.partial(combine_kernel, base, counts), out_shape...]
  transfers between devices with their start and end apart: 11 -> 21, of which waited for: 6 -> 9; matrix products, arithmetic and copies ran while one was open for 0% -> 2% of each run, Pallas kernels for 14% -> 17%
where the time goes in v2:
time: 60.1 us; the launch traced here: 59.8 us
  starting transfers between devices  27.5 us (46%)
  waiting for transfers between devices  15.8 us (26%)
  Pallas kernels  12.7 us (21%)
  local copies, waits for them, and re-layouts  3.6 us (6%)
    ppermute x16, starting transfers between devices, permute(): return lax.ppermute(value, 'energy', pairs)  23 us
    ppermute x16, waiting for transfers between devices, permute(): return lax.ppermute(value, 'energy', pairs)  14 us
    pallas_call x5, Pallas kernels, call(): pl.pallas_call(kernel, out_shape=[jax.ShapeDtypeStruct(array.shape, jnp.f...  9.16 us
    ppermute x2, starting transfers between devices, body(): imags_behind.append(lax.ppermute(self_imag, 'slab', ahead))  2.78 us
    pallas_call x12, Pallas kernels, combine(): pl.pallas_call(functools.partial(combine_kernel, base, counts), out_shape...  2.4 us
    squeeze x2, local copies, waits for them, and re-layouts, body(): real, imag = (lesser_prev[0, :, 0, window], lesser_prev[0, :, 1, window])  2.26 us
    ppermute x2, waiting for transfers between devices, body(): reals_behind.append(lax.ppermute(self_real, 'slab', ahead))  1.78 us
    unnamed x18, local copies, waits for them, and re-layouts  1.34 us
  transfers between devices with their start and end apart: 21, of which 9 were waited for; matrix products, arithmetic and copies ran while one was open for 2% of the time, Pallas kernels for 17%

profile of v2, /device:TPU:10, one launch (start us, length us, event | category | flops | bytes accessed | tf_op | source)
XLA Modules:
  0.0 59.8 jit_solution(11392057675401854080)
XLA Ops:
  0.0 1.2 %slice_bitcast_fusion = (f32[2,160,256]{2,1,0:T(8,128)S(1)}, f32[2,160,256]{2,1,0:T(8,128)S(1)}) fusion(f32[1,2,2,256,256]{4,3,2,1,0:T(8,128)} %param.8), kind=kLoop, calls=%fused_computation | loop fusion | bytes 1310720 | tf_op jit(solution)/shard_map/squeeze | solution.py:362
  1.3 1.6 %collective-permute-start.4 = (f32[2,160,256]{2,1,0:T(8,128)S(1)}, f32[2,160,256]{2,1,0:T(8,128)S(1)}, u32[]{:S(2)}, u32[]{:S(2)}) collective-permute-start(f32[2,160,256]{2,1,0:T(8,128)S(1)} %get-tuple-element.47.refs_2_.refs_0_), channel_id=1, source_target_pairs={{0,2},{1,3},{2,0},{3,1},{4,6},{5,7},{6,4},{7,5},{8,10},{9,11},{10,... | collective-permute-start | bytes 983048 | tf_op jit(solution)/shard_map/ppermute | solution.py:342
  2.9 0.5 collective-permute-start.9
  3.5 1.1 %shard_map.73.weights_ref = f32[136,8,128]{2,1,0:T(8,128)S(1)} custom-call(s32[3]{0:T(128)S(1)} %copy-done, f32[3]{0:T(128)S(1)} %copy-done.1, f32[3]{0:T(128)S(1)} %copy-done.2), custom_call_target="tpu_custom_call" | custom-call | tf_op jit(solution)/shard_map/pallas_call | solution.py:333
  4.8 0.5 collective-permute-start.1
  5.3 4.6 %collective-permute-start.2 = (f32[2,160,256]{2,1,0:T(8,128)S(1)}, f32[2,160,256]{2,1,0:T(8,128)S(1)}, u32[]{:S(2)}, u32[]{:S(2)}) collective-permute-start(f32[2,160,256]{2,1,0:T(8,128)S(1)} %get-tuple-element.26), channel_id=1, source_target_pairs={{4,8},{5,9},{6,10},{7,11},{8,4},{9,5},{10,6},{11,7},{20,24},{21,25... | collective-permute-start | bytes 983048 | tf_op jit(solution)/shard_map/ppermute | solution.py:342
  9.9 1.5 %collective-permute-done.4.refs_0_.refs_1_ = f32[2,160,256]{2,1,0:T(8,128)S(1)} collective-permute-done((f32[2,160,256]{2,1,0:T(8,128)S(1)}, f32[2,160,256]{2,1,0:T(8,128)S(1)}, u32[]{:S(2)}, u32[]{:S(2)}) %collective-permute-start.4) | collective-permute-done | bytes 327712 | tf_op jit(solution)/shard_map/ppermute | solution.py:342
  11.7 0.5 collective-permute-start.5
  12.2 4.6 %collective-permute-start.6 = (f32[2,160,256]{2,1,0:T(8,128)S(1)}, f32[2,160,256]{2,1,0:T(8,128)S(1)}, u32[]{:S(2)}, u32[]{:S(2)}) collective-permute-start(f32[2,160,256]{2,1,0:T(8,128)S(1)} %get-tuple-element.28), channel_id=1, source_target_pairs={{4,8},{5,9},{6,10},{7,11},{8,4},{9,5},{10,6},{11,7},{20,24},{21,25... | collective-permute-start | bytes 983048 | tf_op jit(solution)/shard_map/ppermute | solution.py:342
  16.8 0.9 %collective-permute-done.2.refs_3_.refs_4_ = f32[2,160,256]{2,1,0:T(8,128)S(1)} collective-permute-done((f32[2,160,256]{2,1,0:T(8,128)S(1)}, f32[2,160,256]{2,1,0:T(8,128)S(1)}, u32[]{:S(2)}, u32[]{:S(2)}) %collective-permute-start.2) | collective-permute-done | bytes 327712 | tf_op jit(solution)/shard_map/ppermute | solution.py:342
  17.9 0.7 %collective-permute-start.3 = (f32[2,160,256]{2,1,0:T(8,128)S(1)}, f32[2,160,256]{2,1,0:T(8,128)S(1)}, u32[]{:S(2)}, u32[]{:S(2)}) collective-permute-start(f32[2,160,256]{2,1,0:T(8,128)S(1)} %shard_map.75), channel_id=1, source_target_pairs={{0,2},{1,3},{2,0},{3,1},{4,6},{5,7},{6,4},{7,5},{8,10},{9,11},{10,... | collective-permute-start | bytes 983048 | tf_op jit(solution)/shard_map/ppermute | solution.py:342
  18.6 2.8 %collective-permute-done.5.refs_5_.refs_4_.refs_2_ = f32[2,160,256]{2,1,0:T(8,128)S(1)} collective-permute-done((f32[2,160,256]{2,1,0:T(8,128)S(1)}, f32[2,160,256]{2,1,0:T(8,128)S(1)}, u32[]{:S(2)}, u32[]{:S(2)}) %collective-permute-start.5) | collective-permute-done | bytes 327712 | tf_op jit(solution)/shard_map/ppermute | solution.py:342
  21.4 3.0 %collective-permute-done.6.refs_6_.refs_5_.refs_3_ = f32[2,160,256]{2,1,0:T(8,128)S(1)} collective-permute-done((f32[2,160,256]{2,1,0:T(8,128)S(1)}, f32[2,160,256]{2,1,0:T(8,128)S(1)}, u32[]{:S(2)}, u32[]{:S(2)}) %collective-permute-start.6) | collective-permute-done | bytes 327712 | tf_op jit(solution)/shard_map/ppermute | solution.py:342
  24.8 1.1 %slice_bitcast_fusion.2 = (f32[2,96,256]{2,1,0:T(8,128)S(1)}, f32[2,96,256]{2,1,0:T(8,128)S(1)}) fusion(f32[1,2,2,256,256]{4,3,2,1,0:T(8,128)} %param.8), kind=kLoop, calls=%fused_computation.2 | loop fusion | bytes 786432 | tf_op jit(solution)/shard_map/squeeze | solution.py:362
  25.8 0.6 collective-permute-start.7
  26.7 1.6 %collective-permute-start.14 = (f32[2,160,256]{2,1,0:T(8,128)S(1)}, f32[2,160,256]{2,1,0:T(8,128)S(1)}, u32[]{:S(2)}, u32[]{:S(2)}) collective-permute-start(f32[2,160,256]{2,1,0:T(8,128)S(1)} %shard_map.77.refs_2_), channel_id=1, source_target_pairs={{0,16},{16,0},{1,17},{17,1},{2,18},{18,2},{3,19},{19,3},{4,20},{20... | collective-permute-start | bytes 983048 | tf_op jit(solution)/shard_map/ppermute | solution.py:395
  29.0 3.6 %collective-permute-start.15 = (f32[2,96,256]{2,1,0:T(8,128)S(1)}, f32[2,96,256]{2,1,0:T(8,128)S(1)}, u32[]{:S(2)}, u32[]{:S(2)}) collective-permute-start(f32[2,96,256]{2,1,0:T(8,128)S(1)} %get-tuple-element.38), channel_id=1, source_target_pairs={{4,8},{5,9},{6,10},{7,11},{8,4},{9,5},{10,6},{11,7},{20,24},{21,25... | collective-permute-start | bytes 589832 | tf_op jit(solution)/shard_map/ppermute | solution.py:342
  32.9 1.9 %collective-permute-done.10.refs_0_.refs_1_ = f32[2,96,256]{2,1,0:T(8,128)S(1)} collective-permute-done((f32[2,96,256]{2,1,0:T(8,128)S(1)}, f32[2,96,256]{2,1,0:T(8,128)S(1)}, u32[]{:S(2)}, u32[]{:S(2)}) %collective-permute-start.10) | collective-permute-done | bytes 196640 | tf_op jit(solution)/shard_map/ppermute | solution.py:342
  35.6 3.6 %collective-permute-start.13 = (f32[2,96,256]{2,1,0:T(8,128)S(1)}, f32[2,96,256]{2,1,0:T(8,128)S(1)}, u32[]{:S(2)}, u32[]{:S(2)}) collective-permute-start(f32[2,96,256]{2,1,0:T(8,128)S(1)} %get-tuple-element.35), channel_id=1, source_target_pairs={{4,8},{5,9},{6,10},{7,11},{8,4},{9,5},{10,6},{11,7},{20,24},{21,25... | collective-permute-start | bytes 589832 | tf_op jit(solution)/shard_map/ppermute | solution.py:342
  39.3 1.6 %collective-permute-start.16 = (f32[2,96,256]{2,1,0:T(8,128)S(1)}, f32[2,96,256]{2,1,0:T(8,128)S(1)}, u32[]{:S(2)}, u32[]{:S(2)}) collective-permute-start(f32[2,96,256]{2,1,0:T(8,128)S(1)} %shard_map.82), channel_id=1, source_target_pairs={{0,2},{1,3},{2,0},{3,1},{4,6},{5,7},{6,4},{7,5},{8,10},{9,11},{10,... | collective-permute-start | bytes 589832 | tf_op jit(solution)/shard_map/ppermute | solution.py:342
  40.9 0.5 collective-permute-start.18
  41.5 1.7 %collective-permute-done.13.refs_6_.refs_5_.refs_3_ = f32[2,96,256]{2,1,0:T(8,128)S(1)} collective-permute-done((f32[2,96,256]{2,1,0:T(8,128)S(1)}, f32[2,96,256]{2,1,0:T(8,128)S(1)}, u32[]{:S(2)}, u32[]{:S(2)}) %collective-permute-start.13) | collective-permute-done | bytes 196640 | tf_op jit(solution)/shard_map/ppermute | solution.py:342
  43.1 2.0 %collective-permute-done.16.refs_2_ = f32[2,96,256]{2,1,0:T(8,128)S(1)} collective-permute-done((f32[2,96,256]{2,1,0:T(8,128)S(1)}, f32[2,96,256]{2,1,0:T(8,128)S(1)}, u32[]{:S(2)}, u32[]{:S(2)}) %collective-permute-start.16) | collective-permute-done | bytes 196640 | tf_op jit(solution)/shard_map/ppermute | solution.py:342
  45.6 1.2 %collective-permute-start.19 = (f32[2,96,256]{2,1,0:T(8,128)S(1)}, f32[2,96,256]{2,1,0:T(8,128)S(1)}, u32[]{:S(2)}, u32[]{:S(2)}) collective-permute-start(f32[2,96,256]{2,1,0:T(8,128)S(1)} %shard_map.83.refs_3_), channel_id=1, source_target_pairs={{0,16},{16,0},{1,17},{17,1},{2,18},{18,2},{3,19},{19,3},{4,20},{20... | collective-permute-start | bytes 589832 | tf_op jit(solution)/shard_map/ppermute | solution.py:395
  46.8 1.8 %collective-permute-done.18.real_ref = f32[2,160,256]{2,1,0:T(8,128)S(1)} collective-permute-done((f32[2,160,256]{2,1,0:T(8,128)S(1)}, f32[2,160,256]{2,1,0:T(8,128)S(1)}, u32[]{:S(2)}, u32[]{:S(2)}) %collective-permute-start.18) | collective-permute-done | bytes 327712 | tf_op jit(solution)/shard_map/ppermute | solution.py:396
  48.7 0.6 %collective-permute-start.20 = (f32[2,96,256]{2,1,0:T(8,128)S(1)}, f32[2,96,256]{2,1,0:T(8,128)S(1)}, u32[]{:S(2)}, u32[]{:S(2)}) collective-permute-start(f32[2,96,256]{2,1,0:T(8,128)S(1)} %shard_map.85.refs_1_), channel_id=1, source_target_pairs={{0,16},{16,0},{1,17},{17,1},{2,18},{18,2},{3,19},{19,3},{4,20},{20... | collective-permute-start | bytes 589832 | tf_op jit(solution)/shard_map/ppermute | solution.py:396
  49.4 1.2 %copy-done.6 = f32[2,2,256,256]{3,2,1,0:T(8,128)S(1)} copy-done((f32[2,2,256,256]{3,2,1,0:T(8,128)S(1)}, f32[2,2,256,256]{3,2,1,0:T(8,128)}, u32[]{:S(2)}) %copy-start.6) | copy-done | bytes 1048600
  50.6 2.8 %shard_map.86 = (f32[2,2,256,256]{3,2,1,0:T(8,128)}, f32[2,2,256,256]{3,2,1,0:T(8,128)S(1)}) custom-call(s32[4,4]{1,0:T(4,128)S(1)} %bitcast.25, f32[256,256]{1,0:T(8,128)S(1)} %bitcast.24, f32[2,2,256,256]{3,2,1,0:T(8,128)S(1)} %bitcast.22, f32[2,2,256,256]{3,2,1,0:T(8,128)S(1)} %copy-done.6), custom_call_target="tpu_custom_call" | custom-call | flops 1207959552 | bytes 4456512 | tf_op jit(solution)/shard_map/pallas_call | solution.py:309
  53.4 1.0 %shard_map.87.total_ref = f32[2,2,256,256]{3,2,1,0:T(8,128)S(1)} custom-call(f32[2,2,256,256]{3,2,1,0:T(8,128)S(1)} %get-tuple-element.42.bridge_ref, f32[2,160,256]{2,1,0:T(8,128)S(1)} %collective-permute-done.18.real_ref, f32[2,160,256]{2,1,0:T(8,128)S(1)} %collective-permute-done.14.imag_ref), custom_call_target="tpu_custom_call" | custom-call | flops 805306368 | bytes 2752512 | tf_op jit(solution)/shard_map/pallas_call | solution.py:309
  54.4 2.2 %shard_map.88.source_ref = f32[2,2,256,256]{3,2,1,0:T(8,128)S(1)} custom-call(f32[2,2,256,256]{3,2,1,0:T(8,128)S(1)} %bitcast.23, f32[2,160,256]{2,1,0:T(8,128)S(1)} %shard_map.80.refs_0_, f32[2,96,256]{2,1,0:T(8,128)S(1)} %shard_map.85.refs_1_, f32[2,160,256]{2,1,0:T(8,128)S(1)} %shard_map.77.refs_2_, f32[2,96,256]{2,1,0:T(8,128)S(1)} %shard_map.83.refs_3_), custom_call_target="tpu_custom_call" | custom-call | flops 1610612736 | bytes 3145728 | tf_op jit(solution)/shard_map/pallas_call | solution.py:309
  56.6 0.6 %shard_map.89.half_ref = f32[2,2,256,256]{3,2,1,0:T(8,128)S(1)} custom-call(f32[2,2,256,256]{3,2,1,0:T(8,128)S(1)} %get-tuple-element.42.bridge_ref, f32[2,96,256]{2,1,0:T(8,128)S(1)} %collective-permute-done.19.imag_ref, f32[2,2,256,256]{3,2,1,0:T(8,128)S(1)} %shard_map.87.total_ref), custom_call_target="tpu_custom_call" | custom-call | flops 402653184 | bytes 3342336 | tf_op jit(solution)/shard_map/pallas_call | solution.py:309
  57.2 2.6 %shard_map.90 = f32[2,2,256,256]{3,2,1,0:T(8,128)} custom-call(s32[1]{0:T(128)} %bitcast.flag_ref, f32[2,2,256,256]{3,2,1,0:T(8,128)S(1)} %get-tuple-element.42.bridge_ref, f32[2,2,256,256]{3,2,1,0:T(8,128)S(1)} %shard_map.89.half_ref, f32[2,96,256]{2,1,0:T(8,128)S(1)} %collective-permute-done.20.real_ref, f32[2,2,256,256]{3,2,1,0:T(8,128)S(1)} %shard_map.88.source_ref), custom_call_target="tpu_custom_call" | custom-call | flops 1207959552 | bytes 4390916 | tf_op jit(solution)/shard_map/pallas_call | solution.py:309
  (48 shorter events, 3.9 us)
Async XLA Ops:
  0.0 2.9 %copy-start.3 = (f32[1,2,2,256,256]{4,3,2,1,0:T(8,128)S(1)}, f32[1,2,2,256,256]{4,3,2,1,0:T(8,128)}, u32[]{:S(2)}) copy-start(f32[1,2,2,256,256]{4,3,2,1,0:T(8,128)} %param.7) | copy-start | bytes 3145732
  1.2 3.3 %collective-permute-start = (f32[2,160,256]{2,1,0:T(8,128)S(1)}, f32[2,160,256]{2,1,0:T(8,128)S(1)}, u32[]{:S(2)}, u32[]{:S(2)}) collective-permute-start(f32[2,160,256]{2,1,0:T(8,128)S(1)} %get-tuple-element.48.refs_0_), channel_id=1, source_target_pairs={{0,1},{1,0},{2,3},{3,2},{4,5},{5,4},{6,7},{7,6},{8,9},{9,8},{10,11... | collective-permute-start | bytes 983048 | tf_op jit(solution)/shard_map/ppermute | solution.py:342
  1.3 2.2 %copy-start = (s32[3]{0:T(128)S(1)}, s32[3]{0:T(128)}, u32[]{:S(2)}) copy-start(s32[3]{0:T(128)} %offsets_ref.1) | copy-start | bytes 40
  1.3 2.2 %copy-start.1 = (f32[3]{0:T(128)S(1)}, f32[3]{0:T(128)}, u32[]{:S(2)}) copy-start(f32[3]{0:T(128)} %coupling_ref.1) | copy-start | bytes 40
  1.3 2.1 %copy-start.2 = (f32[3]{0:T(128)S(1)}, f32[3]{0:T(128)}, u32[]{:S(2)}) copy-start(f32[3]{0:T(128)} %occupation_ref.1) | copy-start | bytes 40
  1.3 10.1 %collective-permute-start.4 = (f32[2,160,256]{2,1,0:T(8,128)S(1)}, f32[2,160,256]{2,1,0:T(8,128)S(1)}, u32[]{:S(2)}, u32[]{:S(2)}) collective-permute-start(f32[2,160,256]{2,1,0:T(8,128)S(1)} %get-tuple-element.47.refs_2_.refs_0_), channel_id=1, source_target_pairs={{0,2},{1,3},{2,0},{3,1},{4,6},{5,7},{6,4},{7,5},{8,10},{9,11},{10,... | collective-permute-start | bytes 983048 | tf_op jit(solution)/shard_map/ppermute | solution.py:342
  2.9 32.1 %collective-permute-start.9 = (f32[2,2,256,256]{3,2,1,0:T(8,128)S(1)}, f32[2,2,256,256]{3,2,1,0:T(8,128)S(1)}, u32[]{:S(2)}, u32[]{:S(2)}) collective-permute-start(f32[2,2,256,256]{3,2,1,0:T(8,128)S(1)} %bitcast.21), channel_id=1, source_target_pairs={{0,16},{16,0},{1,17},{17,1},{2,18},{18,2},{3,19},{19,3},{4,20},{20... | collective-permute-start | bytes 3145736 | tf_op jit(solution)/shard_map/ppermute | solution.py:357
  4.8 12.0 %collective-permute-start.1 = (f32[2,160,256]{2,1,0:T(8,128)S(1)}, f32[2,160,256]{2,1,0:T(8,128)S(1)}, u32[]{:S(2)}, u32[]{:S(2)}) collective-permute-start(f32[2,160,256]{2,1,0:T(8,128)S(1)} %get-tuple-element.25), channel_id=1, source_target_pairs={{0,4},{1,5},{2,6},{3,7},{4,0},{5,1},{6,2},{7,3},{8,12},{9,13},{10,... | collective-permute-start | bytes 983048 | tf_op jit(solution)/shard_map/ppermute | solution.py:342
  5.3 12.4 %collective-permute-start.2 = (f32[2,160,256]{2,1,0:T(8,128)S(1)}, f32[2,160,256]{2,1,0:T(8,128)S(1)}, u32[]{:S(2)}, u32[]{:S(2)}) collective-permute-start(f32[2,160,256]{2,1,0:T(8,128)S(1)} %get-tuple-element.26), channel_id=1, source_target_pairs={{4,8},{5,9},{6,10},{7,11},{8,4},{9,5},{10,6},{11,7},{20,24},{21,25... | collective-permute-start | bytes 983048 | tf_op jit(solution)/shard_map/ppermute | solution.py:342
  11.7 9.7 %collective-permute-start.5 = (f32[2,160,256]{2,1,0:T(8,128)S(1)}, f32[2,160,256]{2,1,0:T(8,128)S(1)}, u32[]{:S(2)}, u32[]{:S(2)}) collective-permute-start(f32[2,160,256]{2,1,0:T(8,128)S(1)} %get-tuple-element.27), channel_id=1, source_target_pairs={{0,4},{1,5},{2,6},{3,7},{4,0},{5,1},{6,2},{7,3},{8,12},{9,13},{10,... | collective-permute-start | bytes 983048 | tf_op jit(solution)/shard_map/ppermute | solution.py:342
  12.2 12.2 %collective-permute-start.6 = (f32[2,160,256]{2,1,0:T(8,128)S(1)}, f32[2,160,256]{2,1,0:T(8,128)S(1)}, u32[]{:S(2)}, u32[]{:S(2)}) collective-permute-start(f32[2,160,256]{2,1,0:T(8,128)S(1)} %get-tuple-element.28), channel_id=1, source_target_pairs={{4,8},{5,9},{6,10},{7,11},{8,4},{9,5},{10,6},{11,7},{20,24},{21,25... | collective-permute-start | bytes 983048 | tf_op jit(solution)/shard_map/ppermute | solution.py:342
  17.9 8.5 %collective-permute-start.3 = (f32[2,160,256]{2,1,0:T(8,128)S(1)}, f32[2,160,256]{2,1,0:T(8,128)S(1)}, u32[]{:S(2)}, u32[]{:S(2)}) collective-permute-start(f32[2,160,256]{2,1,0:T(8,128)S(1)} %shard_map.75), channel_id=1, source_target_pairs={{0,2},{1,3},{2,0},{3,1},{4,6},{5,7},{6,4},{7,5},{8,10},{9,11},{10,... | collective-permute-start | bytes 983048 | tf_op jit(solution)/shard_map/ppermute | solution.py:342
  24.7 4.3 %collective-permute-start.11 = (f32[2,160,256]{2,1,0:T(8,128)S(1)}, f32[2,160,256]{2,1,0:T(8,128)S(1)}, u32[]{:S(2)}, u32[]{:S(2)}) collective-permute-start(f32[2,160,256]{2,1,0:T(8,128)S(1)} %shard_map.78), channel_id=1, source_target_pairs={{0,1},{1,0},{2,3},{3,2},{4,5},{5,4},{6,7},{7,6},{8,9},{9,8},{10,11... | collective-permute-start | bytes 983048 | tf_op jit(solution)/shard_map/ppermute | solution.py:342
  25.8 3.0 %collective-permute-start.7 = (f32[2,96,256]{2,1,0:T(8,128)S(1)}, f32[2,96,256]{2,1,0:T(8,128)S(1)}, u32[]{:S(2)}, u32[]{:S(2)}) collective-permute-start(f32[2,96,256]{2,1,0:T(8,128)S(1)} %get-tuple-element.29.refs_0_), channel_id=1, source_target_pairs={{0,1},{1,0},{2,3},{3,2},{4,5},{5,4},{6,7},{7,6},{8,9},{9,8},{10,11... | collective-permute-start | bytes 589832 | tf_op jit(solution)/shard_map/ppermute | solution.py:342
  26.7 12.5 %collective-permute-start.14 = (f32[2,160,256]{2,1,0:T(8,128)S(1)}, f32[2,160,256]{2,1,0:T(8,128)S(1)}, u32[]{:S(2)}, u32[]{:S(2)}) collective-permute-start(f32[2,160,256]{2,1,0:T(8,128)S(1)} %shard_map.77.refs_2_), channel_id=1, source_target_pairs={{0,16},{16,0},{1,17},{17,1},{2,18},{18,2},{3,19},{19,3},{4,20},{20... | collective-permute-start | bytes 983048 | tf_op jit(solution)/shard_map/ppermute | solution.py:395
  28.3 6.5 %collective-permute-start.10 = (f32[2,96,256]{2,1,0:T(8,128)S(1)}, f32[2,96,256]{2,1,0:T(8,128)S(1)}, u32[]{:S(2)}, u32[]{:S(2)}) collective-permute-start(f32[2,96,256]{2,1,0:T(8,128)S(1)} %get-tuple-element.39.refs_2_.refs_0_), channel_id=1, source_target_pairs={{0,2},{1,3},{2,0},{3,1},{4,6},{5,7},{6,4},{7,5},{8,10},{9,11},{10,... | collective-permute-start | bytes 589832 | tf_op jit(solution)/shard_map/ppermute | solution.py:342
  28.9 6.3 %collective-permute-start.8 = (f32[2,96,256]{2,1,0:T(8,128)S(1)}, f32[2,96,256]{2,1,0:T(8,128)S(1)}, u32[]{:S(2)}, u32[]{:S(2)}) collective-permute-start(f32[2,96,256]{2,1,0:T(8,128)S(1)} %get-tuple-element.30), channel_id=1, source_target_pairs={{0,4},{1,5},{2,6},{3,7},{4,0},{5,1},{6,2},{7,3},{8,12},{9,13},{10,... | collective-permute-start | bytes 589832 | tf_op jit(solution)/shard_map/ppermute | solution.py:342
  29.0 10.2 %collective-permute-start.15 = (f32[2,96,256]{2,1,0:T(8,128)S(1)}, f32[2,96,256]{2,1,0:T(8,128)S(1)}, u32[]{:S(2)}, u32[]{:S(2)}) collective-permute-start(f32[2,96,256]{2,1,0:T(8,128)S(1)} %get-tuple-element.38), channel_id=1, source_target_pairs={{4,8},{5,9},{6,10},{7,11},{8,4},{9,5},{10,6},{11,7},{20,24},{21,25... | collective-permute-start | bytes 589832 | tf_op jit(solution)/shard_map/ppermute | solution.py:342
  35.0 10.3 %copy-start.5 = (f32[2,2,256,256]{3,2,1,0:T(8,128)}, f32[2,2,256,256]{3,2,1,0:T(8,128)S(1)}, u32[]{:S(2)}) copy-start(f32[2,2,256,256]{3,2,1,0:T(8,128)S(1)} %collective-permute-done.9.behind_ref) | copy-start | bytes 3145732
  35.3 6.2 %collective-permute-start.12 = (f32[2,96,256]{2,1,0:T(8,128)S(1)}, f32[2,96,256]{2,1,0:T(8,128)S(1)}, u32[]{:S(2)}, u32[]{:S(2)}) collective-permute-start(f32[2,96,256]{2,1,0:T(8,128)S(1)} %get-tuple-element.34), channel_id=1, source_target_pairs={{0,4},{1,5},{2,6},{3,7},{4,0},{5,1},{6,2},{7,3},{8,12},{9,13},{10,... | collective-permute-start | bytes 589832 | tf_op jit(solution)/shard_map/ppermute | solution.py:342
  35.6 7.6 %collective-permute-start.13 = (f32[2,96,256]{2,1,0:T(8,128)S(1)}, f32[2,96,256]{2,1,0:T(8,128)S(1)}, u32[]{:S(2)}, u32[]{:S(2)}) collective-permute-start(f32[2,96,256]{2,1,0:T(8,128)S(1)} %get-tuple-element.35), channel_id=1, source_target_pairs={{4,8},{5,9},{6,10},{7,11},{8,4},{9,5},{10,6},{11,7},{20,24},{21,25... | collective-permute-start | bytes 589832 | tf_op jit(solution)/shard_map/ppermute | solution.py:342
  39.3 5.7 %collective-permute-start.16 = (f32[2,96,256]{2,1,0:T(8,128)S(1)}, f32[2,96,256]{2,1,0:T(8,128)S(1)}, u32[]{:S(2)}, u32[]{:S(2)}) collective-permute-start(f32[2,96,256]{2,1,0:T(8,128)S(1)} %shard_map.82), channel_id=1, source_target_pairs={{0,2},{1,3},{2,0},{3,1},{4,6},{5,7},{6,4},{7,5},{8,10},{9,11},{10,... | collective-permute-start | bytes 589832 | tf_op jit(solution)/shard_map/ppermute | solution.py:342
  40.9 7.6 %collective-permute-start.18 = (f32[2,160,256]{2,1,0:T(8,128)S(1)}, f32[2,160,256]{2,1,0:T(8,128)S(1)}, u32[]{:S(2)}, u32[]{:S(2)}) collective-permute-start(f32[2,160,256]{2,1,0:T(8,128)S(1)} %shard_map.80.refs_0_), channel_id=1, source_target_pairs={{0,16},{16,0},{1,17},{17,1},{2,18},{18,2},{3,19},{19,3},{4,20},{20... | collective-permute-start | bytes 983048 | tf_op jit(solution)/shard_map/ppermute | solution.py:396
  45.5 3.1 %collective-permute-start.17 = (f32[2,96,256]{2,1,0:T(8,128)S(1)}, f32[2,96,256]{2,1,0:T(8,128)S(1)}, u32[]{:S(2)}, u32[]{:S(2)}) collective-permute-start(f32[2,96,256]{2,1,0:T(8,128)S(1)} %shard_map.84), channel_id=1, source_target_pairs={{0,1},{1,0},{2,3},{3,2},{4,5},{5,4},{6,7},{7,6},{8,9},{9,8},{10,11... | collective-permute-start | bytes 589832 | tf_op jit(solution)/shard_map/ppermute | solution.py:342
  45.5 3.8 %copy-start.4 = (f32[1,2,2,256,256]{4,3,2,1,0:T(8,128)S(1)}, f32[1,2,2,256,256]{4,3,2,1,0:T(8,128)}, u32[]{:S(2)}) copy-start(f32[1,2,2,256,256]{4,3,2,1,0:T(8,128)} %param.7) | copy-start | bytes 3145732
  45.5 3.8 %copy-start.7 = (f32[1,256,256]{2,1,0:T(8,128)S(1)}, f32[1,256,256]{2,1,0:T(8,128)}, u32[]{:S(2)}) copy-start(f32[1,256,256]{2,1,0:T(8,128)} %param.9) | copy-start | bytes 786436
  45.6 11.0 %collective-permute-start.19 = (f32[2,96,256]{2,1,0:T(8,128)S(1)}, f32[2,96,256]{2,1,0:T(8,128)S(1)}, u32[]{:S(2)}, u32[]{:S(2)}) collective-permute-start(f32[2,96,256]{2,1,0:T(8,128)S(1)} %shard_map.83.refs_3_), channel_id=1, source_target_pairs={{0,16},{16,0},{1,17},{17,1},{2,18},{18,2},{3,19},{19,3},{4,20},{20... | collective-permute-start | bytes 589832 | tf_op jit(solution)/shard_map/ppermute | solution.py:395
  48.7 0.7 %copy-start.8 = (s32[1,4,4]{2,1,0:T(4,128)S(1)}, s32[1,4,4]{2,1,0:T(4,128)}, u32[]{:S(2)}) copy-start(s32[1,4,4]{2,1,0:T(4,128)} %param.10) | copy-start | bytes 196
  48.7 8.5 %collective-permute-start.20 = (f32[2,96,256]{2,1,0:T(8,128)S(1)}, f32[2,96,256]{2,1,0:T(8,128)S(1)}, u32[]{:S(2)}, u32[]{:S(2)}) collective-permute-start(f32[2,96,256]{2,1,0:T(8,128)S(1)} %shard_map.85.refs_1_), channel_id=1, source_target_pairs={{0,16},{16,0},{1,17},{17,1},{2,18},{18,2},{3,19},{19,3},{4,20},{20... | collective-permute-start | bytes 589832 | tf_op jit(solution)/shard_map/ppermute | solution.py:396
  49.4 1.2 %copy-start.6 = (f32[2,2,256,256]{3,2,1,0:T(8,128)S(1)}, f32[2,2,256,256]{3,2,1,0:T(8,128)}, u32[]{:S(2)}) copy-start(f32[2,2,256,256]{3,2,1,0:T(8,128)} %copy-done.5) | copy-start | bytes 3145732

commit v3 on v2

--- a/solution.py
+++ b/solution.py
@@ -216,21 +216,22 @@
     return split(pair[0]), split(pair[1])
 
 
-def bridge_kernel(tiles, mask_ref, hopping_ref, retarded_ref, behind_ref, coupled_ref, bridge_ref):
+def bridge_kernel(tiles, mask_ref, hopping_ref, retarded_ref, behind_ref, bridge_ref, *coupled_refs):
     size = hopping_ref.shape[0]
     tile = size // tiles
-    row_tile = lax.broadcasted_iota(jnp.int32, (size, size), 0) // tile
-    column_tile = lax.broadcasted_iota(jnp.int32, (size, size), 1) // tile
-    mask = jnp.zeros((size, size), jnp.float32)
+    column_tile = lax.broadcasted_iota(jnp.int32, (1, size), 1) // tile
+    strips = []
     for row in range(tiles):
+        strip = jnp.zeros((1, size), jnp.float32)
         for column in range(tiles):
-            here = (row_tile == row) & (column_tile == column)
-            mask = jnp.where(here, mask_ref[row, column].astype(jnp.float32), mask)
-    masked = split(hopping_ref[...] * mask)
+            strip = jnp.where(column_tile == column, mask_ref[row, column].astype(jnp.float32), strip)
+        strips.append(hopping_ref[row * tile : (row + 1) * tile, :] * strip)
+    masked = split(jnp.concatenate(strips, axis=0))
     for energy in range(retarded_ref.shape[0]):
         coupled = tuple(dot3(split(retarded_ref[energy, part]), masked) for part in range(2))
-        for part in range(2):
-            coupled_ref[energy, part] = coupled[part]
+        for coupled_ref in coupled_refs:
+            for part in range(2):
+                coupled_ref[energy, part] = coupled[part]
         bridge = times(
             split_pair(coupled), split_pair((behind_ref[energy, 0], behind_ref[energy, 1]))
         )
@@ -338,8 +339,13 @@
         compiler_params=pltpu.CompilerParams(vmem_limit_bytes=SMALL_VMEM),
     )(offsets, coupling, occupation)
 
-    def permute(value, pairs):
-        return lax.ppermute(value, "energy", pairs)
+    def permute(value, pairs, name):
+        with jax.named_scope(name):
+            return lax.ppermute(value, "energy", pairs)
+
+    def to_next_slab(value, name):
+        with jax.named_scope(name):
+            return lax.ppermute(value, "slab", ahead)
 
     cores = [(i, i ^ 1) for i in range(devices)]
     across = [(i, i ^ 2) for i in range(devices)]
@@ -354,55 +360,47 @@
     blocks = retarded[0]
     size = blocks.shape[-1]
     windows = row_windows(size)
-    behind = lax.ppermute(blocks, "slab", ahead)
+    behind = to_next_slab(blocks, "slab_retarded")
 
     reals, imags, reals_behind, imags_behind = [], [], [], []
     gates = None
     for number, window in enumerate(windows):
         real, imag = lesser_prev[0, :, 0, window], lesser_prev[0, :, 1, window]
         real_sent, imag_own = real, imag
-        imag_sibling = permute(imag, cores)
+        imag_sibling = permute(imag, cores, f"imag_cores_{number}")
         if gates is not None:
             real_sent = after(real, gates[0])
-            imag_own = after(imag, gates[1], gates[2])
-        real_beside = permute(real_sent, across)
+            imag_own = after(imag, gates[1])
+        real_beside = permute(real_sent, across, f"real_across_{number}")
         send1, send2 = combine(weights, bases[0], [imag_own, imag_sibling, real], 2)
-        got1, got2 = permute(send1, first_lines), permute(send2, second_lines)
+        got1 = permute(send1, first_lines, f"lines1a_{number}")
+        got2 = permute(send2, second_lines, f"lines1b_{number}")
         if gates is not None:
-            real_beside = after(real_beside, gates[3])
+            real_beside = after(real_beside, gates[2])
         send3, send4 = combine(weights, bases[1], [real_beside, imag_sibling, real], 2)
-        got3, got4 = permute(send3, first_lines), permute(send4, second_lines)
+        got4 = permute(send4, second_lines, f"lines2b_{number}")
+        got3 = permute(send3, first_lines, f"lines2a_{number}")
         if number == PIECES - 1:
             got1, behind = lax.optimization_barrier((got1, behind))
         if gates is not None:
             got1 = after(got1, imags_behind[-1])
         beside_sum = combine(weights, bases[2], [imag, imag_sibling, got1, got2], 1)
-        imag_beside = permute(beside_sum, across)
-        if gates is not None:
-            pass
+        imag_beside = permute(beside_sum, across, f"imag_across_{number}")
         self_imag = combine(
             weights, bases[3], [imag, imag_sibling, imag_beside, got1, got2, got3, got4], 1
         )
         real_late = real if gates is None else after(real, self_imag)
         sibling_sum = combine(weights, bases[4], [real_late, real_beside, got1, got2, got3, got4], 1)
-        real_sibling = permute(sibling_sum, cores)
+        real_sibling = permute(sibling_sum, cores, f"real_cores_{number}")
         if gates is not None:
             real_sibling = after(real_sibling, reals_behind[-1])
         self_real = combine(weights, bases[5], [real, real_beside, got3, got4, real_sibling], 1)
-        gates = (imag_beside, self_imag, sibling_sum, self_real)
+        gates = (imag_beside, self_imag, self_real)
         imags.append(self_imag)
         reals.append(self_real)
-        imags_behind.append(lax.ppermute(self_imag, "slab", ahead))
-        reals_behind.append(lax.ppermute(self_real, "slab", ahead))
-
-    behind, reals[-1] = lax.optimization_barrier((behind, reals[-1]))
-    coupled, bridge = call(
-        functools.partial(bridge_kernel, hop_mask.shape[-1]),
-        [hop_mask[0], hopping[0], blocks, behind],
-        [SMEM, VMEM, VMEM, VMEM],
-        [blocks, blocks],
-        12,
-    )
+        imags_behind.append(to_next_slab(self_imag, f"slab_imag_{number}"))
+        reals_behind.append(to_next_slab(self_real, f"slab_real_{number}"))
+
     (source,) = call(
         functools.partial(source_kernel, PIECES),
         [blocks] + reals + imags,
@@ -410,6 +408,13 @@
         [blocks],
         16,
     )
+    bridge, *coupled = call(
+        functools.partial(bridge_kernel, hop_mask.shape[-1]),
+        [hop_mask[0], hopping[0], blocks, after(behind, source)],
+        [SMEM, VMEM, VMEM, VMEM],
+        [blocks] * (2 if slabs > 2 else 1),
+        12,
+    )
     (total,) = call(
         functools.partial(piece_kernel, windows[0]),
         [bridge, reals_behind[0], imags_behind[0]],
@@ -419,7 +424,7 @@
     )
     (half,) = call(
         functools.partial(imag_half_kernel, windows[-1]),
-        [bridge, imags_behind[-1], after(total, source)],
+        [bridge, imags_behind[-1], total],
         [VMEM] * 3,
         [blocks],
         4,
@@ -437,7 +442,7 @@
         incoming = lax.ppermute(lesser, "slab", ahead)
         (lesser,) = call(
             advance_kernel,
-            [(position == turn).astype(jnp.int32).reshape(1), coupled, incoming, source, lesser],
+            [(position == turn).astype(jnp.int32).reshape(1), coupled[0], incoming, source, lesser],
             [SMEM] + [VMEM] * 4,
             [blocks],
             16,

time: 60.1 us -> 59.4 us (0.988)
  waiting for transfers between devices: 15.8 us -> 16.9 us
  local copies, waits for them, and re-layouts: 3.6 us -> 2.97 us
    ppermute x16, starting transfers between devices: 23 us -> 21.8 us  [permute(): return lax.ppermute(value, 'energy', pairs)]
    ppermute x5, waiting for transfers between devices: 1.78 us -> 2.75 us  [to_next_slab(): return lax.ppermute(value, 'slab', ahead)]
    unnamed x18, local copies, waits for them, and re-layouts: 1.34 us -> 0.7 us
    ppermute x5, starting transfers between devices: 4.45 us -> 5.08 us  [to_next_slab(): return lax.ppermute(value, 'slab', ahead)]
  transfers between devices with their start and end apart: 21 -> 21, of which waited for: 9 -> 10; matrix products, arithmetic and copies ran while one was open for 2% -> 2% of each run, Pallas kernels for 17% -> 16%
where the time goes in v3:
time: 59.4 us; the launch traced here: 59.2 us
  starting transfers between devices  26.9 us (45%)
  waiting for transfers between devices  16.9 us (28%)
  Pallas kernels  12.1 us (20%)
  local copies, waits for them, and re-layouts  2.97 us (5%)
    ppermute x16, starting transfers between devices, permute(): return lax.ppermute(value, 'energy', pairs)  21.8 us
    ppermute x16, waiting for transfers between devices, permute(): return lax.ppermute(value, 'energy', pairs)  14.1 us
    pallas_call x5, Pallas kernels, call(): pl.pallas_call(kernel, out_shape=[jax.ShapeDtypeStruct(array.shape, jnp.f...  8.64 us
    ppermute x5, starting transfers between devices, to_next_slab(): return lax.ppermute(value, 'slab', ahead)  5.08 us
    ppermute x5, waiting for transfers between devices, to_next_slab(): return lax.ppermute(value, 'slab', ahead)  2.75 us
    pallas_call x12, Pallas kernels, combine(): pl.pallas_call(functools.partial(combine_kernel, base, counts), out_shape...  2.4 us
    squeeze x2, local copies, waits for them, and re-layouts, body(): real, imag = (lesser_prev[0, :, 0, window], lesser_prev[0, :, 1, window])  2.26 us
  transfers between devices with their start and end apart: 21, of which 10 were waited for; matrix products, arithmetic and copies ran while one was open for 2% of the time, Pallas kernels for 16%

profile of v3, /device:TPU:10, one launch (start us, length us, event | category | flops | bytes accessed | tf_op | source)
XLA Modules:
  0.0 59.2 jit_solution(981308444762872082)
XLA Ops:
  0.0 1.2 %slice_bitcast_fusion = (f32[2,160,256]{2,1,0:T(8,128)S(1)}, f32[2,160,256]{2,1,0:T(8,128)S(1)}) fusion(f32[1,2,2,256,256]{4,3,2,1,0:T(8,128)} %param.8), kind=kLoop, calls=%fused_computation | loop fusion | bytes 1310720 | tf_op jit(solution)/shard_map/squeeze | solution.py:368
  1.3 1.6 %collective-permute-start.4 = (f32[2,160,256]{2,1,0:T(8,128)S(1)}, f32[2,160,256]{2,1,0:T(8,128)S(1)}, u32[]{:S(2)}, u32[]{:S(2)}) collective-permute-start(f32[2,160,256]{2,1,0:T(8,128)S(1)} %get-tuple-element.41.refs_2_.refs_0_), channel_id=1, source_target_pairs={{0,2},{1,3},{2,0},{3,1},{4,6},{5,7},{6,4},{7,5},{8,10},{9,11},{10,... | collective-permute-start | bytes 983048 | tf_op jit(solution)/shard_map/real_across_0/ppermute | solution.py:344
  2.9 0.5 collective-permute-start.9
  3.5 1.1 %shard_map.73.weights_ref = f32[136,8,128]{2,1,0:T(8,128)S(1)} custom-call(s32[3]{0:T(128)S(1)} %copy-done, f32[3]{0:T(128)S(1)} %copy-done.1, f32[3]{0:T(128)S(1)} %copy-done.2), custom_call_target="tpu_custom_call" | custom-call | tf_op jit(solution)/shard_map/pallas_call | solution.py:334
  5.3 4.6 %collective-permute-start.2 = (f32[2,160,256]{2,1,0:T(8,128)S(1)}, f32[2,160,256]{2,1,0:T(8,128)S(1)}, u32[]{:S(2)}, u32[]{:S(2)}) collective-permute-start(f32[2,160,256]{2,1,0:T(8,128)S(1)} %get-tuple-element.23), channel_id=1, source_target_pairs={{4,8},{5,9},{6,10},{7,11},{8,4},{9,5},{10,6},{11,7},{20,24},{21,25... | collective-permute-start | bytes 983048 | tf_op jit(solution)/shard_map/lines1b_0/ppermute | solution.py:344
  9.9 1.5 %collective-permute-done.4.refs_0_.refs_1_ = f32[2,160,256]{2,1,0:T(8,128)S(1)} collective-permute-done((f32[2,160,256]{2,1,0:T(8,128)S(1)}, f32[2,160,256]{2,1,0:T(8,128)S(1)}, u32[]{:S(2)}, u32[]{:S(2)}) %collective-permute-start.4) | collective-permute-done | bytes 327712 | tf_op jit(solution)/shard_map/real_across_0/ppermute | solution.py:344
  11.7 0.5 collective-permute-start.5
  12.2 4.6 %collective-permute-start.6 = (f32[2,160,256]{2,1,0:T(8,128)S(1)}, f32[2,160,256]{2,1,0:T(8,128)S(1)}, u32[]{:S(2)}, u32[]{:S(2)}) collective-permute-start(f32[2,160,256]{2,1,0:T(8,128)S(1)} %get-tuple-element.25), channel_id=1, source_target_pairs={{4,8},{5,9},{6,10},{7,11},{8,4},{9,5},{10,6},{11,7},{20,24},{21,25... | collective-permute-start | bytes 983048 | tf_op jit(solution)/shard_map/lines2b_0/ppermute | solution.py:344
  16.8 0.9 %collective-permute-done.2.refs_3_.refs_4_ = f32[2,160,256]{2,1,0:T(8,128)S(1)} collective-permute-done((f32[2,160,256]{2,1,0:T(8,128)S(1)}, f32[2,160,256]{2,1,0:T(8,128)S(1)}, u32[]{:S(2)}, u32[]{:S(2)}) %collective-permute-start.2) | collective-permute-done | bytes 327712 | tf_op jit(solution)/shard_map/lines1b_0/ppermute | solution.py:344
  17.9 0.7 %collective-permute-start.3 = (f32[2,160,256]{2,1,0:T(8,128)S(1)}, f32[2,160,256]{2,1,0:T(8,128)S(1)}, u32[]{:S(2)}, u32[]{:S(2)}) collective-permute-start(f32[2,160,256]{2,1,0:T(8,128)S(1)} %shard_map.75), channel_id=1, source_target_pairs={{0,2},{1,3},{2,0},{3,1},{4,6},{5,7},{6,4},{7,5},{8,10},{9,11},{10,... | collective-permute-start | bytes 983048 | tf_op jit(solution)/shard_map/imag_across_0/ppermute | solution.py:344
  18.6 2.8 %collective-permute-done.5.refs_5_.refs_4_.refs_2_ = f32[2,160,256]{2,1,0:T(8,128)S(1)} collective-permute-done((f32[2,160,256]{2,1,0:T(8,128)S(1)}, f32[2,160,256]{2,1,0:T(8,128)S(1)}, u32[]{:S(2)}, u32[]{:S(2)}) %collective-permute-start.5) | collective-permute-done | bytes 327712 | tf_op jit(solution)/shard_map/lines2a_0/ppermute | solution.py:344
  21.4 3.0 %collective-permute-done.6.refs_6_.refs_5_.refs_3_ = f32[2,160,256]{2,1,0:T(8,128)S(1)} collective-permute-done((f32[2,160,256]{2,1,0:T(8,128)S(1)}, f32[2,160,256]{2,1,0:T(8,128)S(1)}, u32[]{:S(2)}, u32[]{:S(2)}) %collective-permute-start.6) | collective-permute-done | bytes 327712 | tf_op jit(solution)/shard_map/lines2b_0/ppermute | solution.py:344
  24.8 1.1 %slice_bitcast_fusion.2 = (f32[2,96,256]{2,1,0:T(8,128)S(1)}, f32[2,96,256]{2,1,0:T(8,128)S(1)}) fusion(f32[1,2,2,256,256]{4,3,2,1,0:T(8,128)} %param.8), kind=kLoop, calls=%fused_computation.2 | loop fusion | bytes 786432 | tf_op jit(solution)/shard_map/squeeze | solution.py:368
  25.8 0.6 collective-permute-start.7
  26.7 1.6 %collective-permute-start.14 = (f32[2,160,256]{2,1,0:T(8,128)S(1)}, f32[2,160,256]{2,1,0:T(8,128)S(1)}, u32[]{:S(2)}, u32[]{:S(2)}) collective-permute-start(f32[2,160,256]{2,1,0:T(8,128)S(1)} %shard_map.77.refs_2_), channel_id=1, source_target_pairs={{0,16},{16,0},{1,17},{17,1},{2,18},{18,2},{3,19},{19,3},{4,20},{20... | collective-permute-start | bytes 983048 | tf_op jit(solution)/shard_map/slab_imag_0/ppermute | solution.py:348
  29.0 3.6 %collective-permute-start.15 = (f32[2,96,256]{2,1,0:T(8,128)S(1)}, f32[2,96,256]{2,1,0:T(8,128)S(1)}, u32[]{:S(2)}, u32[]{:S(2)}) collective-permute-start(f32[2,96,256]{2,1,0:T(8,128)S(1)} %get-tuple-element.35), channel_id=1, source_target_pairs={{4,8},{5,9},{6,10},{7,11},{8,4},{9,5},{10,6},{11,7},{20,24},{21,25... | collective-permute-start | bytes 589832 | tf_op jit(solution)/shard_map/lines1b_1/ppermute | solution.py:344
  32.9 1.9 %collective-permute-done.11.refs_0_.refs_1_ = f32[2,96,256]{2,1,0:T(8,128)S(1)} collective-permute-done((f32[2,96,256]{2,1,0:T(8,128)S(1)}, f32[2,96,256]{2,1,0:T(8,128)S(1)}, u32[]{:S(2)}, u32[]{:S(2)}) %collective-permute-start.11) | collective-permute-done | bytes 196640 | tf_op jit(solution)/shard_map/real_across_1/ppermute | solution.py:344
  35.1 3.6 %collective-permute-start.13 = (f32[2,96,256]{2,1,0:T(8,128)S(1)}, f32[2,96,256]{2,1,0:T(8,128)S(1)}, u32[]{:S(2)}, u32[]{:S(2)}) collective-permute-start(f32[2,96,256]{2,1,0:T(8,128)S(1)} %get-tuple-element.32), channel_id=1, source_target_pairs={{4,8},{5,9},{6,10},{7,11},{8,4},{9,5},{10,6},{11,7},{20,24},{21,25... | collective-permute-start | bytes 589832 | tf_op jit(solution)/shard_map/lines2b_1/ppermute | solution.py:344
  38.9 0.6 collective-permute-start.16
  39.5 1.2 %collective-permute-start.18 = (f32[2,160,256]{2,1,0:T(8,128)S(1)}, f32[2,160,256]{2,1,0:T(8,128)S(1)}, u32[]{:S(2)}, u32[]{:S(2)}) collective-permute-start(f32[2,160,256]{2,1,0:T(8,128)S(1)} %shard_map.80.refs_0_), channel_id=1, source_target_pairs={{0,16},{16,0},{1,17},{17,1},{2,18},{18,2},{3,19},{19,3},{4,20},{20... | collective-permute-start | bytes 983048 | tf_op jit(solution)/shard_map/slab_real_0/ppermute | solution.py:348
  40.7 1.9 %collective-permute-done.13.refs_6_.refs_5_.refs_3_ = f32[2,96,256]{2,1,0:T(8,128)S(1)} collective-permute-done((f32[2,96,256]{2,1,0:T(8,128)S(1)}, f32[2,96,256]{2,1,0:T(8,128)S(1)}, u32[]{:S(2)}, u32[]{:S(2)}) %collective-permute-start.13) | collective-permute-done | bytes 196640 | tf_op jit(solution)/shard_map/lines2b_1/ppermute | solution.py:344
  42.7 2.0 %collective-permute-done.16.refs_2_ = f32[2,96,256]{2,1,0:T(8,128)S(1)} collective-permute-done((f32[2,96,256]{2,1,0:T(8,128)S(1)}, f32[2,96,256]{2,1,0:T(8,128)S(1)}, u32[]{:S(2)}, u32[]{:S(2)}) %collective-permute-start.16) | collective-permute-done | bytes 196640 | tf_op jit(solution)/shard_map/imag_across_1/ppermute | solution.py:344
  45.1 0.6 %collective-permute-start.19 = (f32[2,96,256]{2,1,0:T(8,128)S(1)}, f32[2,96,256]{2,1,0:T(8,128)S(1)}, u32[]{:S(2)}, u32[]{:S(2)}) collective-permute-start(f32[2,96,256]{2,1,0:T(8,128)S(1)} %shard_map.83.refs_3_), channel_id=1, source_target_pairs={{0,16},{16,0},{1,17},{17,1},{2,18},{18,2},{3,19},{19,3},{4,20},{20... | collective-permute-start | bytes 589832 | tf_op jit(solution)/shard_map/slab_imag_1/ppermute | solution.py:348
  45.7 1.7 %collective-permute-done.18.real_ref = f32[2,160,256]{2,1,0:T(8,128)S(1)} collective-permute-done((f32[2,160,256]{2,1,0:T(8,128)S(1)}, f32[2,160,256]{2,1,0:T(8,128)S(1)}, u32[]{:S(2)}, u32[]{:S(2)}) %collective-permute-start.18) | collective-permute-done | bytes 327712 | tf_op jit(solution)/shard_map/slab_real_0/ppermute | solution.py:348
  47.5 1.2 %collective-permute-start.20 = (f32[2,96,256]{2,1,0:T(8,128)S(1)}, f32[2,96,256]{2,1,0:T(8,128)S(1)}, u32[]{:S(2)}, u32[]{:S(2)}) collective-permute-start(f32[2,96,256]{2,1,0:T(8,128)S(1)} %shard_map.85.refs_1_), channel_id=1, source_target_pairs={{0,16},{16,0},{1,17},{17,1},{2,18},{18,2},{3,19},{19,3},{4,20},{20... | collective-permute-start | bytes 589832 | tf_op jit(solution)/shard_map/slab_real_1/ppermute | solution.py:348
  48.8 2.2 %shard_map.86.source_ref = f32[2,2,256,256]{3,2,1,0:T(8,128)S(1)} custom-call(f32[2,2,256,256]{3,2,1,0:T(8,128)S(1)} %bitcast.22, f32[2,160,256]{2,1,0:T(8,128)S(1)} %shard_map.80.refs_0_, f32[2,96,256]{2,1,0:T(8,128)S(1)} %shard_map.85.refs_1_, f32[2,160,256]{2,1,0:T(8,128)S(1)} %shard_map.77.refs_2_, f32[2,96,256]{2,1,0:T(8,128)S(1)} %shard_map.83.refs_3_), custom_call_target="tpu_custom_call" | custom-call | flops 1610612736 | bytes 3145728 | tf_op jit(solution)/shard_map/pallas_call | solution.py:310
  51.0 0.7 %copy-done.8 = s32[1,4,4]{2,1,0:T(4,128)S(1)} copy-done((s32[1,4,4]{2,1,0:T(4,128)S(1)}, s32[1,4,4]{2,1,0:T(4,128)}, u32[]{:S(2)}) %copy-start.8) | copy-done | bytes 88
  51.6 2.3 %shard_map.87.bridge_ref = f32[2,2,256,256]{3,2,1,0:T(8,128)S(1)} custom-call(s32[4,4]{1,0:T(4,128)S(1)} %bitcast.25, f32[256,256]{1,0:T(8,128)S(1)} %bitcast.24, f32[2,2,256,256]{3,2,1,0:T(8,128)S(1)} %bitcast.23, f32[2,2,256,256]{3,2,1,0:T(8,128)S(1)} %copy-done.6), custom_call_target="tpu_custom_call" | custom-call | flops 1207959552 | bytes 3407936 | tf_op jit(solution)/shard_map/pallas_call | solution.py:310
  53.9 1.0 %shard_map.88.total_ref = f32[2,2,256,256]{3,2,1,0:T(8,128)S(1)} custom-call(f32[2,2,256,256]{3,2,1,0:T(8,128)S(1)} %shard_map.87.bridge_ref, f32[2,160,256]{2,1,0:T(8,128)S(1)} %collective-permute-done.18.real_ref, f32[2,160,256]{2,1,0:T(8,128)S(1)} %collective-permute-done.14.imag_ref), custom_call_target="tpu_custom_call" | custom-call | flops 805306368 | bytes 2752512 | tf_op jit(solution)/shard_map/pallas_call | solution.py:310
  54.9 0.6 %shard_map.89.half_ref = f32[2,2,256,256]{3,2,1,0:T(8,128)S(1)} custom-call(f32[2,2,256,256]{3,2,1,0:T(8,128)S(1)} %shard_map.87.bridge_ref, f32[2,96,256]{2,1,0:T(8,128)S(1)} %collective-permute-done.19.imag_ref, f32[2,2,256,256]{3,2,1,0:T(8,128)S(1)} %shard_map.88.total_ref), custom_call_target="tpu_custom_call" | custom-call | flops 402653184 | bytes 3342336 | tf_op jit(solution)/shard_map/pallas_call | solution.py:310
  55.5 1.1 %collective-permute-done.20.real_ref = f32[2,96,256]{2,1,0:T(8,128)S(1)} collective-permute-done((f32[2,96,256]{2,1,0:T(8,128)S(1)}, f32[2,96,256]{2,1,0:T(8,128)S(1)}, u32[]{:S(2)}, u32[]{:S(2)}) %collective-permute-start.20) | collective-permute-done | bytes 196640 | tf_op jit(solution)/shard_map/slab_real_1/ppermute | solution.py:348
  56.6 2.6 %shard_map.90 = f32[2,2,256,256]{3,2,1,0:T(8,128)} custom-call(s32[1]{0:T(128)} %bitcast.flag_ref, f32[2,2,256,256]{3,2,1,0:T(8,128)S(1)} %shard_map.87.bridge_ref, f32[2,2,256,256]{3,2,1,0:T(8,128)S(1)} %shard_map.89.half_ref, f32[2,96,256]{2,1,0:T(8,128)S(1)} %collective-permute-done.20.real_ref, f32[2,2,256,256]{3,2,1,0:T(8,128)S(1)} %shard_map.86.source_ref), custom_call_target="tpu_custom_call" | custom-call | flops 1207959552 | bytes 4390916 | tf_op jit(solution)/shard_map/pallas_call | solution.py:310
  (48 shorter events, 4.0 us)
Async XLA Ops:
  0.0 2.9 %copy-start.3 = (f32[1,2,2,256,256]{4,3,2,1,0:T(8,128)S(1)}, f32[1,2,2,256,256]{4,3,2,1,0:T(8,128)}, u32[]{:S(2)}) copy-start(f32[1,2,2,256,256]{4,3,2,1,0:T(8,128)} %param.7) | copy-start | bytes 3145732
  1.2 3.3 %collective-permute-start = (f32[2,160,256]{2,1,0:T(8,128)S(1)}, f32[2,160,256]{2,1,0:T(8,128)S(1)}, u32[]{:S(2)}, u32[]{:S(2)}) collective-permute-start(f32[2,160,256]{2,1,0:T(8,128)S(1)} %get-tuple-element.42.refs_0_), channel_id=1, source_target_pairs={{0,1},{1,0},{2,3},{3,2},{4,5},{5,4},{6,7},{7,6},{8,9},{9,8},{10,11... | collective-permute-start | bytes 983048 | tf_op jit(solution)/shard_map/imag_cores_0/ppermute | solution.py:344
  1.3 2.2 %copy-start = (s32[3]{0:T(128)S(1)}, s32[3]{0:T(128)}, u32[]{:S(2)}) copy-start(s32[3]{0:T(128)} %offsets_ref.1) | copy-start | bytes 40
  1.3 2.2 %copy-start.1 = (f32[3]{0:T(128)S(1)}, f32[3]{0:T(128)}, u32[]{:S(2)}) copy-start(f32[3]{0:T(128)} %coupling_ref.1) | copy-start | bytes 40
  1.3 2.1 %copy-start.2 = (f32[3]{0:T(128)S(1)}, f32[3]{0:T(128)}, u32[]{:S(2)}) copy-start(f32[3]{0:T(128)} %occupation_ref.1) | copy-start | bytes 40
  1.3 10.1 %collective-permute-start.4 = (f32[2,160,256]{2,1,0:T(8,128)S(1)}, f32[2,160,256]{2,1,0:T(8,128)S(1)}, u32[]{:S(2)}, u32[]{:S(2)}) collective-permute-start(f32[2,160,256]{2,1,0:T(8,128)S(1)} %get-tuple-element.41.refs_2_.refs_0_), channel_id=1, source_target_pairs={{0,2},{1,3},{2,0},{3,1},{4,6},{5,7},{6,4},{7,5},{8,10},{9,11},{10,... | collective-permute-start | bytes 983048 | tf_op jit(solution)/shard_map/real_across_0/ppermute | solution.py:344
  2.9 32.2 %collective-permute-start.9 = (f32[2,2,256,256]{3,2,1,0:T(8,128)S(1)}, f32[2,2,256,256]{3,2,1,0:T(8,128)S(1)}, u32[]{:S(2)}, u32[]{:S(2)}) collective-permute-start(f32[2,2,256,256]{3,2,1,0:T(8,128)S(1)} %bitcast.21), channel_id=1, source_target_pairs={{0,16},{16,0},{1,17},{17,1},{2,18},{18,2},{3,19},{19,3},{4,20},{20... | collective-permute-start | bytes 3145736 | tf_op jit(solution)/shard_map/slab_retarded/ppermute | solution.py:348
  4.8 12.0 %collective-permute-start.1 = (f32[2,160,256]{2,1,0:T(8,128)S(1)}, f32[2,160,256]{2,1,0:T(8,128)S(1)}, u32[]{:S(2)}, u32[]{:S(2)}) collective-permute-start(f32[2,160,256]{2,1,0:T(8,128)S(1)} %get-tuple-element.22), channel_id=1, source_target_pairs={{0,4},{1,5},{2,6},{3,7},{4,0},{5,1},{6,2},{7,3},{8,12},{9,13},{10,... | collective-permute-start | bytes 983048 | tf_op jit(solution)/shard_map/lines1a_0/ppermute | solution.py:344
  5.3 12.4 %collective-permute-start.2 = (f32[2,160,256]{2,1,0:T(8,128)S(1)}, f32[2,160,256]{2,1,0:T(8,128)S(1)}, u32[]{:S(2)}, u32[]{:S(2)}) collective-permute-start(f32[2,160,256]{2,1,0:T(8,128)S(1)} %get-tuple-element.23), channel_id=1, source_target_pairs={{4,8},{5,9},{6,10},{7,11},{8,4},{9,5},{10,6},{11,7},{20,24},{21,25... | collective-permute-start | bytes 983048 | tf_op jit(solution)/shard_map/lines1b_0/ppermute | solution.py:344
  11.7 9.7 %collective-permute-start.5 = (f32[2,160,256]{2,1,0:T(8,128)S(1)}, f32[2,160,256]{2,1,0:T(8,128)S(1)}, u32[]{:S(2)}, u32[]{:S(2)}) collective-permute-start(f32[2,160,256]{2,1,0:T(8,128)S(1)} %get-tuple-element.24), channel_id=1, source_target_pairs={{0,4},{1,5},{2,6},{3,7},{4,0},{5,1},{6,2},{7,3},{8,12},{9,13},{10,... | collective-permute-start | bytes 983048 | tf_op jit(solution)/shard_map/lines2a_0/ppermute | solution.py:344
  12.2 12.2 %collective-permute-start.6 = (f32[2,160,256]{2,1,0:T(8,128)S(1)}, f32[2,160,256]{2,1,0:T(8,128)S(1)}, u32[]{:S(2)}, u32[]{:S(2)}) collective-permute-start(f32[2,160,256]{2,1,0:T(8,128)S(1)} %get-tuple-element.25), channel_id=1, source_target_pairs={{4,8},{5,9},{6,10},{7,11},{8,4},{9,5},{10,6},{11,7},{20,24},{21,25... | collective-permute-start | bytes 983048 | tf_op jit(solution)/shard_map/lines2b_0/ppermute | solution.py:344
  17.9 8.5 %collective-permute-start.3 = (f32[2,160,256]{2,1,0:T(8,128)S(1)}, f32[2,160,256]{2,1,0:T(8,128)S(1)}, u32[]{:S(2)}, u32[]{:S(2)}) collective-permute-start(f32[2,160,256]{2,1,0:T(8,128)S(1)} %shard_map.75), channel_id=1, source_target_pairs={{0,2},{1,3},{2,0},{3,1},{4,6},{5,7},{6,4},{7,5},{8,10},{9,11},{10,... | collective-permute-start | bytes 983048 | tf_op jit(solution)/shard_map/imag_across_0/ppermute | solution.py:344
  24.7 4.3 %collective-permute-start.10 = (f32[2,160,256]{2,1,0:T(8,128)S(1)}, f32[2,160,256]{2,1,0:T(8,128)S(1)}, u32[]{:S(2)}, u32[]{:S(2)}) collective-permute-start(f32[2,160,256]{2,1,0:T(8,128)S(1)} %shard_map.79), channel_id=1, source_target_pairs={{0,1},{1,0},{2,3},{3,2},{4,5},{5,4},{6,7},{7,6},{8,9},{9,8},{10,11... | collective-permute-start | bytes 983048 | tf_op jit(solution)/shard_map/real_cores_0/ppermute | solution.py:344
  25.8 3.0 %collective-permute-start.7 = (f32[2,96,256]{2,1,0:T(8,128)S(1)}, f32[2,96,256]{2,1,0:T(8,128)S(1)}, u32[]{:S(2)}, u32[]{:S(2)}) collective-permute-start(f32[2,96,256]{2,1,0:T(8,128)S(1)} %get-tuple-element.26.refs_0_), channel_id=1, source_target_pairs={{0,1},{1,0},{2,3},{3,2},{4,5},{5,4},{6,7},{7,6},{8,9},{9,8},{10,11... | collective-permute-start | bytes 589832 | tf_op jit(solution)/shard_map/imag_cores_1/ppermute | solution.py:344
  26.7 12.0 %collective-permute-start.14 = (f32[2,160,256]{2,1,0:T(8,128)S(1)}, f32[2,160,256]{2,1,0:T(8,128)S(1)}, u32[]{:S(2)}, u32[]{:S(2)}) collective-permute-start(f32[2,160,256]{2,1,0:T(8,128)S(1)} %shard_map.77.refs_2_), channel_id=1, source_target_pairs={{0,16},{16,0},{1,17},{17,1},{2,18},{18,2},{3,19},{19,3},{4,20},{20... | collective-permute-start | bytes 983048 | tf_op jit(solution)/shard_map/slab_imag_0/ppermute | solution.py:348
  28.3 6.5 %collective-permute-start.11 = (f32[2,96,256]{2,1,0:T(8,128)S(1)}, f32[2,96,256]{2,1,0:T(8,128)S(1)}, u32[]{:S(2)}, u32[]{:S(2)}) collective-permute-start(f32[2,96,256]{2,1,0:T(8,128)S(1)} %get-tuple-element.36.refs_2_.refs_0_), channel_id=1, source_target_pairs={{0,2},{1,3},{2,0},{3,1},{4,6},{5,7},{6,4},{7,5},{8,10},{9,11},{10,... | collective-permute-start | bytes 589832 | tf_op jit(solution)/shard_map/real_across_1/ppermute | solution.py:344
  28.9 9.8 %collective-permute-start.8 = (f32[2,96,256]{2,1,0:T(8,128)S(1)}, f32[2,96,256]{2,1,0:T(8,128)S(1)}, u32[]{:S(2)}, u32[]{:S(2)}) collective-permute-start(f32[2,96,256]{2,1,0:T(8,128)S(1)} %get-tuple-element.27), channel_id=1, source_target_pairs={{0,4},{1,5},{2,6},{3,7},{4,0},{5,1},{6,2},{7,3},{8,12},{9,13},{10,... | collective-permute-start | bytes 589832 | tf_op jit(solution)/shard_map/lines1a_1/ppermute | solution.py:344
  29.0 9.7 %collective-permute-start.15 = (f32[2,96,256]{2,1,0:T(8,128)S(1)}, f32[2,96,256]{2,1,0:T(8,128)S(1)}, u32[]{:S(2)}, u32[]{:S(2)}) collective-permute-start(f32[2,96,256]{2,1,0:T(8,128)S(1)} %get-tuple-element.35), channel_id=1, source_target_pairs={{4,8},{5,9},{6,10},{7,11},{8,4},{9,5},{10,6},{11,7},{20,24},{21,25... | collective-permute-start | bytes 589832 | tf_op jit(solution)/shard_map/lines1b_1/ppermute | solution.py:344
  35.0 5.7 %collective-permute-start.12 = (f32[2,96,256]{2,1,0:T(8,128)S(1)}, f32[2,96,256]{2,1,0:T(8,128)S(1)}, u32[]{:S(2)}, u32[]{:S(2)}) collective-permute-start(f32[2,96,256]{2,1,0:T(8,128)S(1)} %get-tuple-element.31), channel_id=1, source_target_pairs={{0,4},{1,5},{2,6},{3,7},{4,0},{5,1},{6,2},{7,3},{8,12},{9,13},{10,... | collective-permute-start | bytes 589832 | tf_op jit(solution)/shard_map/lines2a_1/ppermute | solution.py:344
  35.1 9.7 %copy-start.5 = (f32[2,2,256,256]{3,2,1,0:T(8,128)}, f32[2,2,256,256]{3,2,1,0:T(8,128)S(1)}, u32[]{:S(2)}) copy-start(f32[2,2,256,256]{3,2,1,0:T(8,128)S(1)} %collective-permute-done.9.behind_ref) | copy-start | bytes 3145732
  35.1 7.6 %collective-permute-start.13 = (f32[2,96,256]{2,1,0:T(8,128)S(1)}, f32[2,96,256]{2,1,0:T(8,128)S(1)}, u32[]{:S(2)}, u32[]{:S(2)}) collective-permute-start(f32[2,96,256]{2,1,0:T(8,128)S(1)} %get-tuple-element.32), channel_id=1, source_target_pairs={{4,8},{5,9},{6,10},{7,11},{8,4},{9,5},{10,6},{11,7},{20,24},{21,25... | collective-permute-start | bytes 589832 | tf_op jit(solution)/shard_map/lines2b_1/ppermute | solution.py:344
  38.9 5.7 %collective-permute-start.16 = (f32[2,96,256]{2,1,0:T(8,128)S(1)}, f32[2,96,256]{2,1,0:T(8,128)S(1)}, u32[]{:S(2)}, u32[]{:S(2)}) collective-permute-start(f32[2,96,256]{2,1,0:T(8,128)S(1)} %shard_map.82), channel_id=1, source_target_pairs={{0,2},{1,3},{2,0},{3,1},{4,6},{5,7},{6,4},{7,5},{8,10},{9,11},{10,... | collective-permute-start | bytes 589832 | tf_op jit(solution)/shard_map/imag_across_1/ppermute | solution.py:344
  39.5 7.9 %collective-permute-start.18 = (f32[2,160,256]{2,1,0:T(8,128)S(1)}, f32[2,160,256]{2,1,0:T(8,128)S(1)}, u32[]{:S(2)}, u32[]{:S(2)}) collective-permute-start(f32[2,160,256]{2,1,0:T(8,128)S(1)} %shard_map.80.refs_0_), channel_id=1, source_target_pairs={{0,16},{16,0},{1,17},{17,1},{2,18},{18,2},{3,19},{19,3},{4,20},{20... | collective-permute-start | bytes 983048 | tf_op jit(solution)/shard_map/slab_real_0/ppermute | solution.py:348
  45.0 2.4 %collective-permute-start.17 = (f32[2,96,256]{2,1,0:T(8,128)S(1)}, f32[2,96,256]{2,1,0:T(8,128)S(1)}, u32[]{:S(2)}, u32[]{:S(2)}) collective-permute-start(f32[2,96,256]{2,1,0:T(8,128)S(1)} %shard_map.84), channel_id=1, source_target_pairs={{0,1},{1,0},{2,3},{3,2},{4,5},{5,4},{6,7},{7,6},{8,9},{9,8},{10,11... | collective-permute-start | bytes 589832 | tf_op jit(solution)/shard_map/real_cores_1/ppermute | solution.py:344
  45.1 3.7 %copy-start.4 = (f32[1,2,2,256,256]{4,3,2,1,0:T(8,128)S(1)}, f32[1,2,2,256,256]{4,3,2,1,0:T(8,128)}, u32[]{:S(2)}) copy-start(f32[1,2,2,256,256]{4,3,2,1,0:T(8,128)} %param.7) | copy-start | bytes 3145732
  45.1 9.8 %collective-permute-start.19 = (f32[2,96,256]{2,1,0:T(8,128)S(1)}, f32[2,96,256]{2,1,0:T(8,128)S(1)}, u32[]{:S(2)}, u32[]{:S(2)}) collective-permute-start(f32[2,96,256]{2,1,0:T(8,128)S(1)} %shard_map.83.refs_3_), channel_id=1, source_target_pairs={{0,16},{16,0},{1,17},{17,1},{2,18},{18,2},{3,19},{19,3},{4,20},{20... | collective-permute-start | bytes 589832 | tf_op jit(solution)/shard_map/slab_imag_1/ppermute | solution.py:348
  47.5 3.5 %copy-start.6 = (f32[2,2,256,256]{3,2,1,0:T(8,128)S(1)}, f32[2,2,256,256]{3,2,1,0:T(8,128)}, u32[]{:S(2)}) copy-start(f32[2,2,256,256]{3,2,1,0:T(8,128)} %copy-done.5) | copy-start | bytes 3145732
  47.5 3.5 %copy-start.7 = (f32[1,256,256]{2,1,0:T(8,128)S(1)}, f32[1,256,256]{2,1,0:T(8,128)}, u32[]{:S(2)}) copy-start(f32[1,256,256]{2,1,0:T(8,128)} %param.9) | copy-start | bytes 786436
  47.5 9.1 %collective-permute-start.20 = (f32[2,96,256]{2,1,0:T(8,128)S(1)}, f32[2,96,256]{2,1,0:T(8,128)S(1)}, u32[]{:S(2)}, u32[]{:S(2)}) collective-permute-start(f32[2,96,256]{2,1,0:T(8,128)S(1)} %shard_map.85.refs_1_), channel_id=1, source_target_pairs={{0,16},{16,0},{1,17},{17,1},{2,18},{18,2},{3,19},{19,3},{4,20},{20... | collective-permute-start | bytes 589832 | tf_op jit(solution)/shard_map/slab_real_1/ppermute | solution.py:348
  51.0 0.7 %copy-start.8 = (s32[1,4,4]{2,1,0:T(4,128)S(1)}, s32[1,4,4]{2,1,0:T(4,128)}, u32[]{:S(2)}) copy-start(s32[1,4,4]{2,1,0:T(4,128)} %param.10) | copy-start | bytes 196

commit v4 on v3

--- a/solution.py
+++ b/solution.py
@@ -395,7 +395,7 @@
         if gates is not None:
             real_sibling = after(real_sibling, reals_behind[-1])
         self_real = combine(weights, bases[5], [real, real_beside, got3, got4, real_sibling], 1)
-        gates = (imag_beside, self_imag, self_real)
+        gates = (real_beside, self_imag, self_real)
         imags.append(self_imag)
         reals.append(self_real)
         imags_behind.append(to_next_slab(self_imag, f"slab_imag_{number}"))

time: 59.4 us -> 59.4 us (level)
  no operation moved by 1% of the time
where the time goes in v4:
time: 59.4 us; the launch traced here: 59.2 us
  starting transfers between devices  26.9 us (45%)
  waiting for transfers between devices  16.9 us (28%)
  Pallas kernels  12.1 us (20%)
  local copies, waits for them, and re-layouts  2.97 us (5%)
    ppermute x16, starting transfers between devices, permute(): return lax.ppermute(value, 'energy', pairs)  21.8 us
    ppermute x16, waiting for transfers between devices, permute(): return lax.ppermute(value, 'energy', pairs)  14.1 us
    pallas_call x5, Pallas kernels, call(): pl.pallas_call(kernel, out_shape=[jax.ShapeDtypeStruct(array.shape, jnp.f...  8.64 us
    ppermute x5, starting transfers between devices, to_next_slab(): return lax.ppermute(value, 'slab', ahead)  5.08 us
    ppermute x5, waiting for transfers between devices, to_next_slab(): return lax.ppermute(value, 'slab', ahead)  2.75 us
    pallas_call x12, Pallas kernels, combine(): pl.pallas_call(functools.partial(combine_kernel, base, counts), out_shape...  2.4 us
    squeeze x2, local copies, waits for them, and re-layouts, body(): real, imag = (lesser_prev[0, :, 0, window], lesser_prev[0, :, 1, window])  2.26 us
  transfers between devices with their start and end apart: 21, of which 10 were waited for; matrix products, arithmetic and copies ran while one was open for 2% of the time, Pallas kernels for 16%

profile of v4, /device:TPU:10, one launch (start us, length us, event | category | flops | bytes accessed | tf_op | source)
XLA Modules:
  0.0 59.2 jit_solution(981308444762872082)
XLA Ops:
  0.0 1.2 %slice_bitcast_fusion = (f32[2,160,256]{2,1,0:T(8,128)S(1)}, f32[2,160,256]{2,1,0:T(8,128)S(1)}) fusion(f32[1,2,2,256,256]{4,3,2,1,0:T(8,128)} %param.8), kind=kLoop, calls=%fused_computation | loop fusion | bytes 1310720 | tf_op jit(solution)/shard_map/squeeze | solution.py:368
  1.3 1.6 %collective-permute-start.4 = (f32[2,160,256]{2,1,0:T(8,128)S(1)}, f32[2,160,256]{2,1,0:T(8,128)S(1)}, u32[]{:S(2)}, u32[]{:S(2)}) collective-permute-start(f32[2,160,256]{2,1,0:T(8,128)S(1)} %get-tuple-element.41.refs_2_.refs_0_), channel_id=1, source_target_pairs={{0,2},{1,3},{2,0},{3,1},{4,6},{5,7},{6,4},{7,5},{8,10},{9,11},{10,... | collective-permute-start | bytes 983048 | tf_op jit(solution)/shard_map/real_across_0/ppermute | solution.py:344
  2.9 0.5 collective-permute-start.9
  3.5 1.1 %shard_map.73.weights_ref = f32[136,8,128]{2,1,0:T(8,128)S(1)} custom-call(s32[3]{0:T(128)S(1)} %copy-done, f32[3]{0:T(128)S(1)} %copy-done.1, f32[3]{0:T(128)S(1)} %copy-done.2), custom_call_target="tpu_custom_call" | custom-call | tf_op jit(solution)/shard_map/pallas_call | solution.py:334
  5.3 4.6 %collective-permute-start.2 = (f32[2,160,256]{2,1,0:T(8,128)S(1)}, f32[2,160,256]{2,1,0:T(8,128)S(1)}, u32[]{:S(2)}, u32[]{:S(2)}) collective-permute-start(f32[2,160,256]{2,1,0:T(8,128)S(1)} %get-tuple-element.23), channel_id=1, source_target_pairs={{4,8},{5,9},{6,10},{7,11},{8,4},{9,5},{10,6},{11,7},{20,24},{21,25... | collective-permute-start | bytes 983048 | tf_op jit(solution)/shard_map/lines1b_0/ppermute | solution.py:344
  9.9 1.5 %collective-permute-done.4.refs_0_.refs_1_ = f32[2,160,256]{2,1,0:T(8,128)S(1)} collective-permute-done((f32[2,160,256]{2,1,0:T(8,128)S(1)}, f32[2,160,256]{2,1,0:T(8,128)S(1)}, u32[]{:S(2)}, u32[]{:S(2)}) %collective-permute-start.4) | collective-permute-done | bytes 327712 | tf_op jit(solution)/shard_map/real_across_0/ppermute | solution.py:344
  11.7 0.5 collective-permute-start.5
  12.2 4.6 %collective-permute-start.6 = (f32[2,160,256]{2,1,0:T(8,128)S(1)}, f32[2,160,256]{2,1,0:T(8,128)S(1)}, u32[]{:S(2)}, u32[]{:S(2)}) collective-permute-start(f32[2,160,256]{2,1,0:T(8,128)S(1)} %get-tuple-element.25), channel_id=1, source_target_pairs={{4,8},{5,9},{6,10},{7,11},{8,4},{9,5},{10,6},{11,7},{20,24},{21,25... | collective-permute-start | bytes 983048 | tf_op jit(solution)/shard_map/lines2b_0/ppermute | solution.py:344
  16.8 0.9 %collective-permute-done.2.refs_3_.refs_4_ = f32[2,160,256]{2,1,0:T(8,128)S(1)} collective-permute-done((f32[2,160,256]{2,1,0:T(8,128)S(1)}, f32[2,160,256]{2,1,0:T(8,128)S(1)}, u32[]{:S(2)}, u32[]{:S(2)}) %collective-permute-start.2) | collective-permute-done | bytes 327712 | tf_op jit(solution)/shard_map/lines1b_0/ppermute | solution.py:344
  17.9 0.7 %collective-permute-start.3 = (f32[2,160,256]{2,1,0:T(8,128)S(1)}, f32[2,160,256]{2,1,0:T(8,128)S(1)}, u32[]{:S(2)}, u32[]{:S(2)}) collective-permute-start(f32[2,160,256]{2,1,0:T(8,128)S(1)} %shard_map.75), channel_id=1, source_target_pairs={{0,2},{1,3},{2,0},{3,1},{4,6},{5,7},{6,4},{7,5},{8,10},{9,11},{10,... | collective-permute-start | bytes 983048 | tf_op jit(solution)/shard_map/imag_across_0/ppermute | solution.py:344
  18.6 2.8 %collective-permute-done.5.refs_5_.refs_4_.refs_2_ = f32[2,160,256]{2,1,0:T(8,128)S(1)} collective-permute-done((f32[2,160,256]{2,1,0:T(8,128)S(1)}, f32[2,160,256]{2,1,0:T(8,128)S(1)}, u32[]{:S(2)}, u32[]{:S(2)}) %collective-permute-start.5) | collective-permute-done | bytes 327712 | tf_op jit(solution)/shard_map/lines2a_0/ppermute | solution.py:344
  21.4 3.0 %collective-permute-done.6.refs_6_.refs_5_.refs_3_ = f32[2,160,256]{2,1,0:T(8,128)S(1)} collective-permute-done((f32[2,160,256]{2,1,0:T(8,128)S(1)}, f32[2,160,256]{2,1,0:T(8,128)S(1)}, u32[]{:S(2)}, u32[]{:S(2)}) %collective-permute-start.6) | collective-permute-done | bytes 327712 | tf_op jit(solution)/shard_map/lines2b_0/ppermute | solution.py:344
  24.8 1.1 %slice_bitcast_fusion.2 = (f32[2,96,256]{2,1,0:T(8,128)S(1)}, f32[2,96,256]{2,1,0:T(8,128)S(1)}) fusion(f32[1,2,2,256,256]{4,3,2,1,0:T(8,128)} %param.8), kind=kLoop, calls=%fused_computation.2 | loop fusion | bytes 786432 | tf_op jit(solution)/shard_map/squeeze | solution.py:368
  25.8 0.6 collective-permute-start.7
  26.7 1.6 %collective-permute-start.14 = (f32[2,160,256]{2,1,0:T(8,128)S(1)}, f32[2,160,256]{2,1,0:T(8,128)S(1)}, u32[]{:S(2)}, u32[]{:S(2)}) collective-permute-start(f32[2,160,256]{2,1,0:T(8,128)S(1)} %shard_map.77.refs_2_), channel_id=1, source_target_pairs={{0,16},{16,0},{1,17},{17,1},{2,18},{18,2},{3,19},{19,3},{4,20},{20... | collective-permute-start | bytes 983048 | tf_op jit(solution)/shard_map/slab_imag_0/ppermute | solution.py:348
  29.0 3.6 %collective-permute-start.15 = (f32[2,96,256]{2,1,0:T(8,128)S(1)}, f32[2,96,256]{2,1,0:T(8,128)S(1)}, u32[]{:S(2)}, u32[]{:S(2)}) collective-permute-start(f32[2,96,256]{2,1,0:T(8,128)S(1)} %get-tuple-element.35), channel_id=1, source_target_pairs={{4,8},{5,9},{6,10},{7,11},{8,4},{9,5},{10,6},{11,7},{20,24},{21,25... | collective-permute-start | bytes 589832 | tf_op jit(solution)/shard_map/lines1b_1/ppermute | solution.py:344
  32.9 1.9 %collective-permute-done.11.refs_0_.refs_1_ = f32[2,96,256]{2,1,0:T(8,128)S(1)} collective-permute-done((f32[2,96,256]{2,1,0:T(8,128)S(1)}, f32[2,96,256]{2,1,0:T(8,128)S(1)}, u32[]{:S(2)}, u32[]{:S(2)}) %collective-permute-start.11) | collective-permute-done | bytes 196640 | tf_op jit(solution)/shard_map/real_across_1/ppermute | solution.py:344
  35.1 3.6 %collective-permute-start.13 = (f32[2,96,256]{2,1,0:T(8,128)S(1)}, f32[2,96,256]{2,1,0:T(8,128)S(1)}, u32[]{:S(2)}, u32[]{:S(2)}) collective-permute-start(f32[2,96,256]{2,1,0:T(8,128)S(1)} %get-tuple-element.32), channel_id=1, source_target_pairs={{4,8},{5,9},{6,10},{7,11},{8,4},{9,5},{10,6},{11,7},{20,24},{21,25... | collective-permute-start | bytes 589832 | tf_op jit(solution)/shard_map/lines2b_1/ppermute | solution.py:344
  38.9 0.6 collective-permute-start.16
  39.5 1.2 %collective-permute-start.18 = (f32[2,160,256]{2,1,0:T(8,128)S(1)}, f32[2,160,256]{2,1,0:T(8,128)S(1)}, u32[]{:S(2)}, u32[]{:S(2)}) collective-permute-start(f32[2,160,256]{2,1,0:T(8,128)S(1)} %shard_map.80.refs_0_), channel_id=1, source_target_pairs={{0,16},{16,0},{1,17},{17,1},{2,18},{18,2},{3,19},{19,3},{4,20},{20... | collective-permute-start | bytes 983048 | tf_op jit(solution)/shard_map/slab_real_0/ppermute | solution.py:348
  40.7 1.9 %collective-permute-done.13.refs_6_.refs_5_.refs_3_ = f32[2,96,256]{2,1,0:T(8,128)S(1)} collective-permute-done((f32[2,96,256]{2,1,0:T(8,128)S(1)}, f32[2,96,256]{2,1,0:T(8,128)S(1)}, u32[]{:S(2)}, u32[]{:S(2)}) %collective-permute-start.13) | collective-permute-done | bytes 196640 | tf_op jit(solution)/shard_map/lines2b_1/ppermute | solution.py:344
  42.7 2.0 %collective-permute-done.16.refs_2_ = f32[2,96,256]{2,1,0:T(8,128)S(1)} collective-permute-done((f32[2,96,256]{2,1,0:T(8,128)S(1)}, f32[2,96,256]{2,1,0:T(8,128)S(1)}, u32[]{:S(2)}, u32[]{:S(2)}) %collective-permute-start.16) | collective-permute-done | bytes 196640 | tf_op jit(solution)/shard_map/imag_across_1/ppermute | solution.py:344
  45.1 0.6 %collective-permute-start.19 = (f32[2,96,256]{2,1,0:T(8,128)S(1)}, f32[2,96,256]{2,1,0:T(8,128)S(1)}, u32[]{:S(2)}, u32[]{:S(2)}) collective-permute-start(f32[2,96,256]{2,1,0:T(8,128)S(1)} %shard_map.83.refs_3_), channel_id=1, source_target_pairs={{0,16},{16,0},{1,17},{17,1},{2,18},{18,2},{3,19},{19,3},{4,20},{20... | collective-permute-start | bytes 589832 | tf_op jit(solution)/shard_map/slab_imag_1/ppermute | solution.py:348
  45.7 1.7 %collective-permute-done.18.real_ref = f32[2,160,256]{2,1,0:T(8,128)S(1)} collective-permute-done((f32[2,160,256]{2,1,0:T(8,128)S(1)}, f32[2,160,256]{2,1,0:T(8,128)S(1)}, u32[]{:S(2)}, u32[]{:S(2)}) %collective-permute-start.18) | collective-permute-done | bytes 327712 | tf_op jit(solution)/shard_map/slab_real_0/ppermute | solution.py:348
  47.5 1.2 %collective-permute-start.20 = (f32[2,96,256]{2,1,0:T(8,128)S(1)}, f32[2,96,256]{2,1,0:T(8,128)S(1)}, u32[]{:S(2)}, u32[]{:S(2)}) collective-permute-start(f32[2,96,256]{2,1,0:T(8,128)S(1)} %shard_map.85.refs_1_), channel_id=1, source_target_pairs={{0,16},{16,0},{1,17},{17,1},{2,18},{18,2},{3,19},{19,3},{4,20},{20... | collective-permute-start | bytes 589832 | tf_op jit(solution)/shard_map/slab_real_1/ppermute | solution.py:348
  48.8 2.2 %shard_map.86.source_ref = f32[2,2,256,256]{3,2,1,0:T(8,128)S(1)} custom-call(f32[2,2,256,256]{3,2,1,0:T(8,128)S(1)} %bitcast.22, f32[2,160,256]{2,1,0:T(8,128)S(1)} %shard_map.80.refs_0_, f32[2,96,256]{2,1,0:T(8,128)S(1)} %shard_map.85.refs_1_, f32[2,160,256]{2,1,0:T(8,128)S(1)} %shard_map.77.refs_2_, f32[2,96,256]{2,1,0:T(8,128)S(1)} %shard_map.83.refs_3_), custom_call_target="tpu_custom_call" | custom-call | flops 1610612736 | bytes 3145728 | tf_op jit(solution)/shard_map/pallas_call | solution.py:310
  51.0 0.7 %copy-done.8 = s32[1,4,4]{2,1,0:T(4,128)S(1)} copy-done((s32[1,4,4]{2,1,0:T(4,128)S(1)}, s32[1,4,4]{2,1,0:T(4,128)}, u32[]{:S(2)}) %copy-start.8) | copy-done | bytes 88
  51.6 2.3 %shard_map.87.bridge_ref = f32[2,2,256,256]{3,2,1,0:T(8,128)S(1)} custom-call(s32[4,4]{1,0:T(4,128)S(1)} %bitcast.25, f32[256,256]{1,0:T(8,128)S(1)} %bitcast.24, f32[2,2,256,256]{3,2,1,0:T(8,128)S(1)} %bitcast.23, f32[2,2,256,256]{3,2,1,0:T(8,128)S(1)} %copy-done.6), custom_call_target="tpu_custom_call" | custom-call | flops 1207959552 | bytes 3407936 | tf_op jit(solution)/shard_map/pallas_call | solution.py:310
  53.9 1.0 %shard_map.88.total_ref = f32[2,2,256,256]{3,2,1,0:T(8,128)S(1)} custom-call(f32[2,2,256,256]{3,2,1,0:T(8,128)S(1)} %shard_map.87.bridge_ref, f32[2,160,256]{2,1,0:T(8,128)S(1)} %collective-permute-done.18.real_ref, f32[2,160,256]{2,1,0:T(8,128)S(1)} %collective-permute-done.14.imag_ref), custom_call_target="tpu_custom_call" | custom-call | flops 805306368 | bytes 2752512 | tf_op jit(solution)/shard_map/pallas_call | solution.py:310
  54.9 0.6 %shard_map.89.half_ref = f32[2,2,256,256]{3,2,1,0:T(8,128)S(1)} custom-call(f32[2,2,256,256]{3,2,1,0:T(8,128)S(1)} %shard_map.87.bridge_ref, f32[2,96,256]{2,1,0:T(8,128)S(1)} %collective-permute-done.19.imag_ref, f32[2,2,256,256]{3,2,1,0:T(8,128)S(1)} %shard_map.88.total_ref), custom_call_target="tpu_custom_call" | custom-call | flops 402653184 | bytes 3342336 | tf_op jit(solution)/shard_map/pallas_call | solution.py:310
  55.5 1.1 %collective-permute-done.20.real_ref = f32[2,96,256]{2,1,0:T(8,128)S(1)} collective-permute-done((f32[2,96,256]{2,1,0:T(8,128)S(1)}, f32[2,96,256]{2,1,0:T(8,128)S(1)}, u32[]{:S(2)}, u32[]{:S(2)}) %collective-permute-start.20) | collective-permute-done | bytes 196640 | tf_op jit(solution)/shard_map/slab_real_1/ppermute | solution.py:348
  56.6 2.6 %shard_map.90 = f32[2,2,256,256]{3,2,1,0:T(8,128)} custom-call(s32[1]{0:T(128)} %bitcast.flag_ref, f32[2,2,256,256]{3,2,1,0:T(8,128)S(1)} %shard_map.87.bridge_ref, f32[2,2,256,256]{3,2,1,0:T(8,128)S(1)} %shard_map.89.half_ref, f32[2,96,256]{2,1,0:T(8,128)S(1)} %collective-permute-done.20.real_ref, f32[2,2,256,256]{3,2,1,0:T(8,128)S(1)} %shard_map.86.source_ref), custom_call_target="tpu_custom_call" | custom-call | flops 1207959552 | bytes 4390916 | tf_op jit(solution)/shard_map/pallas_call | solution.py:310
  (48 shorter events, 4.0 us)
Async XLA Ops:
  0.0 2.9 %copy-start.3 = (f32[1,2,2,256,256]{4,3,2,1,0:T(8,128)S(1)}, f32[1,2,2,256,256]{4,3,2,1,0:T(8,128)}, u32[]{:S(2)}) copy-start(f32[1,2,2,256,256]{4,3,2,1,0:T(8,128)} %param.7) | copy-start | bytes 3145732
  1.2 3.3 %collective-permute-start = (f32[2,160,256]{2,1,0:T(8,128)S(1)}, f32[2,160,256]{2,1,0:T(8,128)S(1)}, u32[]{:S(2)}, u32[]{:S(2)}) collective-permute-start(f32[2,160,256]{2,1,0:T(8,128)S(1)} %get-tuple-element.42.refs_0_), channel_id=1, source_target_pairs={{0,1},{1,0},{2,3},{3,2},{4,5},{5,4},{6,7},{7,6},{8,9},{9,8},{10,11... | collective-permute-start | bytes 983048 | tf_op jit(solution)/shard_map/imag_cores_0/ppermute | solution.py:344
  1.3 2.2 %copy-start = (s32[3]{0:T(128)S(1)}, s32[3]{0:T(128)}, u32[]{:S(2)}) copy-start(s32[3]{0:T(128)} %offsets_ref.1) | copy-start | bytes 40
  1.3 2.2 %copy-start.1 = (f32[3]{0:T(128)S(1)}, f32[3]{0:T(128)}, u32[]{:S(2)}) copy-start(f32[3]{0:T(128)} %coupling_ref.1) | copy-start | bytes 40
  1.3 2.1 %copy-start.2 = (f32[3]{0:T(128)S(1)}, f32[3]{0:T(128)}, u32[]{:S(2)}) copy-start(f32[3]{0:T(128)} %occupation_ref.1) | copy-start | bytes 40
  1.3 10.1 %collective-permute-start.4 = (f32[2,160,256]{2,1,0:T(8,128)S(1)}, f32[2,160,256]{2,1,0:T(8,128)S(1)}, u32[]{:S(2)}, u32[]{:S(2)}) collective-permute-start(f32[2,160,256]{2,1,0:T(8,128)S(1)} %get-tuple-element.41.refs_2_.refs_0_), channel_id=1, source_target_pairs={{0,2},{1,3},{2,0},{3,1},{4,6},{5,7},{6,4},{7,5},{8,10},{9,11},{10,... | collective-permute-start | bytes 983048 | tf_op jit(solution)/shard_map/real_across_0/ppermute | solution.py:344
  2.9 32.2 %collective-permute-start.9 = (f32[2,2,256,256]{3,2,1,0:T(8,128)S(1)}, f32[2,2,256,256]{3,2,1,0:T(8,128)S(1)}, u32[]{:S(2)}, u32[]{:S(2)}) collective-permute-start(f32[2,2,256,256]{3,2,1,0:T(8,128)S(1)} %bitcast.21), channel_id=1, source_target_pairs={{0,16},{16,0},{1,17},{17,1},{2,18},{18,2},{3,19},{19,3},{4,20},{20... | collective-permute-start | bytes 3145736 | tf_op jit(solution)/shard_map/slab_retarded/ppermute | solution.py:348
  4.8 12.0 %collective-permute-start.1 = (f32[2,160,256]{2,1,0:T(8,128)S(1)}, f32[2,160,256]{2,1,0:T(8,128)S(1)}, u32[]{:S(2)}, u32[]{:S(2)}) collective-permute-start(f32[2,160,256]{2,1,0:T(8,128)S(1)} %get-tuple-element.22), channel_id=1, source_target_pairs={{0,4},{1,5},{2,6},{3,7},{4,0},{5,1},{6,2},{7,3},{8,12},{9,13},{10,... | collective-permute-start | bytes 983048 | tf_op jit(solution)/shard_map/lines1a_0/ppermute | solution.py:344
  5.3 12.4 %collective-permute-start.2 = (f32[2,160,256]{2,1,0:T(8,128)S(1)}, f32[2,160,256]{2,1,0:T(8,128)S(1)}, u32[]{:S(2)}, u32[]{:S(2)}) collective-permute-start(f32[2,160,256]{2,1,0:T(8,128)S(1)} %get-tuple-element.23), channel_id=1, source_target_pairs={{4,8},{5,9},{6,10},{7,11},{8,4},{9,5},{10,6},{11,7},{20,24},{21,25... | collective-permute-start | bytes 983048 | tf_op jit(solution)/shard_map/lines1b_0/ppermute | solution.py:344
  11.7 9.7 %collective-permute-start.5 = (f32[2,160,256]{2,1,0:T(8,128)S(1)}, f32[2,160,256]{2,1,0:T(8,128)S(1)}, u32[]{:S(2)}, u32[]{:S(2)}) collective-permute-start(f32[2,160,256]{2,1,0:T(8,128)S(1)} %get-tuple-element.24), channel_id=1, source_target_pairs={{0,4},{1,5},{2,6},{3,7},{4,0},{5,1},{6,2},{7,3},{8,12},{9,13},{10,... | collective-permute-start | bytes 983048 | tf_op jit(solution)/shard_map/lines2a_0/ppermute | solution.py:344
  12.2 12.2 %collective-permute-start.6 = (f32[2,160,256]{2,1,0:T(8,128)S(1)}, f32[2,160,256]{2,1,0:T(8,128)S(1)}, u32[]{:S(2)}, u32[]{:S(2)}) collective-permute-start(f32[2,160,256]{2,1,0:T(8,128)S(1)} %get-tuple-element.25), channel_id=1, source_target_pairs={{4,8},{5,9},{6,10},{7,11},{8,4},{9,5},{10,6},{11,7},{20,24},{21,25... | collective-permute-start | bytes 983048 | tf_op jit(solution)/shard_map/lines2b_0/ppermute | solution.py:344
  17.9 8.5 %collective-permute-start.3 = (f32[2,160,256]{2,1,0:T(8,128)S(1)}, f32[2,160,256]{2,1,0:T(8,128)S(1)}, u32[]{:S(2)}, u32[]{:S(2)}) collective-permute-start(f32[2,160,256]{2,1,0:T(8,128)S(1)} %shard_map.75), channel_id=1, source_target_pairs={{0,2},{1,3},{2,0},{3,1},{4,6},{5,7},{6,4},{7,5},{8,10},{9,11},{10,... | collective-permute-start | bytes 983048 | tf_op jit(solution)/shard_map/imag_across_0/ppermute | solution.py:344
  24.7 4.3 %collective-permute-start.10 = (f32[2,160,256]{2,1,0:T(8,128)S(1)}, f32[2,160,256]{2,1,0:T(8,128)S(1)}, u32[]{:S(2)}, u32[]{:S(2)}) collective-permute-start(f32[2,160,256]{2,1,0:T(8,128)S(1)} %shard_map.79), channel_id=1, source_target_pairs={{0,1},{1,0},{2,3},{3,2},{4,5},{5,4},{6,7},{7,6},{8,9},{9,8},{10,11... | collective-permute-start | bytes 983048 | tf_op jit(solution)/shard_map/real_cores_0/ppermute | solution.py:344
  25.8 3.0 %collective-permute-start.7 = (f32[2,96,256]{2,1,0:T(8,128)S(1)}, f32[2,96,256]{2,1,0:T(8,128)S(1)}, u32[]{:S(2)}, u32[]{:S(2)}) collective-permute-start(f32[2,96,256]{2,1,0:T(8,128)S(1)} %get-tuple-element.26.refs_0_), channel_id=1, source_target_pairs={{0,1},{1,0},{2,3},{3,2},{4,5},{5,4},{6,7},{7,6},{8,9},{9,8},{10,11... | collective-permute-start | bytes 589832 | tf_op jit(solution)/shard_map/imag_cores_1/ppermute | solution.py:344
  26.7 12.0 %collective-permute-start.14 = (f32[2,160,256]{2,1,0:T(8,128)S(1)}, f32[2,160,256]{2,1,0:T(8,128)S(1)}, u32[]{:S(2)}, u32[]{:S(2)}) collective-permute-start(f32[2,160,256]{2,1,0:T(8,128)S(1)} %shard_map.77.refs_2_), channel_id=1, source_target_pairs={{0,16},{16,0},{1,17},{17,1},{2,18},{18,2},{3,19},{19,3},{4,20},{20... | collective-permute-start | bytes 983048 | tf_op jit(solution)/shard_map/slab_imag_0/ppermute | solution.py:348
  28.3 6.5 %collective-permute-start.11 = (f32[2,96,256]{2,1,0:T(8,128)S(1)}, f32[2,96,256]{2,1,0:T(8,128)S(1)}, u32[]{:S(2)}, u32[]{:S(2)}) collective-permute-start(f32[2,96,256]{2,1,0:T(8,128)S(1)} %get-tuple-element.36.refs_2_.refs_0_), channel_id=1, source_target_pairs={{0,2},{1,3},{2,0},{3,1},{4,6},{5,7},{6,4},{7,5},{8,10},{9,11},{10,... | collective-permute-start | bytes 589832 | tf_op jit(solution)/shard_map/real_across_1/ppermute | solution.py:344
  28.9 9.8 %collective-permute-start.8 = (f32[2,96,256]{2,1,0:T(8,128)S(1)}, f32[2,96,256]{2,1,0:T(8,128)S(1)}, u32[]{:S(2)}, u32[]{:S(2)}) collective-permute-start(f32[2,96,256]{2,1,0:T(8,128)S(1)} %get-tuple-element.27), channel_id=1, source_target_pairs={{0,4},{1,5},{2,6},{3,7},{4,0},{5,1},{6,2},{7,3},{8,12},{9,13},{10,... | collective-permute-start | bytes 589832 | tf_op jit(solution)/shard_map/lines1a_1/ppermute | solution.py:344
  29.0 9.7 %collective-permute-start.15 = (f32[2,96,256]{2,1,0:T(8,128)S(1)}, f32[2,96,256]{2,1,0:T(8,128)S(1)}, u32[]{:S(2)}, u32[]{:S(2)}) collective-permute-start(f32[2,96,256]{2,1,0:T(8,128)S(1)} %get-tuple-element.35), channel_id=1, source_target_pairs={{4,8},{5,9},{6,10},{7,11},{8,4},{9,5},{10,6},{11,7},{20,24},{21,25... | collective-permute-start | bytes 589832 | tf_op jit(solution)/shard_map/lines1b_1/ppermute | solution.py:344
  35.0 5.7 %collective-permute-start.12 = (f32[2,96,256]{2,1,0:T(8,128)S(1)}, f32[2,96,256]{2,1,0:T(8,128)S(1)}, u32[]{:S(2)}, u32[]{:S(2)}) collective-permute-start(f32[2,96,256]{2,1,0:T(8,128)S(1)} %get-tuple-element.31), channel_id=1, source_target_pairs={{0,4},{1,5},{2,6},{3,7},{4,0},{5,1},{6,2},{7,3},{8,12},{9,13},{10,... | collective-permute-start | bytes 589832 | tf_op jit(solution)/shard_map/lines2a_1/ppermute | solution.py:344
  35.1 9.7 %copy-start.5 = (f32[2,2,256,256]{3,2,1,0:T(8,128)}, f32[2,2,256,256]{3,2,1,0:T(8,128)S(1)}, u32[]{:S(2)}) copy-start(f32[2,2,256,256]{3,2,1,0:T(8,128)S(1)} %collective-permute-done.9.behind_ref) | copy-start | bytes 3145732
  35.1 7.6 %collective-permute-start.13 = (f32[2,96,256]{2,1,0:T(8,128)S(1)}, f32[2,96,256]{2,1,0:T(8,128)S(1)}, u32[]{:S(2)}, u32[]{:S(2)}) collective-permute-start(f32[2,96,256]{2,1,0:T(8,128)S(1)} %get-tuple-element.32), channel_id=1, source_target_pairs={{4,8},{5,9},{6,10},{7,11},{8,4},{9,5},{10,6},{11,7},{20,24},{21,25... | collective-permute-start | bytes 589832 | tf_op jit(solution)/shard_map/lines2b_1/ppermute | solution.py:344
  38.9 5.7 %collective-permute-start.16 = (f32[2,96,256]{2,1,0:T(8,128)S(1)}, f32[2,96,256]{2,1,0:T(8,128)S(1)}, u32[]{:S(2)}, u32[]{:S(2)}) collective-permute-start(f32[2,96,256]{2,1,0:T(8,128)S(1)} %shard_map.82), channel_id=1, source_target_pairs={{0,2},{1,3},{2,0},{3,1},{4,6},{5,7},{6,4},{7,5},{8,10},{9,11},{10,... | collective-permute-start | bytes 589832 | tf_op jit(solution)/shard_map/imag_across_1/ppermute | solution.py:344
  39.5 7.9 %collective-permute-start.18 = (f32[2,160,256]{2,1,0:T(8,128)S(1)}, f32[2,160,256]{2,1,0:T(8,128)S(1)}, u32[]{:S(2)}, u32[]{:S(2)}) collective-permute-start(f32[2,160,256]{2,1,0:T(8,128)S(1)} %shard_map.80.refs_0_), channel_id=1, source_target_pairs={{0,16},{16,0},{1,17},{17,1},{2,18},{18,2},{3,19},{19,3},{4,20},{20... | collective-permute-start | bytes 983048 | tf_op jit(solution)/shard_map/slab_real_0/ppermute | solution.py:348
  45.0 2.4 %collective-permute-start.17 = (f32[2,96,256]{2,1,0:T(8,128)S(1)}, f32[2,96,256]{2,1,0:T(8,128)S(1)}, u32[]{:S(2)}, u32[]{:S(2)}) collective-permute-start(f32[2,96,256]{2,1,0:T(8,128)S(1)} %shard_map.84), channel_id=1, source_target_pairs={{0,1},{1,0},{2,3},{3,2},{4,5},{5,4},{6,7},{7,6},{8,9},{9,8},{10,11... | collective-permute-start | bytes 589832 | tf_op jit(solution)/shard_map/real_cores_1/ppermute | solution.py:344
  45.1 3.7 %copy-start.4 = (f32[1,2,2,256,256]{4,3,2,1,0:T(8,128)S(1)}, f32[1,2,2,256,256]{4,3,2,1,0:T(8,128)}, u32[]{:S(2)}) copy-start(f32[1,2,2,256,256]{4,3,2,1,0:T(8,128)} %param.7) | copy-start | bytes 3145732
  45.1 9.8 %collective-permute-start.19 = (f32[2,96,256]{2,1,0:T(8,128)S(1)}, f32[2,96,256]{2,1,0:T(8,128)S(1)}, u32[]{:S(2)}, u32[]{:S(2)}) collective-permute-start(f32[2,96,256]{2,1,0:T(8,128)S(1)} %shard_map.83.refs_3_), channel_id=1, source_target_pairs={{0,16},{16,0},{1,17},{17,1},{2,18},{18,2},{3,19},{19,3},{4,20},{20... | collective-permute-start | bytes 589832 | tf_op jit(solution)/shard_map/slab_imag_1/ppermute | solution.py:348
  47.5 3.5 %copy-start.6 = (f32[2,2,256,256]{3,2,1,0:T(8,128)S(1)}, f32[2,2,256,256]{3,2,1,0:T(8,128)}, u32[]{:S(2)}) copy-start(f32[2,2,256,256]{3,2,1,0:T(8,128)} %copy-done.5) | copy-start | bytes 3145732
  47.5 3.5 %copy-start.7 = (f32[1,256,256]{2,1,0:T(8,128)S(1)}, f32[1,256,256]{2,1,0:T(8,128)}, u32[]{:S(2)}) copy-start(f32[1,256,256]{2,1,0:T(8,128)} %param.9) | copy-start | bytes 786436
  47.5 9.1 %collective-permute-start.20 = (f32[2,96,256]{2,1,0:T(8,128)S(1)}, f32[2,96,256]{2,1,0:T(8,128)S(1)}, u32[]{:S(2)}, u32[]{:S(2)}) collective-permute-start(f32[2,96,256]{2,1,0:T(8,128)S(1)} %shard_map.85.refs_1_), channel_id=1, source_target_pairs={{0,16},{16,0},{1,17},{17,1},{2,18},{18,2},{3,19},{19,3},{4,20},{20... | collective-permute-start | bytes 589832 | tf_op jit(solution)/shard_map/slab_real_1/ppermute | solution.py:348
  51.0 0.7 %copy-start.8 = (s32[1,4,4]{2,1,0:T(4,128)S(1)}, s32[1,4,4]{2,1,0:T(4,128)}, u32[]{:S(2)}) copy-start(s32[1,4,4]{2,1,0:T(4,128)} %param.10) | copy-start | bytes 196

commit v5 on v3

--- a/solution.py
+++ b/solution.py
@@ -393,7 +393,7 @@
         sibling_sum = combine(weights, bases[4], [real_late, real_beside, got1, got2, got3, got4], 1)
         real_sibling = permute(sibling_sum, cores, f"real_cores_{number}")
         if gates is not None:
-            real_sibling = after(real_sibling, reals_behind[-1])
+            got4 = after(got4, reals_behind[-1])
         self_real = combine(weights, bases[5], [real, real_beside, got3, got4, real_sibling], 1)
         gates = (imag_beside, self_imag, self_real)
         imags.append(self_imag)

time: 59.4 us -> 59.4 us (level)
  no operation moved by 1% of the time
where the time goes in v5:
time: 59.4 us; the launch traced here: 59.2 us
  starting transfers between devices  27.1 us (46%)
  waiting for transfers between devices  16.6 us (28%)
  Pallas kernels  12.1 us (20%)
  local copies, waits for them, and re-layouts  2.97 us (5%)
    ppermute x16, starting transfers between devices, permute(): return lax.ppermute(value, 'energy', pairs)  21.8 us
    ppermute x16, waiting for transfers between devices, permute(): return lax.ppermute(value, 'energy', pairs)  14.1 us
    pallas_call x5, Pallas kernels, call(): pl.pallas_call(kernel, out_shape=[jax.ShapeDtypeStruct(array.shape, jnp.f...  8.63 us
    ppermute x5, starting transfers between devices, to_next_slab(): return lax.ppermute(value, 'slab', ahead)  5.35 us
    ppermute x5, waiting for transfers between devices, to_next_slab(): return lax.ppermute(value, 'slab', ahead)  2.48 us
    pallas_call x12, Pallas kernels, combine(): pl.pallas_call(functools.partial(combine_kernel, base, counts), out_shape...  2.4 us
    squeeze x2, local copies, waits for them, and re-layouts, body(): real, imag = (lesser_prev[0, :, 0, window], lesser_prev[0, :, 1, window])  2.26 us
  transfers between devices with their start and end apart: 21, of which 10 were waited for; matrix products, arithmetic and copies ran while one was open for 2% of the time, Pallas kernels for 16%

profile of v5, /device:TPU:10, one launch (start us, length us, event | category | flops | bytes accessed | tf_op | source)
XLA Modules:
  0.0 59.2 jit_solution(15845123112559403473)
XLA Ops:
  0.0 1.2 %slice_bitcast_fusion = (f32[2,160,256]{2,1,0:T(8,128)S(1)}, f32[2,160,256]{2,1,0:T(8,128)S(1)}) fusion(f32[1,2,2,256,256]{4,3,2,1,0:T(8,128)} %param.8), kind=kLoop, calls=%fused_computation | loop fusion | bytes 1310720 | tf_op jit(solution)/shard_map/squeeze | solution.py:368
  1.3 1.6 %collective-permute-start.4 = (f32[2,160,256]{2,1,0:T(8,128)S(1)}, f32[2,160,256]{2,1,0:T(8,128)S(1)}, u32[]{:S(2)}, u32[]{:S(2)}) collective-permute-start(f32[2,160,256]{2,1,0:T(8,128)S(1)} %get-tuple-element.41.refs_2_.refs_0_), channel_id=1, source_target_pairs={{0,2},{1,3},{2,0},{3,1},{4,6},{5,7},{6,4},{7,5},{8,10},{9,11},{10,... | collective-permute-start | bytes 983048 | tf_op jit(solution)/shard_map/real_across_0/ppermute | solution.py:344
  2.9 0.5 collective-permute-start.9
  3.5 1.1 %shard_map.73.weights_ref = f32[136,8,128]{2,1,0:T(8,128)S(1)} custom-call(s32[3]{0:T(128)S(1)} %copy-done, f32[3]{0:T(128)S(1)} %copy-done.1, f32[3]{0:T(128)S(1)} %copy-done.2), custom_call_target="tpu_custom_call" | custom-call | tf_op jit(solution)/shard_map/pallas_call | solution.py:334
  4.8 0.5 collective-permute-start.1
  5.3 4.6 %collective-permute-start.2 = (f32[2,160,256]{2,1,0:T(8,128)S(1)}, f32[2,160,256]{2,1,0:T(8,128)S(1)}, u32[]{:S(2)}, u32[]{:S(2)}) collective-permute-start(f32[2,160,256]{2,1,0:T(8,128)S(1)} %get-tuple-element.23), channel_id=1, source_target_pairs={{4,8},{5,9},{6,10},{7,11},{8,4},{9,5},{10,6},{11,7},{20,24},{21,25... | collective-permute-start | bytes 983048 | tf_op jit(solution)/shard_map/lines1b_0/ppermute | solution.py:344
  9.9 1.5 %collective-permute-done.4.refs_0_.refs_1_ = f32[2,160,256]{2,1,0:T(8,128)S(1)} collective-permute-done((f32[2,160,256]{2,1,0:T(8,128)S(1)}, f32[2,160,256]{2,1,0:T(8,128)S(1)}, u32[]{:S(2)}, u32[]{:S(2)}) %collective-permute-start.4) | collective-permute-done | bytes 327712 | tf_op jit(solution)/shard_map/real_across_0/ppermute | solution.py:344
  11.7 0.5 collective-permute-start.5
  12.2 4.6 %collective-permute-start.6 = (f32[2,160,256]{2,1,0:T(8,128)S(1)}, f32[2,160,256]{2,1,0:T(8,128)S(1)}, u32[]{:S(2)}, u32[]{:S(2)}) collective-permute-start(f32[2,160,256]{2,1,0:T(8,128)S(1)} %get-tuple-element.25), channel_id=1, source_target_pairs={{4,8},{5,9},{6,10},{7,11},{8,4},{9,5},{10,6},{11,7},{20,24},{21,25... | collective-permute-start | bytes 983048 | tf_op jit(solution)/shard_map/lines2b_0/ppermute | solution.py:344
  16.8 0.9 %collective-permute-done.2.refs_3_.refs_4_ = f32[2,160,256]{2,1,0:T(8,128)S(1)} collective-permute-done((f32[2,160,256]{2,1,0:T(8,128)S(1)}, f32[2,160,256]{2,1,0:T(8,128)S(1)}, u32[]{:S(2)}, u32[]{:S(2)}) %collective-permute-start.2) | collective-permute-done | bytes 327712 | tf_op jit(solution)/shard_map/lines1b_0/ppermute | solution.py:344
  17.9 0.7 %collective-permute-start.3 = (f32[2,160,256]{2,1,0:T(8,128)S(1)}, f32[2,160,256]{2,1,0:T(8,128)S(1)}, u32[]{:S(2)}, u32[]{:S(2)}) collective-permute-start(f32[2,160,256]{2,1,0:T(8,128)S(1)} %shard_map.75), channel_id=1, source_target_pairs={{0,2},{1,3},{2,0},{3,1},{4,6},{5,7},{6,4},{7,5},{8,10},{9,11},{10,... | collective-permute-start | bytes 983048 | tf_op jit(solution)/shard_map/imag_across_0/ppermute | solution.py:344
  18.6 2.8 %collective-permute-done.5.refs_5_.refs_4_.refs_2_ = f32[2,160,256]{2,1,0:T(8,128)S(1)} collective-permute-done((f32[2,160,256]{2,1,0:T(8,128)S(1)}, f32[2,160,256]{2,1,0:T(8,128)S(1)}, u32[]{:S(2)}, u32[]{:S(2)}) %collective-permute-start.5) | collective-permute-done | bytes 327712 | tf_op jit(solution)/shard_map/lines2a_0/ppermute | solution.py:344
  21.4 3.0 %collective-permute-done.6.refs_6_.refs_5_.refs_3_ = f32[2,160,256]{2,1,0:T(8,128)S(1)} collective-permute-done((f32[2,160,256]{2,1,0:T(8,128)S(1)}, f32[2,160,256]{2,1,0:T(8,128)S(1)}, u32[]{:S(2)}, u32[]{:S(2)}) %collective-permute-start.6) | collective-permute-done | bytes 327712 | tf_op jit(solution)/shard_map/lines2b_0/ppermute | solution.py:344
  24.8 1.1 %slice_bitcast_fusion.2 = (f32[2,96,256]{2,1,0:T(8,128)S(1)}, f32[2,96,256]{2,1,0:T(8,128)S(1)}) fusion(f32[1,2,2,256,256]{4,3,2,1,0:T(8,128)} %param.8), kind=kLoop, calls=%fused_computation.2 | loop fusion | bytes 786432 | tf_op jit(solution)/shard_map/squeeze | solution.py:368
  25.8 0.6 collective-permute-start.7
  26.7 1.6 %collective-permute-start.15 = (f32[2,160,256]{2,1,0:T(8,128)S(1)}, f32[2,160,256]{2,1,0:T(8,128)S(1)}, u32[]{:S(2)}, u32[]{:S(2)}) collective-permute-start(f32[2,160,256]{2,1,0:T(8,128)S(1)} %shard_map.77.refs_2_), channel_id=1, source_target_pairs={{0,16},{16,0},{1,17},{17,1},{2,18},{18,2},{3,19},{19,3},{4,20},{20... | collective-permute-start | bytes 983048 | tf_op jit(solution)/shard_map/slab_imag_0/ppermute | solution.py:348
  29.0 3.6 %collective-permute-start.16 = (f32[2,96,256]{2,1,0:T(8,128)S(1)}, f32[2,96,256]{2,1,0:T(8,128)S(1)}, u32[]{:S(2)}, u32[]{:S(2)}) collective-permute-start(f32[2,96,256]{2,1,0:T(8,128)S(1)} %get-tuple-element.36), channel_id=1, source_target_pairs={{4,8},{5,9},{6,10},{7,11},{8,4},{9,5},{10,6},{11,7},{20,24},{21,25... | collective-permute-start | bytes 589832 | tf_op jit(solution)/shard_map/lines1b_1/ppermute | solution.py:344
  32.9 1.9 %collective-permute-done.11.refs_0_.refs_1_ = f32[2,96,256]{2,1,0:T(8,128)S(1)} collective-permute-done((f32[2,96,256]{2,1,0:T(8,128)S(1)}, f32[2,96,256]{2,1,0:T(8,128)S(1)}, u32[]{:S(2)}, u32[]{:S(2)}) %collective-permute-start.11) | collective-permute-done | bytes 196640 | tf_op jit(solution)/shard_map/real_across_1/ppermute | solution.py:344
  35.1 3.6 %collective-permute-start.13 = (f32[2,96,256]{2,1,0:T(8,128)S(1)}, f32[2,96,256]{2,1,0:T(8,128)S(1)}, u32[]{:S(2)}, u32[]{:S(2)}) collective-permute-start(f32[2,96,256]{2,1,0:T(8,128)S(1)} %get-tuple-element.32), channel_id=1, source_target_pairs={{4,8},{5,9},{6,10},{7,11},{8,4},{9,5},{10,6},{11,7},{20,24},{21,25... | collective-permute-start | bytes 589832 | tf_op jit(solution)/shard_map/lines2b_1/ppermute | solution.py:344
  38.9 0.6 collective-permute-start.17
  39.5 1.2 %collective-permute-start.14 = (f32[2,160,256]{2,1,0:T(8,128)S(1)}, f32[2,160,256]{2,1,0:T(8,128)S(1)}, u32[]{:S(2)}, u32[]{:S(2)}) collective-permute-start(f32[2,160,256]{2,1,0:T(8,128)S(1)} %shard_map.80.refs_0_), channel_id=1, source_target_pairs={{0,16},{16,0},{1,17},{17,1},{2,18},{18,2},{3,19},{19,3},{4,20},{20... | collective-permute-start | bytes 983048 | tf_op jit(solution)/shard_map/slab_real_0/ppermute | solution.py:348
  40.7 1.9 %collective-permute-done.13.refs_6_.refs_5_.refs_3_ = f32[2,96,256]{2,1,0:T(8,128)S(1)} collective-permute-done((f32[2,96,256]{2,1,0:T(8,128)S(1)}, f32[2,96,256]{2,1,0:T(8,128)S(1)}, u32[]{:S(2)}, u32[]{:S(2)}) %collective-permute-start.13) | collective-permute-done | bytes 196640 | tf_op jit(solution)/shard_map/lines2b_1/ppermute | solution.py:344
  42.7 2.0 %collective-permute-done.17.refs_2_ = f32[2,96,256]{2,1,0:T(8,128)S(1)} collective-permute-done((f32[2,96,256]{2,1,0:T(8,128)S(1)}, f32[2,96,256]{2,1,0:T(8,128)S(1)}, u32[]{:S(2)}, u32[]{:S(2)}) %collective-permute-start.17) | collective-permute-done | bytes 196640 | tf_op jit(solution)/shard_map/imag_across_1/ppermute | solution.py:344
  45.1 2.3 %collective-permute-done.14.real_ref = f32[2,160,256]{2,1,0:T(8,128)S(1)} collective-permute-done((f32[2,160,256]{2,1,0:T(8,128)S(1)}, f32[2,160,256]{2,1,0:T(8,128)S(1)}, u32[]{:S(2)}, u32[]{:S(2)}) %collective-permute-start.14) | collective-permute-done | bytes 327712 | tf_op jit(solution)/shard_map/slab_real_0/ppermute | solution.py:348
  47.4 1.2 %collective-permute-start.19 = (f32[2,96,256]{2,1,0:T(8,128)S(1)}, f32[2,96,256]{2,1,0:T(8,128)S(1)}, u32[]{:S(2)}, u32[]{:S(2)}) collective-permute-start(f32[2,96,256]{2,1,0:T(8,128)S(1)} %shard_map.83.refs_3_), channel_id=1, source_target_pairs={{0,16},{16,0},{1,17},{17,1},{2,18},{18,2},{3,19},{19,3},{4,20},{20... | collective-permute-start | bytes 589832 | tf_op jit(solution)/shard_map/slab_imag_1/ppermute | solution.py:348
  48.7 0.9 %collective-permute-start.20 = (f32[2,96,256]{2,1,0:T(8,128)S(1)}, f32[2,96,256]{2,1,0:T(8,128)S(1)}, u32[]{:S(2)}, u32[]{:S(2)}) collective-permute-start(f32[2,96,256]{2,1,0:T(8,128)S(1)} %shard_map.85.refs_1_), channel_id=1, source_target_pairs={{0,16},{16,0},{1,17},{17,1},{2,18},{18,2},{3,19},{19,3},{4,20},{20... | collective-permute-start | bytes 589832 | tf_op jit(solution)/shard_map/slab_real_1/ppermute | solution.py:348
  49.6 2.2 %shard_map.86.source_ref = f32[2,2,256,256]{3,2,1,0:T(8,128)S(1)} custom-call(f32[2,2,256,256]{3,2,1,0:T(8,128)S(1)} %bitcast.22, f32[2,160,256]{2,1,0:T(8,128)S(1)} %shard_map.80.refs_0_, f32[2,96,256]{2,1,0:T(8,128)S(1)} %shard_map.85.refs_1_, f32[2,160,256]{2,1,0:T(8,128)S(1)} %shard_map.77.refs_2_, f32[2,96,256]{2,1,0:T(8,128)S(1)} %shard_map.83.refs_3_), custom_call_target="tpu_custom_call" | custom-call | flops 1610612736 | bytes 3145728 | tf_op jit(solution)/shard_map/pallas_call | solution.py:310
  51.9 0.7 %copy-done.8 = s32[1,4,4]{2,1,0:T(4,128)S(1)} copy-done((s32[1,4,4]{2,1,0:T(4,128)S(1)}, s32[1,4,4]{2,1,0:T(4,128)}, u32[]{:S(2)}) %copy-start.8) | copy-done | bytes 88
  52.5 2.3 %shard_map.87.bridge_ref = f32[2,2,256,256]{3,2,1,0:T(8,128)S(1)} custom-call(s32[4,4]{1,0:T(4,128)S(1)} %bitcast.25, f32[256,256]{1,0:T(8,128)S(1)} %bitcast.24, f32[2,2,256,256]{3,2,1,0:T(8,128)S(1)} %bitcast.23, f32[2,2,256,256]{3,2,1,0:T(8,128)S(1)} %copy-done.6), custom_call_target="tpu_custom_call" | custom-call | flops 1207959552 | bytes 3407936 | tf_op jit(solution)/shard_map/pallas_call | solution.py:310
  54.8 1.0 %shard_map.88.total_ref = f32[2,2,256,256]{3,2,1,0:T(8,128)S(1)} custom-call(f32[2,2,256,256]{3,2,1,0:T(8,128)S(1)} %shard_map.87.bridge_ref, f32[2,160,256]{2,1,0:T(8,128)S(1)} %collective-permute-done.14.real_ref, f32[2,160,256]{2,1,0:T(8,128)S(1)} %collective-permute-done.15.imag_ref), custom_call_target="tpu_custom_call" | custom-call | flops 805306368 | bytes 2752512 | tf_op jit(solution)/shard_map/pallas_call | solution.py:310
  55.8 0.6 %shard_map.89.half_ref = f32[2,2,256,256]{3,2,1,0:T(8,128)S(1)} custom-call(f32[2,2,256,256]{3,2,1,0:T(8,128)S(1)} %shard_map.87.bridge_ref, f32[2,96,256]{2,1,0:T(8,128)S(1)} %collective-permute-done.19.imag_ref, f32[2,2,256,256]{3,2,1,0:T(8,128)S(1)} %shard_map.88.total_ref), custom_call_target="tpu_custom_call" | custom-call | flops 402653184 | bytes 3342336 | tf_op jit(solution)/shard_map/pallas_call | solution.py:310
  56.6 2.6 %shard_map.90 = f32[2,2,256,256]{3,2,1,0:T(8,128)} custom-call(s32[1]{0:T(128)} %bitcast.flag_ref, f32[2,2,256,256]{3,2,1,0:T(8,128)S(1)} %shard_map.87.bridge_ref, f32[2,2,256,256]{3,2,1,0:T(8,128)S(1)} %shard_map.89.half_ref, f32[2,96,256]{2,1,0:T(8,128)S(1)} %collective-permute-done.20.real_ref, f32[2,2,256,256]{3,2,1,0:T(8,128)S(1)} %shard_map.86.source_ref), custom_call_target="tpu_custom_call" | custom-call | flops 1207959552 | bytes 4390916 | tf_op jit(solution)/shard_map/pallas_call | solution.py:310
  (48 shorter events, 3.6 us)
Async XLA Ops:
  0.0 2.9 %copy-start.3 = (f32[1,2,2,256,256]{4,3,2,1,0:T(8,128)S(1)}, f32[1,2,2,256,256]{4,3,2,1,0:T(8,128)}, u32[]{:S(2)}) copy-start(f32[1,2,2,256,256]{4,3,2,1,0:T(8,128)} %param.7) | copy-start | bytes 3145732
  1.2 3.3 %collective-permute-start = (f32[2,160,256]{2,1,0:T(8,128)S(1)}, f32[2,160,256]{2,1,0:T(8,128)S(1)}, u32[]{:S(2)}, u32[]{:S(2)}) collective-permute-start(f32[2,160,256]{2,1,0:T(8,128)S(1)} %get-tuple-element.42.refs_0_), channel_id=1, source_target_pairs={{0,1},{1,0},{2,3},{3,2},{4,5},{5,4},{6,7},{7,6},{8,9},{9,8},{10,11... | collective-permute-start | bytes 983048 | tf_op jit(solution)/shard_map/imag_cores_0/ppermute | solution.py:344
  1.3 2.2 %copy-start = (s32[3]{0:T(128)S(1)}, s32[3]{0:T(128)}, u32[]{:S(2)}) copy-start(s32[3]{0:T(128)} %offsets_ref.1) | copy-start | bytes 40
  1.3 2.2 %copy-start.1 = (f32[3]{0:T(128)S(1)}, f32[3]{0:T(128)}, u32[]{:S(2)}) copy-start(f32[3]{0:T(128)} %coupling_ref.1) | copy-start | bytes 40
  1.3 2.1 %copy-start.2 = (f32[3]{0:T(128)S(1)}, f32[3]{0:T(128)}, u32[]{:S(2)}) copy-start(f32[3]{0:T(128)} %occupation_ref.1) | copy-start | bytes 40
  1.3 10.1 %collective-permute-start.4 = (f32[2,160,256]{2,1,0:T(8,128)S(1)}, f32[2,160,256]{2,1,0:T(8,128)S(1)}, u32[]{:S(2)}, u32[]{:S(2)}) collective-permute-start(f32[2,160,256]{2,1,0:T(8,128)S(1)} %get-tuple-element.41.refs_2_.refs_0_), channel_id=1, source_target_pairs={{0,2},{1,3},{2,0},{3,1},{4,6},{5,7},{6,4},{7,5},{8,10},{9,11},{10,... | collective-permute-start | bytes 983048 | tf_op jit(solution)/shard_map/real_across_0/ppermute | solution.py:344
  2.9 32.2 %collective-permute-start.9 = (f32[2,2,256,256]{3,2,1,0:T(8,128)S(1)}, f32[2,2,256,256]{3,2,1,0:T(8,128)S(1)}, u32[]{:S(2)}, u32[]{:S(2)}) collective-permute-start(f32[2,2,256,256]{3,2,1,0:T(8,128)S(1)} %bitcast.21), channel_id=1, source_target_pairs={{0,16},{16,0},{1,17},{17,1},{2,18},{18,2},{3,19},{19,3},{4,20},{20... | collective-permute-start | bytes 3145736 | tf_op jit(solution)/shard_map/slab_retarded/ppermute | solution.py:348
  4.8 12.0 %collective-permute-start.1 = (f32[2,160,256]{2,1,0:T(8,128)S(1)}, f32[2,160,256]{2,1,0:T(8,128)S(1)}, u32[]{:S(2)}, u32[]{:S(2)}) collective-permute-start(f32[2,160,256]{2,1,0:T(8,128)S(1)} %get-tuple-element.22), channel_id=1, source_target_pairs={{0,4},{1,5},{2,6},{3,7},{4,0},{5,1},{6,2},{7,3},{8,12},{9,13},{10,... | collective-permute-start | bytes 983048 | tf_op jit(solution)/shard_map/lines1a_0/ppermute | solution.py:344
  5.3 12.4 %collective-permute-start.2 = (f32[2,160,256]{2,1,0:T(8,128)S(1)}, f32[2,160,256]{2,1,0:T(8,128)S(1)}, u32[]{:S(2)}, u32[]{:S(2)}) collective-permute-start(f32[2,160,256]{2,1,0:T(8,128)S(1)} %get-tuple-element.23), channel_id=1, source_target_pairs={{4,8},{5,9},{6,10},{7,11},{8,4},{9,5},{10,6},{11,7},{20,24},{21,25... | collective-permute-start | bytes 983048 | tf_op jit(solution)/shard_map/lines1b_0/ppermute | solution.py:344
  11.7 9.7 %collective-permute-start.5 = (f32[2,160,256]{2,1,0:T(8,128)S(1)}, f32[2,160,256]{2,1,0:T(8,128)S(1)}, u32[]{:S(2)}, u32[]{:S(2)}) collective-permute-start(f32[2,160,256]{2,1,0:T(8,128)S(1)} %get-tuple-element.24), channel_id=1, source_target_pairs={{0,4},{1,5},{2,6},{3,7},{4,0},{5,1},{6,2},{7,3},{8,12},{9,13},{10,... | collective-permute-start | bytes 983048 | tf_op jit(solution)/shard_map/lines2a_0/ppermute | solution.py:344
  12.2 12.2 %collective-permute-start.6 = (f32[2,160,256]{2,1,0:T(8,128)S(1)}, f32[2,160,256]{2,1,0:T(8,128)S(1)}, u32[]{:S(2)}, u32[]{:S(2)}) collective-permute-start(f32[2,160,256]{2,1,0:T(8,128)S(1)} %get-tuple-element.25), channel_id=1, source_target_pairs={{4,8},{5,9},{6,10},{7,11},{8,4},{9,5},{10,6},{11,7},{20,24},{21,25... | collective-permute-start | bytes 983048 | tf_op jit(solution)/shard_map/lines2b_0/ppermute | solution.py:344
  17.9 8.5 %collective-permute-start.3 = (f32[2,160,256]{2,1,0:T(8,128)S(1)}, f32[2,160,256]{2,1,0:T(8,128)S(1)}, u32[]{:S(2)}, u32[]{:S(2)}) collective-permute-start(f32[2,160,256]{2,1,0:T(8,128)S(1)} %shard_map.75), channel_id=1, source_target_pairs={{0,2},{1,3},{2,0},{3,1},{4,6},{5,7},{6,4},{7,5},{8,10},{9,11},{10,... | collective-permute-start | bytes 983048 | tf_op jit(solution)/shard_map/imag_across_0/ppermute | solution.py:344
  24.7 4.3 %collective-permute-start.10 = (f32[2,160,256]{2,1,0:T(8,128)S(1)}, f32[2,160,256]{2,1,0:T(8,128)S(1)}, u32[]{:S(2)}, u32[]{:S(2)}) collective-permute-start(f32[2,160,256]{2,1,0:T(8,128)S(1)} %shard_map.79), channel_id=1, source_target_pairs={{0,1},{1,0},{2,3},{3,2},{4,5},{5,4},{6,7},{7,6},{8,9},{9,8},{10,11... | collective-permute-start | bytes 983048 | tf_op jit(solution)/shard_map/real_cores_0/ppermute | solution.py:344
  25.8 3.0 %collective-permute-start.7 = (f32[2,96,256]{2,1,0:T(8,128)S(1)}, f32[2,96,256]{2,1,0:T(8,128)S(1)}, u32[]{:S(2)}, u32[]{:S(2)}) collective-permute-start(f32[2,96,256]{2,1,0:T(8,128)S(1)} %get-tuple-element.26.refs_0_), channel_id=1, source_target_pairs={{0,1},{1,0},{2,3},{3,2},{4,5},{5,4},{6,7},{7,6},{8,9},{9,8},{10,11... | collective-permute-start | bytes 589832 | tf_op jit(solution)/shard_map/imag_cores_1/ppermute | solution.py:344
  26.7 12.0 %collective-permute-start.15 = (f32[2,160,256]{2,1,0:T(8,128)S(1)}, f32[2,160,256]{2,1,0:T(8,128)S(1)}, u32[]{:S(2)}, u32[]{:S(2)}) collective-permute-start(f32[2,160,256]{2,1,0:T(8,128)S(1)} %shard_map.77.refs_2_), channel_id=1, source_target_pairs={{0,16},{16,0},{1,17},{17,1},{2,18},{18,2},{3,19},{19,3},{4,20},{20... | collective-permute-start | bytes 983048 | tf_op jit(solution)/shard_map/slab_imag_0/ppermute | solution.py:348
  28.3 6.5 %collective-permute-start.11 = (f32[2,96,256]{2,1,0:T(8,128)S(1)}, f32[2,96,256]{2,1,0:T(8,128)S(1)}, u32[]{:S(2)}, u32[]{:S(2)}) collective-permute-start(f32[2,96,256]{2,1,0:T(8,128)S(1)} %get-tuple-element.37.refs_2_.refs_0_), channel_id=1, source_target_pairs={{0,2},{1,3},{2,0},{3,1},{4,6},{5,7},{6,4},{7,5},{8,10},{9,11},{10,... | collective-permute-start | bytes 589832 | tf_op jit(solution)/shard_map/real_across_1/ppermute | solution.py:344
  28.9 9.8 %collective-permute-start.8 = (f32[2,96,256]{2,1,0:T(8,128)S(1)}, f32[2,96,256]{2,1,0:T(8,128)S(1)}, u32[]{:S(2)}, u32[]{:S(2)}) collective-permute-start(f32[2,96,256]{2,1,0:T(8,128)S(1)} %get-tuple-element.27), channel_id=1, source_target_pairs={{0,4},{1,5},{2,6},{3,7},{4,0},{5,1},{6,2},{7,3},{8,12},{9,13},{10,... | collective-permute-start | bytes 589832 | tf_op jit(solution)/shard_map/lines1a_1/ppermute | solution.py:344
  29.0 9.7 %collective-permute-start.16 = (f32[2,96,256]{2,1,0:T(8,128)S(1)}, f32[2,96,256]{2,1,0:T(8,128)S(1)}, u32[]{:S(2)}, u32[]{:S(2)}) collective-permute-start(f32[2,96,256]{2,1,0:T(8,128)S(1)} %get-tuple-element.36), channel_id=1, source_target_pairs={{4,8},{5,9},{6,10},{7,11},{8,4},{9,5},{10,6},{11,7},{20,24},{21,25... | collective-permute-start | bytes 589832 | tf_op jit(solution)/shard_map/lines1b_1/ppermute | solution.py:344
  35.0 5.7 %collective-permute-start.12 = (f32[2,96,256]{2,1,0:T(8,128)S(1)}, f32[2,96,256]{2,1,0:T(8,128)S(1)}, u32[]{:S(2)}, u32[]{:S(2)}) collective-permute-start(f32[2,96,256]{2,1,0:T(8,128)S(1)} %get-tuple-element.31), channel_id=1, source_target_pairs={{0,4},{1,5},{2,6},{3,7},{4,0},{5,1},{6,2},{7,3},{8,12},{9,13},{10,... | collective-permute-start | bytes 589832 | tf_op jit(solution)/shard_map/lines2a_1/ppermute | solution.py:344
  35.1 9.7 %copy-start.5 = (f32[2,2,256,256]{3,2,1,0:T(8,128)}, f32[2,2,256,256]{3,2,1,0:T(8,128)S(1)}, u32[]{:S(2)}) copy-start(f32[2,2,256,256]{3,2,1,0:T(8,128)S(1)} %collective-permute-done.9.behind_ref) | copy-start | bytes 3145732
  35.1 7.6 %collective-permute-start.13 = (f32[2,96,256]{2,1,0:T(8,128)S(1)}, f32[2,96,256]{2,1,0:T(8,128)S(1)}, u32[]{:S(2)}, u32[]{:S(2)}) collective-permute-start(f32[2,96,256]{2,1,0:T(8,128)S(1)} %get-tuple-element.32), channel_id=1, source_target_pairs={{4,8},{5,9},{6,10},{7,11},{8,4},{9,5},{10,6},{11,7},{20,24},{21,25... | collective-permute-start | bytes 589832 | tf_op jit(solution)/shard_map/lines2b_1/ppermute | solution.py:344
  38.9 5.7 %collective-permute-start.17 = (f32[2,96,256]{2,1,0:T(8,128)S(1)}, f32[2,96,256]{2,1,0:T(8,128)S(1)}, u32[]{:S(2)}, u32[]{:S(2)}) collective-permute-start(f32[2,96,256]{2,1,0:T(8,128)S(1)} %shard_map.82), channel_id=1, source_target_pairs={{0,2},{1,3},{2,0},{3,1},{4,6},{5,7},{6,4},{7,5},{8,10},{9,11},{10,... | collective-permute-start | bytes 589832 | tf_op jit(solution)/shard_map/imag_across_1/ppermute | solution.py:344
  39.5 7.9 %collective-permute-start.14 = (f32[2,160,256]{2,1,0:T(8,128)S(1)}, f32[2,160,256]{2,1,0:T(8,128)S(1)}, u32[]{:S(2)}, u32[]{:S(2)}) collective-permute-start(f32[2,160,256]{2,1,0:T(8,128)S(1)} %shard_map.80.refs_0_), channel_id=1, source_target_pairs={{0,16},{16,0},{1,17},{17,1},{2,18},{18,2},{3,19},{19,3},{4,20},{20... | collective-permute-start | bytes 983048 | tf_op jit(solution)/shard_map/slab_real_0/ppermute | solution.py:348
  45.0 3.5 %collective-permute-start.18 = (f32[2,96,256]{2,1,0:T(8,128)S(1)}, f32[2,96,256]{2,1,0:T(8,128)S(1)}, u32[]{:S(2)}, u32[]{:S(2)}) collective-permute-start(f32[2,96,256]{2,1,0:T(8,128)S(1)} %shard_map.84), channel_id=1, source_target_pairs={{0,1},{1,0},{2,3},{3,2},{4,5},{5,4},{6,7},{7,6},{8,9},{9,8},{10,11... | collective-permute-start | bytes 589832 | tf_op jit(solution)/shard_map/real_cores_1/ppermute | solution.py:344
  45.1 4.5 %copy-start.4 = (f32[1,2,2,256,256]{4,3,2,1,0:T(8,128)S(1)}, f32[1,2,2,256,256]{4,3,2,1,0:T(8,128)}, u32[]{:S(2)}) copy-start(f32[1,2,2,256,256]{4,3,2,1,0:T(8,128)} %param.7) | copy-start | bytes 3145732
  47.4 8.4 %collective-permute-start.19 = (f32[2,96,256]{2,1,0:T(8,128)S(1)}, f32[2,96,256]{2,1,0:T(8,128)S(1)}, u32[]{:S(2)}, u32[]{:S(2)}) collective-permute-start(f32[2,96,256]{2,1,0:T(8,128)S(1)} %shard_map.83.refs_3_), channel_id=1, source_target_pairs={{0,16},{16,0},{1,17},{17,1},{2,18},{18,2},{3,19},{19,3},{4,20},{20... | collective-permute-start | bytes 589832 | tf_op jit(solution)/shard_map/slab_imag_1/ppermute | solution.py:348
  48.7 3.2 %copy-start.6 = (f32[2,2,256,256]{3,2,1,0:T(8,128)S(1)}, f32[2,2,256,256]{3,2,1,0:T(8,128)}, u32[]{:S(2)}) copy-start(f32[2,2,256,256]{3,2,1,0:T(8,128)} %copy-done.5) | copy-start | bytes 3145732
  48.7 3.2 %copy-start.7 = (f32[1,256,256]{2,1,0:T(8,128)S(1)}, f32[1,256,256]{2,1,0:T(8,128)}, u32[]{:S(2)}) copy-start(f32[1,256,256]{2,1,0:T(8,128)} %param.9) | copy-start | bytes 786436
  48.7 7.9 %collective-permute-start.20 = (f32[2,96,256]{2,1,0:T(8,128)S(1)}, f32[2,96,256]{2,1,0:T(8,128)S(1)}, u32[]{:S(2)}, u32[]{:S(2)}) collective-permute-start(f32[2,96,256]{2,1,0:T(8,128)S(1)} %shard_map.85.refs_1_), channel_id=1, source_target_pairs={{0,16},{16,0},{1,17},{17,1},{2,18},{18,2},{3,19},{19,3},{4,20},{20... | collective-permute-start | bytes 589832 | tf_op jit(solution)/shard_map/slab_real_1/ppermute | solution.py:348
  51.8 0.7 %copy-start.8 = (s32[1,4,4]{2,1,0:T(4,128)S(1)}, s32[1,4,4]{2,1,0:T(4,128)}, u32[]{:S(2)}) copy-start(s32[1,4,4]{2,1,0:T(4,128)} %param.10) | copy-start | bytes 196
